TPU v7x, 256 devices: a whole 4x4x8 slice. The times are simulated.
256 devices in a mesh: seq: 128 (over x_hi, y, z, core), head: 2 (over x_lo).
Axes of the slice: x: 4 (x_hi: 2, x_lo: 2; x = x_hi * 2 + x_lo), y: 4, z: 8, core: 2. Of those that a mesh axis runs over, the one named last changes fastest.
Arguments:
- queries: bfloat16 [65536, 768], P('seq', 'head'), may hold values from -6 to 6
- keys: bfloat16 [65536, 768], P('seq', 'head'), may hold values from -6 to 6
- values: bfloat16 [65536, 768], P('seq', 'head'), may hold values from -6 to 6
- weight_out: bfloat16 [768, 768], P('head'), may hold values from -0.21875 to 0.21875
- cotangent: bfloat16 [65536, 768], P('seq', 'head'), may hold values from -6 to 6
Outputs:
- mixed: bfloat16 [65536, 768], P('seq', 'head')
- query_grad: bfloat16 [65536, 768], P('seq', 'head')
- key_grad: bfloat16 [65536, 768], P('seq', 'head')
- value_grad: bfloat16 [65536, 768], P('seq', 'head')
All inputs are finite; a program needn't handle non-finite values.
Results may differ from a plain program's by a relative error of at most 0.034.
Values may be sent and summed in bfloat16 or wider, within the bound.
No kernel may reach another device: no remote copies, remote signals or barrier semaphores. Data moves between devices by JAX's collectives and lax.ppermute only.
A program may use at most 128 MiB of HBM per device.

v0:
```python
import functools

import jax
import jax.numpy as jnp
import numpy as np
from jax import lax
from jax.experimental import pallas as pl
from jax.experimental.pallas import tpu as pltpu
from jax.sharding import PartitionSpec as P

HEAD_DIM = 64
LOCAL_HEADS = 6
ROWS = 512
KEPT = 64
SCALE = HEAD_DIM ** -0.5
BF = jnp.bfloat16
F32 = jnp.float32
MASKED = 1e30


def kept_rows(head):
    phase = head // 8
    third = [16 * i + phase for i in range(4)]
    second = [4 * i + phase for i in range(16) if i % 4]
    first = [i for i in range(64) if i % 4 != phase]
    return [8 * i + head % 8 for i in third + second + first]


def one_hot_tables():
    table = np.zeros((2, LOCAL_HEADS * KEPT, ROWS), np.float32)
    for half in range(2):
        for local in range(LOCAL_HEADS):
            for place, row in enumerate(kept_rows(half * LOCAL_HEADS + local)):
                table[half, local * KEPT + place, row] = 1.0
    return table


def subset_table(groups, wide, narrow):
    table = np.zeros((groups * narrow, groups * wide), np.float32)
    for group in range(groups):
        for place in range(narrow):
            table[group * narrow + place, group * wide + place] = 1.0
    return table


def dot_nn(left, right):
    return lax.dot_general(left, right, (((1,), (0,)), ((), ())), preferred_element_type=F32)


def dot_nt(left, right):
    return lax.dot_general(left, right, (((1,), (1,)), ((), ())), preferred_element_type=F32)


def dot_tn(left, right):
    return lax.dot_general(left, right, (((0,), (0,)), ((), ())), preferred_element_type=F32)


def split2(value):
    high = value.astype(BF)
    return high, (value - high.astype(F32)).astype(BF)


def split3(value):
    high = value.astype(BF)
    rest = value - high.astype(F32)
    middle = rest.astype(BF)
    return high, middle, (rest - middle.astype(F32)).astype(BF)


def stat_block(log_row, delta_row):
    pieces = split3(log_row) + split3(delta_row)
    rows = [piece.astype(F32) for piece in pieces]
    zero = jnp.zeros_like(log_row)
    return jnp.concatenate(rows + [zero, zero], axis=0)


def stat_rows(block):
    block = block.astype(F32)
    log_row = block[0:1] + block[1:2] + block[2:3]
    delta_row = block[3:4] + block[4:5] + block[5:6]
    return log_row, delta_row


def head_cols(ref, head):
    return ref[:, head * HEAD_DIM:(head + 1) * HEAD_DIM]


def log_add(first, second):
    peak = jnp.maximum(first, second)
    return peak + jnp.log(jnp.exp(first - peak) + jnp.exp(second - peak))


def local_forward(q_ref, k_ref, v_ref, out_t_ref, log_ref):
    for head in range(LOCAL_HEADS):
        query = head_cols(q_ref, head) * BF(SCALE)
        scores = dot_nt(head_cols(k_ref, head), query)
        peak = jnp.max(scores, axis=0, keepdims=True)
        powers = jnp.exp(scores - peak)
        total = jnp.sum(powers, axis=0, keepdims=True)
        weighted = dot_tn(head_cols(v_ref, head), powers.astype(BF))
        out_t_ref[head * HEAD_DIM:(head + 1) * HEAD_DIM, :] = weighted / total
        log_ref[head:head + 1, :] = peak + jnp.log(total)
    log_ref[LOCAL_HEADS:, :] = jnp.zeros((8 - LOCAL_HEADS, ROWS), F32)


def pack_rows(q_ref, k_ref, v_ref, own_cot_ref, other_cot_ref, own_w_ref, other_w_ref, hot_ref, out_t_ref, log_ref,
              grad_ref, delta_ref, payload_ref):
    grad = dot_nt(own_cot_ref[...], own_w_ref[...]) + dot_nt(other_cot_ref[...], other_w_ref[...])
    grad_ref[...] = grad.astype(BF)
    grad_t = dot_nt(own_w_ref[...], own_cot_ref[...]) + dot_nt(other_w_ref[...], other_cot_ref[...])
    product = grad_t.astype(BF).astype(F32) * out_t_ref[...]
    delta_ref[LOCAL_HEADS:, :] = jnp.zeros((8 - LOCAL_HEADS, ROWS), F32)
    for head in range(LOCAL_HEADS):
        hot = hot_ref[head * KEPT:(head + 1) * KEPT, :]
        delta = jnp.sum(product[head * HEAD_DIM:(head + 1) * HEAD_DIM], axis=0, keepdims=True)
        delta_ref[head:head + 1, :] = delta
        joined = jnp.concatenate(
            [head_cols(ref, head) for ref in (q_ref, k_ref, v_ref, grad_ref)], axis=1
        )
        payload_ref[head, :KEPT, :] = dot_nn(hot, joined).astype(BF)
        stats = stat_block(log_ref[head:head + 1, :], delta).astype(BF)
        payload_ref[head, KEPT:, :] = widen_stats(dot_nt(stats, hot))
    for spare in range(LOCAL_HEADS, 8):
        payload_ref[spare] = jnp.zeros((KEPT + 16, 256), BF)


def widen_stats(block):
    wide = jnp.concatenate([block, jnp.zeros((8, 256 - block.shape[1]), F32)], axis=1)
    return jnp.concatenate([wide, jnp.zeros((8, 256), F32)], axis=0).astype(BF)


def local_backward(q_ref, k_ref, v_ref, grad_ref, log_ref, delta_ref, kept_ref, out_t_ref,
                   dq_ref, dk_ref, dv_ref, att_t_ref):
    dq_t = []
    for head in range(LOCAL_HEADS):
        span = slice(head * HEAD_DIM, (head + 1) * HEAD_DIM)
        query = head_cols(q_ref, head) * BF(SCALE)
        key = head_cols(k_ref, head)
        grad = head_cols(grad_ref, head)
        kept = kept_ref[head:head + 1, :]
        probability = jnp.exp(dot_nt(key, query) - (log_ref[head:head + 1, :] + kept * MASKED))
        score_grad = probability * (dot_nt(head_cols(v_ref, head), grad) - delta_ref[head:head + 1, :])
        score_grad = score_grad.astype(BF)
        dv_ref[:, span] = dot_nn(probability.astype(BF), grad)
        dk_ref[:, span] = dot_nn(score_grad, query)
        dq_t.append(dot_tn(key, score_grad))
        att_t_ref[span, :] = (out_t_ref[span, :] * (1.0 - kept)).astype(BF)
    dq_ref[...] = jnp.concatenate(dq_t, axis=0).T * SCALE


def set_stats(query, key, value, grad):
    scores = dot_nt(key, query)
    peak = jnp.max(scores, axis=0, keepdims=True)
    powers = jnp.exp(scores - peak)
    total = jnp.sum(powers, axis=0, keepdims=True)
    prob_grad = dot_nt(value, grad)
    delta = jnp.sum(powers * prob_grad, axis=0, keepdims=True) / total
    return powers, total, peak + jnp.log(total), delta


def merge(old_log, old_delta, new_log, new_delta):
    joint = log_add(old_log, new_log)
    return joint, jnp.exp(old_log - joint) * old_delta + jnp.exp(new_log - joint) * new_delta


def split_cols(data):
    return (data[:, :64] * BF(SCALE), data[:, 64:128], data[:, 128:192], data[:, 192:])


def first_data(block_ref):
    return block_ref[:, :KEPT, :].reshape(ROWS, 256)


def gathered(block_ref):
    data = block_ref[:, :128, :].reshape(ROWS, 256)
    stats = jnp.concatenate([block_ref[i, 128:136, :128].astype(F32) for i in range(4)], axis=1)
    return data, stats


def level_one(block_ref, pick_ref, payload_ref, stat_ref, out_t_ref):
    data = first_data(block_ref)
    query, key, value, grad = split_cols(data)
    stats = jnp.concatenate([block_ref[i, KEPT:KEPT + 8, :KEPT].astype(F32) for i in range(8)], axis=1)
    old_log, old_delta = stat_rows(stats)
    powers, total, new_log, new_delta = set_stats(query, key, value, grad)
    joint, delta = merge(old_log, old_delta, new_log, new_delta)
    out_t_ref[...] = dot_tn(value, powers.astype(BF)) * (jnp.exp(new_log - joint) / total)
    stat_ref[0:1, :] = joint
    stat_ref[1:2, :] = delta
    stat_ref[2:, :] = jnp.zeros((6, ROWS), F32)
    payload_ref[:128, :] = block_ref[:, :16, :].reshape(128, 256)
    picked = dot_nt(stat_block(joint, delta).astype(BF), pick_ref[...])
    payload_ref[128:, :] = widen_stats(picked)


def level_two(block_ref, pick_ref, payload_ref, stat_ref, out_t_ref):
    data, stats = gathered(block_ref)
    query, key, value, grad = split_cols(data)
    old_log, old_delta = stat_rows(stats)
    powers, total, new_log, new_delta = set_stats(query, key, value, grad)
    joint, delta = merge(old_log, old_delta, new_log, new_delta)
    weight = (jnp.exp(new_log - joint) / total)[:, :128]
    out_t_ref[...] = dot_tn(value, powers[:, :128].astype(BF)) * weight
    stat_ref[0:1, :] = joint
    stat_ref[1:2, :] = delta
    stat_ref[2:, :] = jnp.zeros((6, ROWS), F32)
    payload_ref[:128, :] = dot_nn(pick_ref[...], data).astype(BF)
    picked = dot_nt(stat_block(joint, delta).astype(BF), pick_ref[...])
    payload_ref[128:, :] = widen_stats(picked)


def set_grads(data, log_row, delta_row, own):
    query, key, value, grad = split_cols(data)
    probability = jnp.exp(dot_nt(key, query) - log_row)
    score_grad = (probability * (dot_nt(value, grad) - delta_row)).astype(BF)
    key_grad = dot_nn(score_grad[:own], query)
    value_grad = dot_nn(probability[:own].astype(BF), grad)
    query_grad_t = dot_tn(key, score_grad[:, :own]) * SCALE
    return query_grad_t, jnp.concatenate([key_grad, value_grad], axis=1)


def spread_lanes(value, pick):
    high, low = split2(value)
    return dot_nn(high, pick) + dot_nn(low, pick)


def spread_stats(log_row, delta_row, pick):
    return stat_rows(dot_nn(stat_block(log_row, delta_row).astype(BF), pick))


def level_three(first_ref, second_ref, third_ref, stat1_ref, stat2_ref, out1_ref, out2_ref, pick2_ref, pick3_ref,
                payload_ref):
    pick2 = pick2_ref[...]
    pick3 = pick3_ref[...]
    in_second = jnp.sum(pick2.astype(F32), axis=0, keepdims=True) > 0.5
    in_third = jnp.sum(pick3.astype(F32), axis=0, keepdims=True) > 0.5

    data3, stats3 = gathered(third_ref)
    query, key, value, grad = split_cols(data3)
    old_log, old_delta = stat_rows(stats3)
    powers, total, new_log, new_delta = set_stats(query, key, value, grad)
    log3, delta3 = merge(old_log, old_delta, new_log, new_delta)
    weight = (jnp.exp(new_log - log3) / total)[:, :128]
    out3 = dot_tn(value, powers[:, :128].astype(BF)) * weight
    dq3, dkv3 = set_grads(data3, log3, delta3, 128)

    spread_log, spread_delta = spread_stats(log3[:, :128], delta3[:, :128], pick3)
    log2 = jnp.where(in_third, spread_log, stat2_ref[0:1, :])
    delta2 = jnp.where(in_third, spread_delta, stat2_ref[1:2, :])
    data2, _ = gathered(second_ref)
    dq2, dkv2 = set_grads(data2, log2, delta2, 128)
    own3 = pick3[:32, :128]
    own_lane = lax.broadcasted_iota(jnp.int32, (1, 128), 1) < 32
    merged_t = jnp.concatenate([dq3, out3], axis=0)
    merged_t = jnp.where(own_lane, merged_t, 0.0)
    own_pick = jnp.concatenate([own3, jnp.zeros((96, 128), BF)], axis=0)
    fade2 = jnp.exp(stat2_ref[0:1, :128] - log2[:, :128])
    base_t = jnp.concatenate([dq2, out2_ref[...] * fade2], axis=0)
    merged_t = base_t + spread_lanes(merged_t, own_pick)
    high, low = split2(dkv3[:32])
    dkv2 = dkv2 + dot_tn(own3, high) + dot_tn(own3, low)

    spread_log, spread_delta = spread_stats(log2[:, :128], delta2[:, :128], pick2)
    log1 = jnp.where(in_second, spread_log, stat1_ref[0:1, :])
    delta1 = jnp.where(in_second, spread_delta, stat1_ref[1:2, :])
    data1 = first_data(first_ref)
    dq1, dkv1 = set_grads(data1, log1, delta1, ROWS)
    fade1 = jnp.exp(stat1_ref[0:1, :] - log1)
    base_t = jnp.concatenate([dq1, out1_ref[...] * fade1], axis=0)
    merged_t = base_t + spread_lanes(merged_t, pick2)
    high, low = split2(dkv2)
    dkv1 = dkv1 + dot_tn(pick2, high) + dot_tn(pick2, low)

    rows = jnp.concatenate([merged_t.T, dkv1], axis=1).astype(BF)
    payload_ref[:, :KEPT, :] = rows.reshape(8, KEPT, 256)
    stats = stat_block(log1, delta1)
    for owner in range(8):
        payload_ref[owner, KEPT:, :] = widen_stats(stats[:, owner * KEPT:(owner + 1) * KEPT])


def kept_attended(back_ref, hot_ref, out_t_ref, log_ref, att_ref):
    for head in range(LOCAL_HEADS):
        span = slice(head * HEAD_DIM, (head + 1) * HEAD_DIM)
        hot = hot_ref[head * KEPT:(head + 1) * KEPT, :]
        high, low = split2(out_t_ref[span, :])
        local = dot_nt(high, hot) + dot_nt(low, hot)
        zero = jnp.zeros((1, ROWS), F32)
        local_log, _ = stat_rows(dot_nt(stat_block(log_ref[head:head + 1, :], zero).astype(BF), hot))
        log_total, _ = stat_rows(back_ref[head, KEPT:KEPT + 8, :KEPT])
        sparse = back_ref[head, :KEPT, 64:128].astype(F32).T
        att_ref[span, :] = (local * jnp.exp(local_log - log_total) + sparse).astype(BF)


def final_grads(q_ref, k_ref, v_ref, sent_ref, back_ref, tall_ref, dq_ref, dk_ref, dv_ref,
                dq_out_ref, dk_out_ref, dv_out_ref):
    for head in range(LOCAL_HEADS):
        span = slice(head * HEAD_DIM, (head + 1) * HEAD_DIM)
        key = head_cols(k_ref, head)
        query = sent_ref[head, :KEPT, :64] * BF(SCALE)
        grad = sent_ref[head, :KEPT, 192:]
        tall = head_cols(tall_ref, head)
        log_total, delta = stat_rows(back_ref[head, KEPT:KEPT + 8, :KEPT])
        probability = jnp.exp(dot_nt(key, query) - log_total)
        score_grad = (probability * (dot_nt(head_cols(v_ref, head), grad) - delta)).astype(BF)
        back = back_ref[head, :KEPT, :]
        dk_more = dot_nn(
            jnp.concatenate([score_grad, tall], axis=1), jnp.concatenate([query, back[:, 128:192]], axis=0)
        )
        dv_more = dot_nn(
            jnp.concatenate([probability.astype(BF), tall], axis=1),
            jnp.concatenate([grad, back[:, 192:]], axis=0),
        )
        high, low = split2(dot_tn(score_grad, key) * SCALE + back[:, :64].astype(F32))
        dq_more = dot_nn(jnp.concatenate([tall, tall], axis=1), jnp.concatenate([high, low], axis=0))
        dq_out_ref[:, span] = (dq_ref[:, span] + dq_more).astype(BF)
        dk_out_ref[:, span] = (dk_ref[:, span] + dk_more).astype(BF)
        dv_out_ref[:, span] = (dv_ref[:, span] + dv_more).astype(BF)


def mix_rows(own_att_ref, other_att_ref, own_kept_ref, other_kept_ref, own_hot_ref, other_hot_ref,
             own_w_ref, other_w_ref, mixed_ref):
    total = jnp.zeros((ROWS, 384), F32)
    for att_ref, kept_ref, hot_ref, w_ref in (
        (own_att_ref, own_kept_ref, own_hot_ref, own_w_ref),
        (other_att_ref, other_kept_ref, other_hot_ref, other_w_ref),
    ):
        parts = []
        for head in range(LOCAL_HEADS):
            span = slice(head * HEAD_DIM, (head + 1) * HEAD_DIM)
            hot = hot_ref[head * KEPT:(head + 1) * KEPT, :]
            parts.append((att_ref[span, :].astype(F32) + dot_nn(kept_ref[span, :], hot)).astype(BF))
        total = total + dot_tn(jnp.concatenate(parts, axis=0), w_ref[...])
    mixed_ref[...] = total.astype(BF)


def call(kernel, outs, *args, flops=0):
    shapes = tuple(jax.ShapeDtypeStruct(shape, dtype) for shape, dtype in outs)
    moved = sum(a.size * a.dtype.itemsize for a in args) + sum(
        int(np.prod(shape)) * jnp.dtype(dtype).itemsize for shape, dtype in outs
    )
    result = pl.pallas_call(
        kernel,
        out_shape=shapes,
        in_specs=[pl.BlockSpec(memory_space=pltpu.VMEM)] * len(args),
        out_specs=tuple(pl.BlockSpec(memory_space=pltpu.VMEM) for _ in outs),
        compiler_params=pltpu.CompilerParams(vmem_limit_bytes=40 * 1024 * 1024),
        cost_estimate=pl.CostEstimate(flops=flops, bytes_accessed=moved, transcendentals=0),
        name=kernel.__name__,
    )(*args)
    return result


def partner(array):
    return lax.ppermute(array, "head", [(0, 1), (1, 0)])


def flip(array, bit):
    return lax.ppermute(array, "seq", [(i, i ^ 1 << bit) for i in range(lax.axis_size("seq"))])


def body(queries, keys, values, weight_out, cotangent):
    seq_count = lax.axis_size("seq")
    half = lax.axis_index("head")
    octets = [[8 * i + j for j in range(8)] for i in range(seq_count // 8)]
    hots = jnp.asarray(one_hot_tables(), BF)
    own_hot = lax.dynamic_index_in_dim(hots, half, 0, keepdims=False)
    other_hot = lax.dynamic_index_in_dim(hots, 1 - half, 0, keepdims=False)
    tall = lax.dynamic_index_in_dim(jnp.asarray(np.swapaxes(one_hot_tables(), 1, 2), BF), half, 0, keepdims=False)
    pick2 = jnp.asarray(subset_table(8, 64, 16), BF)
    pick3 = jnp.asarray(subset_table(32, 16, 4), BF)
    kept_table = np.zeros((2, 8, ROWS), np.float32)
    for head in range(2 * LOCAL_HEADS):
        kept_table[head // LOCAL_HEADS, head % LOCAL_HEADS, kept_rows(head)] = 1.0
    kept = lax.dynamic_index_in_dim(jnp.asarray(kept_table), half, 0, keepdims=False)
    own_w = lax.dynamic_slice_in_dim(weight_out, half * 384, 384, 1)
    other_w = lax.dynamic_slice_in_dim(weight_out, (1 - half) * 384, 384, 1)

    other_cot = partner(cotangent)
    out_t, log0 = call(local_forward, [((384, ROWS), F32), ((8, ROWS), F32)], queries, keys, values, flops=400000000)
    grad, delta0, sent = call(
        pack_rows,
        [((ROWS, 384), BF), ((8, ROWS), F32), ((8, KEPT + 16, 256), BF)],
        queries, keys, values, cotangent, other_cot, own_w, other_w, own_hot, out_t, log0, flops=600000000,
    )
    block1 = lax.all_to_all(sent, "seq", 0, 0, axis_index_groups=octets)
    mix_w = partner(other_w)
    dq, dk, dv, att_t = call(
        local_backward,
        [((ROWS, 384), F32), ((ROWS, 384), F32), ((ROWS, 384), F32), ((384, ROWS), BF)],
        queries, keys, values, grad, log0, delta0, kept, out_t, flops=1000000000,
    )
    other_att_t = partner(att_t)

    sent2, stat1, out1 = call(
        level_one, [((144, 256), BF), ((8, ROWS), F32), ((64, ROWS), F32)], block1, pick2, flops=100000000
    )
    block2 = jnp.stack([sent2, flip(sent2, 3)])
    block2 = jnp.concatenate([block2, flip(block2, 4)])
    sent3, stat2, out2 = call(
        level_two, [((144, 256), BF), ((8, ROWS), F32), ((64, 128), F32)], block2, pick3, flops=100000000
    )
    block3 = jnp.stack([sent3, flip(sent3, 5)])
    block3 = jnp.concatenate([block3, flip(block3, 6)])
    (returned,) = call(
        level_three, [((8, KEPT + 16, 256), BF)],
        block1, block2, block3, stat1, stat2, out1, out2, pick2, pick3, flops=300000000,
    )
    back = lax.all_to_all(returned, "seq", 0, 0, axis_index_groups=octets)
    (own_kept,) = call(kept_attended, [((384, KEPT), BF)], back, own_hot, out_t, log0, flops=50000000)
    other_kept = partner(own_kept)
    query_grad, key_grad, value_grad = call(
        final_grads, [((ROWS, 384), BF)] * 3, queries, keys, values, sent, back, tall, dq, dk, dv, flops=200000000
    )
    (mixed,) = call(
        mix_rows, [((ROWS, 384), BF)],
        att_t, other_att_t, own_kept, other_kept, own_hot, other_hot, own_w, mix_w, flops=400000000,
    )
    return mixed, query_grad, key_grad, value_grad


def solution(mesh):
    specs = P("seq", "head")
    return jax.shard_map(
        body,
        mesh=mesh,
        in_specs=(specs, specs, specs, P("head", None), specs),
        out_specs=(specs, specs, specs, specs),
        check_vma=False,
    )
```

profile of v0, /device:TPU:2, one launch (start us, length us, event | category | flops | bytes accessed | tf_op | source)
XLA Modules:
  0.0 98.3 jit_solution(10345033320789726705)
XLA Ops:
  0.6 2.4 %collective-permute-start = (bf16[512,384]{1,0:T(8,128)(2,1)}, bf16[512,384]{1,0:T(8,128)(2,1)S(1)}, u32[]{:S(2)}, u32[]{:S(2)}) collective-permute-start(bf16[512,384]{1,0:T(8,128)(2,1)} %own_cot_ref.1), channel_id=1, source_target_pairs={{0,1},{1,0},{2,3},{3,2},{4,5},{5,4},{6,7},{7,6},{8,9},{9,8},{10,11... | collective-permute-start | bytes 1179656 | tf_op jit(solution)/shard_map/ppermute | solution.py:354
  3.0 0.0 copy-start
  3.0 1.0 %copy-done = bf16[512,384]{1,0:T(8,128)(2,1)S(1)} copy-done((bf16[512,384]{1,0:T(8,128)(2,1)S(1)}, bf16[512,384]{1,0:T(8,128)(2,1)}, u32[]{:S(2)}) %copy-start) | copy-done | bytes 393240
  4.0 0.0 copy-start.2
  4.0 1.0 %copy-done.2 = bf16[512,384]{1,0:T(8,128)(2,1)S(1)} copy-done((bf16[512,384]{1,0:T(8,128)(2,1)S(1)}, bf16[512,384]{1,0:T(8,128)(2,1)}, u32[]{:S(2)}) %copy-start.2) | copy-done | bytes 393240
  5.0 1.0 %copy-done.4 = bf16[512,384]{1,0:T(8,128)(2,1)S(1)} copy-done((bf16[512,384]{1,0:T(8,128)(2,1)S(1)}, bf16[512,384]{1,0:T(8,128)(2,1)}, u32[]{:S(2)}) %copy-start.4) | copy-done | bytes 393240
  6.0 3.4 %local_forward.1 = (f32[384,512]{1,0:T(8,128)S(1)}, f32[8,512]{1,0:T(8,128)S(1)}) custom-call(bf16[512,384]{1,0:T(8,128)(2,1)S(1)} %copy-done, bf16[512,384]{1,0:T(8,128)(2,1)S(1)} %copy-done.2, bf16[512,384]{1,0:T(8,128)(2,1)S(1)} %copy-done.4), custom_call_target="tpu_custom_call" | custom-call | flops 400000000 | bytes 1982464 | tf_op jit(solution)/shard_map/local_forward/pallas_call | solution.py:341
  9.4 0.0 copy-done.21
  9.4 0.0 copy-start.20
  9.4 0.8 constant_dynamic-slice_fusion
  10.2 0.4 copy-done.20
  10.7 0.1 dynamic-slice_bitcast_fusion.1
  10.7 1.1 %collective-permute-done.other_cot_ref = bf16[512,384]{1,0:T(8,128)(2,1)S(1)} collective-permute-done((bf16[512,384]{1,0:T(8,128)(2,1)}, bf16[512,384]{1,0:T(8,128)(2,1)S(1)}, u32[]{:S(2)}, u32[]{:S(2)}) %collective-permute-start) | collective-permute-done | bytes 393248 | tf_op jit(solution)/shard_map/ppermute | solution.py:354
  11.8 0.0 copy-done.17
  11.8 2.5 %pack_rows.1 = (bf16[512,384]{1,0:T(8,128)(2,1)S(1)}, f32[8,512]{1,0:T(8,128)S(1)}, bf16[8,80,256]{2,1,0:T(8,128)(2,1)S(1)}) custom-call(bf16[512,384]{1,0:T(8,128)(2,1)S(1)} %copy-done, bf16[512,384]{1,0:T(8,128)(2,1)S(1)} %copy-done.2, bf16[512,384]{1,0:T(8,128)(2,1)S(1)} %copy-done.4, bf16[512,384]{1,0:T(8,128)(2,1)S(1)} %copy-done.17, ...), custom_call_target="tpu_custom_call" | custom-call | flops 600000000 | bytes 4489216 | tf_op jit(solution)/shard_map/pack_rows/pallas_call | solution.py:341
  14.3 0.8 copy-done.18
  15.1 17.0 %all_to_all.10.block_ref.first_ref = bf16[8,80,256]{2,1,0:T(8,128)(2,1)S(1)} all-to-all(bf16[8,80,256]{2,1,0:T(8,128)(2,1)S(1)} %get-tuple-element.27.sent_ref), channel_id=1, replica_groups={{0,2,4,6,8,10,12,14},{16,18,20,22,24,26,28,30},{32,34,36,38,40,42,44,46..., dimensions={0} | all-to-all | bytes 655360 | tf_op jit(solution)/shard_map/all_to_all | solution.py:385
  32.0 0.0 copy-done.6
  32.0 0.0 copy-done.15
  32.0 0.8 level_one.1
  32.8 4.5 %collective-permute-start.2 = (bf16[144,256]{1,0:T(8,128)(2,1)S(1)}, bf16[144,256]{1,0:T(8,128)(2,1)S(1)}, u32[]{:S(2)}, u32[]{:S(2)}) collective-permute-start(bf16[144,256]{1,0:T(8,128)(2,1)S(1)} %get-tuple-element.28), channel_id=1, source_target_pairs={{0,16},{2,18},{4,20},{6,22},{8,24},{10,26},{12,28},{14,30},{16,0},... | collective-permute-start | bytes 221192 | tf_op jit(solution)/shard_map/ppermute | solution.py:358
  37.4 4.6 %collective-permute-done.2 = bf16[144,256]{1,0:T(8,128)(2,1)S(1)} collective-permute-done((bf16[144,256]{1,0:T(8,128)(2,1)S(1)}, bf16[144,256]{1,0:T(8,128)(2,1)S(1)}, u32[]{:S(2)}, u32[]{:S(2)}) %collective-permute-start.2) | collective-permute-done | bytes 73760 | tf_op jit(solution)/shard_map/ppermute | solution.py:358
  42.0 0.0 copy-start.16
  42.0 1.7 %collective-permute-start.3 = (bf16[2,144,256]{2,1,0:T(8,128)(2,1)S(1)}, bf16[2,144,256]{2,1,0:T(8,128)(2,1)S(1)}, u32[]{:S(2)}, u32[]{:S(2)}) collective-permute-start(bf16[2,144,256]{2,1,0:T(8,128)(2,1)S(1)} %pad_maximum_fusion.2), channel_id=1, source_target_pairs={{0,32},{2,34},{4,36},{6,38},{8,40},{10,42},{12,44},{14,46},{16,48}... | collective-permute-start | bytes 442376 | tf_op jit(solution)/shard_map/ppermute | solution.py:358
  43.6 3.6 %collective-permute-done.3 = bf16[2,144,256]{2,1,0:T(8,128)(2,1)S(1)} collective-permute-done((bf16[2,144,256]{2,1,0:T(8,128)(2,1)S(1)}, bf16[2,144,256]{2,1,0:T(8,128)(2,1)S(1)}, u32[]{:S(2)}, u32[]{:S(2)}) %collective-permute-start.3) | collective-permute-done | bytes 147488 | tf_op jit(solution)/shard_map/ppermute | solution.py:358
  47.2 0.0 copy-done.16
  47.2 0.8 level_two.1
  48.0 3.2 %collective-permute-start.4 = (bf16[144,256]{1,0:T(8,128)(2,1)S(1)}, bf16[144,256]{1,0:T(8,128)(2,1)S(1)}, u32[]{:S(2)}, u32[]{:S(2)}) collective-permute-start(bf16[144,256]{1,0:T(8,128)(2,1)S(1)} %get-tuple-element.29), channel_id=1, source_target_pairs={{0,64},{2,66},{4,68},{6,70},{8,72},{10,74},{12,76},{14,78},{16,80}... | collective-permute-start | bytes 221192 | tf_op jit(solution)/shard_map/ppermute | solution.py:358
  51.3 2.7 %collective-permute-done.4 = bf16[144,256]{1,0:T(8,128)(2,1)S(1)} collective-permute-done((bf16[144,256]{1,0:T(8,128)(2,1)S(1)}, bf16[144,256]{1,0:T(8,128)(2,1)S(1)}, u32[]{:S(2)}, u32[]{:S(2)}) %collective-permute-start.4) | collective-permute-done | bytes 73760 | tf_op jit(solution)/shard_map/ppermute | solution.py:358
  54.0 2.2 %collective-permute-start.5 = (bf16[2,144,256]{2,1,0:T(8,128)(2,1)S(1)}, bf16[2,144,256]{2,1,0:T(8,128)(2,1)S(1)}, u32[]{:S(2)}, u32[]{:S(2)}) collective-permute-start(bf16[2,144,256]{2,1,0:T(8,128)(2,1)S(1)} %pad_maximum_fusion.3), channel_id=1, source_target_pairs={{0,128},{2,130},{4,132},{6,134},{8,136},{10,138},{12,140},{14,142}... | collective-permute-start | bytes 442376 | tf_op jit(solution)/shard_map/ppermute | solution.py:358
  56.2 4.5 %collective-permute-done.5 = bf16[2,144,256]{2,1,0:T(8,128)(2,1)S(1)} collective-permute-done((bf16[2,144,256]{2,1,0:T(8,128)(2,1)S(1)}, bf16[2,144,256]{2,1,0:T(8,128)(2,1)S(1)}, u32[]{:S(2)}, u32[]{:S(2)}) %collective-permute-start.5) | collective-permute-done | bytes 147488 | tf_op jit(solution)/shard_map/ppermute | solution.py:358
  60.7 0.0 copy-start.3
  60.8 0.0 copy-start.5
  60.8 2.2 %level_three.1 = bf16[8,80,256]{2,1,0:T(8,128)(2,1)S(1)} custom-call(bf16[8,80,256]{2,1,0:T(8,128)(2,1)S(1)} %all_to_all.10.block_ref.first_ref, bf16[4,144,256]{2,1,0:T(8,128)(2,1)S(1)} %pad_maximum_fusion.block_ref.second_ref, bf16[4,144,256]{2,1,0:T(8,128)(2,1)S(1)} %pad_maximum_fusion.1.third_ref, f32[8,512]{1,0:T(8,128)S(1)} %get-tuple-element.30.stat1_ref, ...), custom_call_target="tpu_custom_call" | custom-call | flops 300000000 | bytes 1703936 | tf_op jit(solution)/shard_map/level_three/pallas_call | solution.py:341
  62.9 0.0 copy-start.8
  62.9 0.7 copy-done.8
  63.7 3.7 %all-to-all-start.1 = ((bf16[8,80,256]{2,1,0:T(8,128)(2,1)}), bf16[8,80,256]{2,1,0:T(8,128)(2,1)S(1)}, u32[]{:S(2)}, u32[]{:S(2)}) async-start(bf16[8,80,256]{2,1,0:T(8,128)(2,1)} %copy-done.8), calls=%async_computation.1 | async-start | bytes 655360 | tf_op jit(solution)/shard_map/all_to_all | solution.py:408
  67.4 0.0 copy-done.22
  67.4 0.0 copy-done.3
  67.4 0.0 copy-done.5
  67.5 0.0 copy-done.1
  67.5 0.0 copy-start.19
  67.5 1.0 %copy-done.19 = bf16[512,384]{1,0:T(8,128)(2,1)S(1)} copy-done((bf16[512,384]{1,0:T(8,128)(2,1)S(1)}, bf16[512,384]{1,0:T(8,128)(2,1)}, u32[]{:S(2)}) %copy-start.19) | copy-done | bytes 393240
  68.5 4.4 %local_backward.1 = (f32[512,384]{1,0:T(8,128)S(1)}, f32[512,384]{1,0:T(8,128)S(1)}, f32[512,384]{1,0:T(8,128)S(1)}, bf16[384,512]{1,0:T(8,128)(2,1)}) custom-call(bf16[512,384]{1,0:T(8,128)(2,1)S(1)} %copy-done.1, bf16[512,384]{1,0:T(8,128)(2,1)S(1)} %copy-done.3, bf16[512,384]{1,0:T(8,128)(2,1)S(1)} %copy-done.5, bf16[512,384]{1,0:T(8,128)(2,1)S(1)} %copy-done.19, ...), custom_call_target="tpu_custom_call" | custom-call | flops 1000000000 | bytes 5160960 | tf_op jit(solution)/shard_map/local_backward/pallas_call | solution.py:341
  72.8 0.9 copy-done.9
  73.7 0.9 copy-done.11
  74.6 0.9 copy-done.13
  75.5 0.5 collective-permute-start.1
  76.1 1.5 %collective-permute-start.7 = (bf16[384,384]{1,0:T(8,128)(2,1)}, bf16[384,384]{1,0:T(8,128)(2,1)}, u32[]{:S(2)}, u32[]{:S(2)}) collective-permute-start(bf16[384,384]{1,0:T(8,128)(2,1)} %get-tuple-element.42.other_w_ref), channel_id=1, source_target_pairs={{0,1},{1,0},{2,3},{3,2},{4,5},{5,4},{6,7},{7,6},{8,9},{9,8},{10,11... | collective-permute-start | bytes 884744 | tf_op jit(solution)/shard_map/ppermute | solution.py:354
  77.5 0.7 all-to-all-done.1.back_ref
  78.3 0.5 kept_attended.1.own_kept_ref
  78.8 0.0 copy-start.7
  78.8 0.6 collective-permute-start.6
  79.4 1.0 %dynamic-slice_bitcast_fusion.tall_ref = bf16[512,384]{1,0:T(8,128)(2,1)S(1)} fusion(bf16[2,512,384]{2,1,0:T(8,128)(2,1)} %constant.40.clone, s32[]{:T(128)S(6)} %select_n.19), kind=kLoop, calls=%fused_computation | loop fusion | bytes 786436 | tf_op jit(solution)/shard_map/jit(dynamic_index_in_dim)/squeeze | solution.py:368
  80.4 0.0 copy-done.10
  80.4 0.0 copy-done.12
  80.5 0.0 copy-done.7
  80.5 0.0 copy-start.14
  80.5 1.1 %copy-done.14 = f32[512,384]{1,0:T(8,128)S(1)} copy-done((f32[512,384]{1,0:T(8,128)S(1)}, f32[512,384]{1,0:T(8,128)}, u32[]{:S(2)}) %copy-start.14) | copy-done | bytes 786456
  81.6 4.1 %final_grads.1 = (bf16[512,384]{1,0:T(8,128)(2,1)}, bf16[512,384]{1,0:T(8,128)(2,1)}, bf16[512,384]{1,0:T(8,128)(2,1)}) custom-call(bf16[512,384]{1,0:T(8,128)(2,1)S(1)} %copy-done.1, bf16[512,384]{1,0:T(8,128)(2,1)S(1)} %copy-done.3, bf16[512,384]{1,0:T(8,128)(2,1)S(1)} %copy-done.5, bf16[8,80,256]{2,1,0:T(8,128)(2,1)S(1)} %copy-done.7, ...), custom_call_target="tpu_custom_call" | custom-call | flops 200000000 | bytes 5767168 | tf_op jit(solution)/shard_map/final_grads/pallas_call | solution.py:341
  85.7 8.5 %collective-permute-done.7.other_w_ref = bf16[384,384]{1,0:T(8,128)(2,1)} collective-permute-done((bf16[384,384]{1,0:T(8,128)(2,1)}, bf16[384,384]{1,0:T(8,128)(2,1)}, u32[]{:S(2)}, u32[]{:S(2)}) %collective-permute-start.7) | collective-permute-done | bytes 294944 | tf_op jit(solution)/shard_map/ppermute | solution.py:354
  94.1 0.0 collective-permute-done.1.other_att_ref
  94.1 1.3 %collective-permute-done.6.other_kept_ref = bf16[384,64]{1,0:T(8,128)(2,1)S(1)} collective-permute-done((bf16[384,64]{1,0:T(8,128)(2,1)S(1)}, bf16[384,64]{1,0:T(8,128)(2,1)S(1)}, u32[]{:S(2)}, u32[]{:S(2)}) %collective-permute-start.6) | collective-permute-done | bytes 49184 | tf_op jit(solution)/shard_map/ppermute | solution.py:354
  95.4 3.0 %mix_rows.1 = bf16[512,384]{1,0:T(8,128)(2,1)} custom-call(bf16[384,512]{1,0:T(8,128)(2,1)} %get-tuple-element.26.own_att_ref, bf16[384,512]{1,0:T(8,128)(2,1)} %collective-permute-done.1.other_att_ref, bf16[384,64]{1,0:T(8,128)(2,1)S(1)} %kept_attended.1.own_kept_ref, bf16[384,64]{1,0:T(8,128)(2,1)S(1)} %collective-permute-done.6.other_kept_ref, ...), custom_call_target="tpu_custom_call" | custom-call | flops 400000000 | bytes 2654208 | tf_op jit(solution)/shard_map/mix_rows/pallas_call | solution.py:341
  (18 shorter events, 0.1 us)
Async XLA Ops:
  0.6 11.2 %collective-permute-start = (bf16[512,384]{1,0:T(8,128)(2,1)}, bf16[512,384]{1,0:T(8,128)(2,1)S(1)}, u32[]{:S(2)}, u32[]{:S(2)}) collective-permute-start(bf16[512,384]{1,0:T(8,128)(2,1)} %own_cot_ref.1), channel_id=1, source_target_pairs={{0,1},{1,0},{2,3},{3,2},{4,5},{5,4},{6,7},{7,6},{8,9},{9,8},{10,11... | collective-permute-start | bytes 1179656 | tf_op jit(solution)/shard_map/ppermute | solution.py:354
  3.0 1.0 %copy-start = (bf16[512,384]{1,0:T(8,128)(2,1)S(1)}, bf16[512,384]{1,0:T(8,128)(2,1)}, u32[]{:S(2)}) copy-start(bf16[512,384]{1,0:T(8,128)(2,1)} %q_ref.7) | copy-start | bytes 1179652
  4.0 1.0 %copy-start.2 = (bf16[512,384]{1,0:T(8,128)(2,1)S(1)}, bf16[512,384]{1,0:T(8,128)(2,1)}, u32[]{:S(2)}) copy-start(bf16[512,384]{1,0:T(8,128)(2,1)} %k_ref.7) | copy-start | bytes 1179652
  5.0 1.0 %copy-start.4 = (bf16[512,384]{1,0:T(8,128)(2,1)S(1)}, bf16[512,384]{1,0:T(8,128)(2,1)}, u32[]{:S(2)}) copy-start(bf16[512,384]{1,0:T(8,128)(2,1)} %v_ref.7) | copy-start | bytes 1179652
  6.0 3.4 %copy-start.21 = (bf16[384,768]{1,0:T(8,128)(2,1)S(1)}, bf16[384,768]{1,0:T(8,128)(2,1)}, u32[]{:S(2)}) copy-start(bf16[384,768]{1,0:T(8,128)(2,1)} %param.13) | copy-start | bytes 1769476
  9.4 1.2 %copy-start.20 = (bf16[2,384,512]{2,1,0:T(8,128)(2,1)S(1)}, bf16[2,384,512]{2,1,0:T(8,128)(2,1)}, u32[]{:S(2)}) copy-start(bf16[2,384,512]{2,1,0:T(8,128)(2,1)} %constant.39.clone) | copy-start | bytes 2359300
  10.6 1.1 %copy-start.17 = (bf16[512,384]{1,0:T(8,128)(2,1)S(1)}, bf16[512,384]{1,0:T(8,128)(2,1)}, u32[]{:S(2)}) copy-start(bf16[512,384]{1,0:T(8,128)(2,1)} %own_cot_ref.1) | copy-start | bytes 1179652
  14.3 0.8 copy-start.18
  15.1 17.0 %copy-start.6 = (bf16[8,80,256]{2,1,0:T(8,128)(2,1)}, bf16[8,80,256]{2,1,0:T(8,128)(2,1)S(1)}, u32[]{:S(2)}) copy-start(bf16[8,80,256]{2,1,0:T(8,128)(2,1)S(1)} %get-tuple-element.27.sent_ref) | copy-start | bytes 983044
  15.1 17.0 %copy-start.15 = (bf16[128,512]{1,0:T(8,128)(2,1)S(1)}, bf16[128,512]{1,0:T(8,128)(2,1)}, u32[]{:S(2)}) copy-start(bf16[128,512]{1,0:T(8,128)(2,1)} %constant.41.clone.pick_ref.pick2_ref) | copy-start | bytes 393220
  32.8 9.1 %collective-permute-start.2 = (bf16[144,256]{1,0:T(8,128)(2,1)S(1)}, bf16[144,256]{1,0:T(8,128)(2,1)S(1)}, u32[]{:S(2)}, u32[]{:S(2)}) collective-permute-start(bf16[144,256]{1,0:T(8,128)(2,1)S(1)} %get-tuple-element.28), channel_id=1, source_target_pairs={{0,16},{2,18},{4,20},{6,22},{8,24},{10,26},{12,28},{14,30},{16,0},... | collective-permute-start | bytes 221192 | tf_op jit(solution)/shard_map/ppermute | solution.py:358
  42.0 5.3 %copy-start.16 = (bf16[128,512]{1,0:T(8,128)(2,1)S(1)}, bf16[128,512]{1,0:T(8,128)(2,1)}, u32[]{:S(2)}) copy-start(bf16[128,512]{1,0:T(8,128)(2,1)} %constant.42.clone.pick_ref.pick3_ref) | copy-start | bytes 393220
  42.0 5.2 %collective-permute-start.3 = (bf16[2,144,256]{2,1,0:T(8,128)(2,1)S(1)}, bf16[2,144,256]{2,1,0:T(8,128)(2,1)S(1)}, u32[]{:S(2)}, u32[]{:S(2)}) collective-permute-start(bf16[2,144,256]{2,1,0:T(8,128)(2,1)S(1)} %pad_maximum_fusion.2), channel_id=1, source_target_pairs={{0,32},{2,34},{4,36},{6,38},{8,40},{10,42},{12,44},{14,46},{16,48}... | collective-permute-start | bytes 442376 | tf_op jit(solution)/shard_map/ppermute | solution.py:358
  48.0 5.9 %collective-permute-start.4 = (bf16[144,256]{1,0:T(8,128)(2,1)S(1)}, bf16[144,256]{1,0:T(8,128)(2,1)S(1)}, u32[]{:S(2)}, u32[]{:S(2)}) collective-permute-start(bf16[144,256]{1,0:T(8,128)(2,1)S(1)} %get-tuple-element.29), channel_id=1, source_target_pairs={{0,64},{2,66},{4,68},{6,70},{8,72},{10,74},{12,76},{14,78},{16,80}... | collective-permute-start | bytes 221192 | tf_op jit(solution)/shard_map/ppermute | solution.py:358
  54.0 6.7 %collective-permute-start.5 = (bf16[2,144,256]{2,1,0:T(8,128)(2,1)S(1)}, bf16[2,144,256]{2,1,0:T(8,128)(2,1)S(1)}, u32[]{:S(2)}, u32[]{:S(2)}) collective-permute-start(bf16[2,144,256]{2,1,0:T(8,128)(2,1)S(1)} %pad_maximum_fusion.3), channel_id=1, source_target_pairs={{0,128},{2,130},{4,132},{6,134},{8,136},{10,138},{12,140},{14,142}... | collective-permute-start | bytes 442376 | tf_op jit(solution)/shard_map/ppermute | solution.py:358
  60.7 6.7 %copy-start.3 = (bf16[512,384]{1,0:T(8,128)(2,1)S(1)}, bf16[512,384]{1,0:T(8,128)(2,1)}, u32[]{:S(2)}) copy-start(bf16[512,384]{1,0:T(8,128)(2,1)} %k_ref.7) | copy-start | bytes 1179652
  60.8 6.7 %copy-start.5 = (bf16[512,384]{1,0:T(8,128)(2,1)S(1)}, bf16[512,384]{1,0:T(8,128)(2,1)}, u32[]{:S(2)}) copy-start(bf16[512,384]{1,0:T(8,128)(2,1)} %v_ref.7) | copy-start | bytes 1179652
  62.9 0.7 copy-start.8
  63.6 3.8 %copy-start.22 = (f32[2,8,512]{2,1,0:T(8,128)S(1)}, f32[2,8,512]{2,1,0:T(8,128)}, u32[]{:S(2)}) copy-start(f32[2,8,512]{2,1,0:T(8,128)} %constant.43.clone) | copy-start | bytes 98308
  63.6 3.8 %copy-start.1 = (bf16[512,384]{1,0:T(8,128)(2,1)S(1)}, bf16[512,384]{1,0:T(8,128)(2,1)}, u32[]{:S(2)}) copy-start(bf16[512,384]{1,0:T(8,128)(2,1)} %q_ref.7) | copy-start | bytes 1179652
  63.7 14.6 %all-to-all-start.1 = ((bf16[8,80,256]{2,1,0:T(8,128)(2,1)}), bf16[8,80,256]{2,1,0:T(8,128)(2,1)S(1)}, u32[]{:S(2)}, u32[]{:S(2)}) async-start(bf16[8,80,256]{2,1,0:T(8,128)(2,1)} %copy-done.8), calls=%async_computation.1 | async-start | bytes 655360 | tf_op jit(solution)/shard_map/all_to_all | solution.py:408
  67.5 1.0 %copy-start.19 = (bf16[512,384]{1,0:T(8,128)(2,1)S(1)}, bf16[512,384]{1,0:T(8,128)(2,1)}, u32[]{:S(2)}) copy-start(bf16[512,384]{1,0:T(8,128)(2,1)} %copy-done.18) | copy-start | bytes 1179652
  72.8 0.9 copy-start.9
  73.7 0.9 copy-start.11
  74.6 0.9 copy-start.13
  75.5 18.6 %collective-permute-start.1 = (bf16[384,512]{1,0:T(8,128)(2,1)}, bf16[384,512]{1,0:T(8,128)(2,1)}, u32[]{:S(2)}, u32[]{:S(2)}) collective-permute-start(bf16[384,512]{1,0:T(8,128)(2,1)} %get-tuple-element.26.own_att_ref), channel_id=1, source_target_pairs={{0,1},{1,0},{2,3},{3,2},{4,5},{5,4},{6,7},{7,6},{8,9},{9,8},{10,11... | collective-permute-start | bytes 1179656 | tf_op jit(solution)/shard_map/ppermute | solution.py:354
  76.1 18.1 %collective-permute-start.7 = (bf16[384,384]{1,0:T(8,128)(2,1)}, bf16[384,384]{1,0:T(8,128)(2,1)}, u32[]{:S(2)}, u32[]{:S(2)}) collective-permute-start(bf16[384,384]{1,0:T(8,128)(2,1)} %get-tuple-element.42.other_w_ref), channel_id=1, source_target_pairs={{0,1},{1,0},{2,3},{3,2},{4,5},{5,4},{6,7},{7,6},{8,9},{9,8},{10,11... | collective-permute-start | bytes 884744 | tf_op jit(solution)/shard_map/ppermute | solution.py:354
  78.3 2.1 %copy-start.10 = (f32[512,384]{1,0:T(8,128)S(1)}, f32[512,384]{1,0:T(8,128)}, u32[]{:S(2)}) copy-start(f32[512,384]{1,0:T(8,128)} %copy-done.9) | copy-start | bytes 2359300
  78.3 2.2 %copy-start.12 = (f32[512,384]{1,0:T(8,128)S(1)}, f32[512,384]{1,0:T(8,128)}, u32[]{:S(2)}) copy-start(f32[512,384]{1,0:T(8,128)} %copy-done.11) | copy-start | bytes 2359300
  78.8 1.7 %copy-start.7 = (bf16[8,80,256]{2,1,0:T(8,128)(2,1)S(1)}, bf16[8,80,256]{2,1,0:T(8,128)(2,1)}, u32[]{:S(2)}) copy-start(bf16[8,80,256]{2,1,0:T(8,128)(2,1)} %copy-done.6) | copy-start | bytes 983044
  78.8 16.6 %collective-permute-start.6 = (bf16[384,64]{1,0:T(8,128)(2,1)S(1)}, bf16[384,64]{1,0:T(8,128)(2,1)S(1)}, u32[]{:S(2)}, u32[]{:S(2)}) collective-permute-start(bf16[384,64]{1,0:T(8,128)(2,1)S(1)} %kept_attended.1.own_kept_ref), channel_id=1, source_target_pairs={{0,1},{1,0},{2,3},{3,2},{4,5},{5,4},{6,7},{7,6},{8,9},{9,8},{10,11... | collective-permute-start | bytes 147464 | tf_op jit(solution)/shard_map/ppermute | solution.py:354
  80.5 1.1 %copy-start.14 = (f32[512,384]{1,0:T(8,128)S(1)}, f32[512,384]{1,0:T(8,128)}, u32[]{:S(2)}) copy-start(f32[512,384]{1,0:T(8,128)} %copy-done.13) | copy-start | bytes 2359300
where the time goes:
time: 99.8 us; the launch traced here: 98.3 us
  waiting for transfers between devices  26.9 us (27%)
  Pallas kernels  21.6 us (22%)
  starting transfers between devices  20.4 us (20%)
  blocking collectives  17 us (17%)
  local copies, waits for them, and re-layouts  11.6 us (12%)
    pallas_call x9, Pallas kernels, call(): pl.pallas_call(kernel, out_shape=shapes, in_specs=[pl.BlockSpec(memory_sp...  21.6 us
    all_to_all x1, blocking collectives, body(): block1 = lax.all_to_all(sent, 'seq', 0, 0, axis_index_groups=octets)  17 us
    ppermute x4, waiting for transfers between devices, flip(): lax.ppermute(array, 'seq', [(i, i ^ 1 << bit) for i in range(lax.axis_siz...  15.3 us
    ppermute x4, starting transfers between devices, flip(): lax.ppermute(array, 'seq', [(i, i ^ 1 << bit) for i in range(lax.axis_siz...  11.7 us
    ppermute x4, waiting for transfers between devices, partner(): return lax.ppermute(array, 'head', [(0, 1), (1, 0)])  10.8 us
    unnamed x46, local copies, waits for them, and re-layouts  9.75 us
    ppermute x4, starting transfers between devices, partner(): return lax.ppermute(array, 'head', [(0, 1), (1, 0)])  5.01 us
    all_to_all x1, starting transfers between devices, body(): back = lax.all_to_all(returned, 'seq', 0, 0, axis_index_groups=octets)  3.75 us
  transfers between devices with their start and end apart: 9, of which 8 were waited for; matrix products, arithmetic and copies ran while one was open for 2% of the time, Pallas kernels for 13%

commit v1 on v0

v1 whole, which is shorter than its diff:
```python
import jax
import jax.numpy as jnp
import numpy as np
from jax import lax
from jax.experimental import pallas as pl
from jax.experimental.pallas import tpu as pltpu
from jax.sharding import PartitionSpec as P

HEAD_DIM = 64
LOCAL_HEADS = 6
PAIRS = LOCAL_HEADS // 2
ROWS = 512
KEPT = 64
WIDE = 384
SCALE = HEAD_DIM ** -0.5
BF = jnp.bfloat16
F32 = jnp.float32
MASKED = 1e30
VMEM_LIMIT = 24 * 1024 * 1024


def iota(shape, axis):
    return lax.broadcasted_iota(jnp.int32, shape, axis)


def kept_row(place, head):
    phase = lax.shift_right_logical(head, 3)
    third = 16 * place + phase
    later = place - 4
    second = 4 * (later + lax.shift_right_arithmetic(later * 11, 5) + 1) + phase
    last = place - 16
    group = lax.shift_right_arithmetic(last * 171, 9)
    spot = last - 3 * group
    first = 4 * group + spot + jnp.where(spot >= phase, 1, 0)
    chosen = jnp.where(place < 4, third, jnp.where(place < 16, second, first))
    return 8 * chosen + jnp.bitwise_and(head, 7)


def one_hot(match):
    return jnp.where(match, 1.0, 0.0).astype(BF)


def flat_pick(head):
    return one_hot(iota((KEPT, ROWS), 1) == kept_row(iota((KEPT, ROWS), 0), head))


def tall_pick(head):
    return one_hot(iota((ROWS, KEPT), 0) == kept_row(iota((ROWS, KEPT), 1), head))


def subset_pick(wide, narrow):
    place = iota((128, ROWS), 0)
    group = lax.shift_right_logical(place, narrow)
    target = lax.shift_left(group, wide) + jnp.bitwise_and(place, (1 << narrow) - 1)
    return one_hot(iota((128, ROWS), 1) == target)


def dot_nn(left, right):
    return lax.dot_general(left, right, (((1,), (0,)), ((), ())), preferred_element_type=F32)


def dot_nt(left, right):
    return lax.dot_general(left, right, (((1,), (1,)), ((), ())), preferred_element_type=F32)


def dot_tn(left, right):
    return lax.dot_general(left, right, (((0,), (0,)), ((), ())), preferred_element_type=F32)


def split2(value):
    high = value.astype(BF)
    return high, (value - high.astype(F32)).astype(BF)


def split3(value):
    high = value.astype(BF)
    rest = value - high.astype(F32)
    middle = rest.astype(BF)
    return high, middle, (rest - middle.astype(F32)).astype(BF)


def stat_block(log_row, delta_row):
    pieces = split3(log_row) + split3(delta_row)
    rows = [piece.astype(F32) for piece in pieces]
    zero = jnp.zeros_like(log_row)
    return jnp.concatenate(rows + [zero, zero], axis=0)


def stat_rows(block):
    block = block.astype(F32)
    log_row = block[0:1] + block[1:2] + block[2:3]
    delta_row = block[3:4] + block[4:5] + block[5:6]
    return log_row, delta_row


def log_add(first, second):
    peak = jnp.maximum(first, second)
    return peak + jnp.log(jnp.exp(first - peak) + jnp.exp(second - peak))


def span(local):
    return slice(local * HEAD_DIM, (local + 1) * HEAD_DIM)


def cols(pair):
    return slice(pair * 128, (pair + 1) * 128)


def owner_of(info_ref, local):
    return jnp.bitwise_xor(info_ref[1], local)


def head_of(half, local):
    return half * LOCAL_HEADS + local


def local_forward(info_ref, q_ref, k_ref, v_ref, q_out_ref, k_out_ref, v_out_ref, out_t_ref, log_ref,
                  att_t_ref, kept_out_ref, kept_log_ref, sems):
    moves = []
    for pair in range(PAIRS):
        for which, (source, target) in enumerate(((q_ref, q_out_ref), (k_ref, k_out_ref), (v_ref, v_out_ref))):
            move = pltpu.make_async_copy(
                source.at[:, cols(pair)], target.at[:, cols(pair)], sems.at[pair, which]
            )
            move.start()
            moves.append(move)
    log_ref[LOCAL_HEADS:, :] = jnp.zeros((8 - LOCAL_HEADS, ROWS), F32)
    kept_log_ref[LOCAL_HEADS:, :] = jnp.zeros((8 - LOCAL_HEADS, KEPT), F32)
    for local in range(LOCAL_HEADS):
        if local % 2 == 0:
            for move in moves[local // 2 * 3:local // 2 * 3 + 3]:
                move.wait()
        scores = dot_nt(k_out_ref[:, span(local)], q_out_ref[:, span(local)] * BF(SCALE))
        peak = jnp.max(scores, axis=0, keepdims=True)
        powers = jnp.exp(scores - peak)
        total = jnp.sum(powers, axis=0, keepdims=True)
        out_t = dot_tn(v_out_ref[:, span(local)], powers.astype(BF)) / total
        log_row = peak + jnp.log(total)
        out_t_ref[span(local), :] = out_t
        log_ref[local:local + 1, :] = log_row
        head = head_of(info_ref[0], local)
        is_kept = jnp.bitwise_and(iota((1, ROWS), 1), 7) == jnp.bitwise_and(head, 7)
        att_t_ref[span(local), :] = jnp.where(is_kept, 0.0, out_t).astype(BF)
        hot = flat_pick(head)
        high, low = split2(out_t)
        kept_out_ref[:, span(local)] = dot_nt(hot, high) + dot_nt(hot, low)
        kept_log_ref[local:local + 1, :] = stat_rows(dot_nt(stat_block(log_row, log_row).astype(BF), hot))[0]


def pack_rows(info_ref, q_ref, k_ref, v_ref, own_cot_ref, other_cot_ref, w_ref, out_t_ref, log_ref,
              grad_ref, delta_ref, payload_ref):
    own_w = w_ref[:, pl.ds(pl.multiple_of(info_ref[0] * WIDE, 128), WIDE)]
    other_w = w_ref[:, pl.ds(pl.multiple_of((1 - info_ref[0]) * WIDE, 128), WIDE)]
    grad = (dot_nt(own_cot_ref[...], own_w) + dot_nt(other_cot_ref[...], other_w)).astype(BF)
    grad_ref[...] = grad
    product = grad.astype(F32).T * out_t_ref[...]
    delta_ref[LOCAL_HEADS:, :] = jnp.zeros((8 - LOCAL_HEADS, ROWS), F32)
    for local in range(LOCAL_HEADS):
        owner = owner_of(info_ref, local)
        hot = flat_pick(head_of(info_ref[0], local))
        delta = jnp.sum(product[span(local)], axis=0, keepdims=True)
        delta_ref[local:local + 1, :] = delta
        joined = jnp.concatenate([part[:, span(local)] for part in (q_ref, k_ref, v_ref, grad)], axis=1)
        rows = dot_nn(hot, joined).astype(BF)
        payload_ref[owner, :KEPT, :] = rows[:, :128]
        payload_ref[owner, KEPT:2 * KEPT, :] = rows[:, 128:]
        stats = stat_block(log_ref[local:local + 1, :], delta).astype(BF)
        payload_ref[owner, 2 * KEPT:, :] = widen_stats(dot_nt(stats, hot))
    for spare in range(LOCAL_HEADS, 8):
        payload_ref[owner_of(info_ref, spare)] = jnp.zeros((2 * KEPT + 16, 128), BF)


def widen_stats(block):
    if block.shape[1] < 128:
        block = jnp.concatenate([block, jnp.zeros((8, 128 - block.shape[1]), F32)], axis=1)
    return jnp.concatenate([block, jnp.zeros((8, 128), F32)], axis=0).astype(BF)


def local_backward(info_ref, q_ref, k_ref, v_ref, grad_ref, log_ref, delta_ref, dq_ref, dk_ref, dv_ref):
    for pair in range(PAIRS):
        dq_t, dk, dv = [], [], []
        for local in (2 * pair, 2 * pair + 1):
            query = q_ref[:, span(local)] * BF(SCALE)
            key = k_ref[:, span(local)]
            grad = grad_ref[:, span(local)]
            head = head_of(info_ref[0], local)
            is_kept = jnp.bitwise_and(iota((1, ROWS), 1), 7) == jnp.bitwise_and(head, 7)
            log_row = jnp.where(is_kept, MASKED, log_ref[local:local + 1, :])
            probability = jnp.exp(dot_nt(key, query) - log_row)
            score_grad = probability * (dot_nt(v_ref[:, span(local)], grad) - delta_ref[local:local + 1, :])
            score_grad = score_grad.astype(BF)
            dv.append(dot_nn(probability.astype(BF), grad))
            dk.append(dot_nn(score_grad, query))
            dq_t.append(dot_tn(key, score_grad))
        dq_ref[:, cols(pair)] = jnp.concatenate(dq_t, axis=0).T * SCALE
        dk_ref[:, cols(pair)] = jnp.concatenate(dk, axis=1)
        dv_ref[:, cols(pair)] = jnp.concatenate(dv, axis=1)


def set_stats(query, key, value, grad):
    scores = dot_nt(key, query)
    peak = jnp.max(scores, axis=0, keepdims=True)
    powers = jnp.exp(scores - peak)
    total = jnp.sum(powers, axis=0, keepdims=True)
    prob_grad = dot_nt(value, grad)
    delta = jnp.sum(powers * prob_grad, axis=0, keepdims=True) / total
    return powers, total, peak + jnp.log(total), delta


def merge(old_log, old_delta, new_log, new_delta):
    joint = log_add(old_log, new_log)
    return joint, jnp.exp(old_log - joint) * old_delta + jnp.exp(new_log - joint) * new_delta


def split_set(joined, other):
    return joined[:, :64] * BF(SCALE), joined[:, 64:], other[:, :64], other[:, 64:]


def first_set(block_ref):
    return split_set(
        block_ref[:, :KEPT, :].reshape(ROWS, 128), block_ref[:, KEPT:2 * KEPT, :].reshape(ROWS, 128)
    )


def later_set(block_ref):
    return split_set(block_ref[:, :128, :].reshape(ROWS, 128), block_ref[:, 128:256, :].reshape(ROWS, 128))


def later_stats(block_ref):
    return stat_rows(jnp.concatenate([block_ref[i, 256:264, :].astype(F32) for i in range(4)], axis=1))


def level_one(block_ref, payload_ref, stat_ref, out_t_ref):
    query, key, value, grad = first_set(block_ref)
    stats = jnp.concatenate([block_ref[i, 128:136, :KEPT].astype(F32) for i in range(8)], axis=1)
    old_log, old_delta = stat_rows(stats)
    powers, total, new_log, new_delta = set_stats(query, key, value, grad)
    joint, delta = merge(old_log, old_delta, new_log, new_delta)
    out_t_ref[...] = dot_tn(value, powers.astype(BF)) * (jnp.exp(new_log - joint) / total)
    stat_ref[0:1, :] = joint
    stat_ref[1:2, :] = delta
    stat_ref[2:, :] = jnp.zeros((6, ROWS), F32)
    payload_ref[:128, :] = block_ref[:, :16, :].reshape(128, 128)
    payload_ref[128:256, :] = block_ref[:, KEPT:KEPT + 16, :].reshape(128, 128)
    picked = dot_nt(stat_block(joint, delta).astype(BF), subset_pick(6, 4))
    payload_ref[256:, :] = widen_stats(picked)


def level_two(block_ref, payload_ref, stat_ref, out_t_ref):
    pick = subset_pick(4, 2)
    query, key, value, grad = later_set(block_ref)
    old_log, old_delta = later_stats(block_ref)
    powers, total, new_log, new_delta = set_stats(query, key, value, grad)
    joint, delta = merge(old_log, old_delta, new_log, new_delta)
    weight = (jnp.exp(new_log - joint) / total)[:, :128]
    out_t_ref[...] = dot_tn(value, powers[:, :128].astype(BF)) * weight
    stat_ref[0:1, :] = joint
    stat_ref[1:2, :] = delta
    stat_ref[2:, :] = jnp.zeros((6, ROWS), F32)
    payload_ref[:128, :] = dot_nn(pick, block_ref[:, :128, :].reshape(ROWS, 128)).astype(BF)
    payload_ref[128:256, :] = dot_nn(pick, block_ref[:, 128:256, :].reshape(ROWS, 128)).astype(BF)
    picked = dot_nt(stat_block(joint, delta).astype(BF), pick)
    payload_ref[256:, :] = widen_stats(picked)


def set_grads(data, log_row, delta_row, own):
    query, key, value, grad = data
    probability = jnp.exp(dot_nt(key, query) - log_row)
    score_grad = (probability * (dot_nt(value, grad) - delta_row)).astype(BF)
    key_grad = dot_nn(score_grad[:own], query)
    value_grad = dot_nn(probability[:own].astype(BF), grad)
    query_grad_t = dot_tn(key, score_grad[:, :own]) * SCALE
    return query_grad_t, jnp.concatenate([key_grad, value_grad], axis=1)


def spread_lanes(value, pick):
    high, low = split2(value)
    return dot_nn(high, pick) + dot_nn(low, pick)


def spread_stats(log_row, delta_row, pick):
    return stat_rows(dot_nn(stat_block(log_row, delta_row).astype(BF), pick))


def level_three(first_ref, second_ref, third_ref, stat1_ref, stat2_ref, out1_ref, out2_ref, payload_ref):
    pick2 = subset_pick(6, 4)
    pick3 = subset_pick(4, 2)
    in_second = jnp.sum(pick2.astype(F32), axis=0, keepdims=True) > 0.5
    in_third = jnp.sum(pick3.astype(F32), axis=0, keepdims=True) > 0.5

    data3 = later_set(third_ref)
    query, key, value, grad = data3
    old_log, old_delta = later_stats(third_ref)
    powers, total, new_log, new_delta = set_stats(query, key, value, grad)
    log3, delta3 = merge(old_log, old_delta, new_log, new_delta)
    weight = (jnp.exp(new_log - log3) / total)[:, :128]
    out3 = dot_tn(value, powers[:, :128].astype(BF)) * weight
    dq3, dkv3 = set_grads(data3, log3, delta3, 128)

    spread_log, spread_delta = spread_stats(log3[:, :128], delta3[:, :128], pick3)
    log2 = jnp.where(in_third, spread_log, stat2_ref[0:1, :])
    delta2 = jnp.where(in_third, spread_delta, stat2_ref[1:2, :])
    data2 = later_set(second_ref)
    dq2, dkv2 = set_grads(data2, log2, delta2, 128)
    own3 = pick3[:32, :128]
    own_lane = lax.broadcasted_iota(jnp.int32, (1, 128), 1) < 32
    merged_t = jnp.concatenate([dq3, out3], axis=0)
    merged_t = jnp.where(own_lane, merged_t, 0.0)
    own_pick = jnp.concatenate([own3, jnp.zeros((96, 128), BF)], axis=0)
    fade2 = jnp.exp(stat2_ref[0:1, :128] - log2[:, :128])
    base_t = jnp.concatenate([dq2, out2_ref[...] * fade2], axis=0)
    merged_t = base_t + spread_lanes(merged_t, own_pick)
    high, low = split2(dkv3[:32])
    dkv2 = dkv2 + dot_tn(own3, high) + dot_tn(own3, low)

    spread_log, spread_delta = spread_stats(log2[:, :128], delta2[:, :128], pick2)
    log1 = jnp.where(in_second, spread_log, stat1_ref[0:1, :])
    delta1 = jnp.where(in_second, spread_delta, stat1_ref[1:2, :])
    data1 = first_set(first_ref)
    dq1, dkv1 = set_grads(data1, log1, delta1, ROWS)
    fade1 = jnp.exp(stat1_ref[0:1, :] - log1)
    base_t = jnp.concatenate([dq1, out1_ref[...] * fade1], axis=0)
    merged_t = base_t + spread_lanes(merged_t, pick2)
    high, low = split2(dkv2)
    dkv1 = dkv1 + dot_tn(pick2, high) + dot_tn(pick2, low)

    payload_ref[:, :KEPT, :] = merged_t.T.astype(BF).reshape(8, KEPT, 128)
    payload_ref[:, KEPT:2 * KEPT, :] = dkv1.astype(BF).reshape(8, KEPT, 128)
    stats = stat_block(log1, delta1)
    for owner in range(8):
        payload_ref[owner, 2 * KEPT:, :] = widen_stats(stats[:, owner * KEPT:(owner + 1) * KEPT])


def returned_stats(block):
    return stat_rows(block[2 * KEPT:2 * KEPT + 8, :KEPT])


def kept_attended(info_ref, back_ref, kept_out_ref, kept_log_ref, att_ref):
    for local in range(LOCAL_HEADS):
        block = back_ref[owner_of(info_ref, local)]
        log_total, _ = returned_stats(block)
        fade = jnp.exp(kept_log_ref[local:local + 1, :] - log_total)
        fade = jnp.broadcast_to(fade, (HEAD_DIM, KEPT)).T
        sparse = block[:KEPT, 64:].astype(F32)
        att_ref[:, span(local)] = (kept_out_ref[:, span(local)] * fade + sparse).astype(BF)


def diagonal(first, second):
    zero = jnp.zeros_like(first)
    return jnp.concatenate(
        [jnp.concatenate([first, zero], axis=1), jnp.concatenate([zero, second], axis=1)], axis=0
    )


def tall_pair(half, pair):
    return jnp.concatenate([tall_pick(head_of(half, 2 * pair)), tall_pick(head_of(half, 2 * pair + 1))], axis=1)


def final_grads(info_ref, q_ref, k_ref, v_ref, sent_ref, back_ref, dq_ref, dk_ref, dv_ref,
                dq_out_ref, dk_out_ref, dv_out_ref, held, sems):
    moves = []
    for pair in range(PAIRS):
        sent = [sent_ref[owner_of(info_ref, 2 * pair + spot)] for spot in range(2)]
        back = [back_ref[owner_of(info_ref, 2 * pair + spot)] for spot in range(2)]
        key = k_ref[:, cols(pair)]
        query = diagonal(*(block[:KEPT, :64] * BF(SCALE) for block in sent))
        grad = diagonal(*(block[KEPT:2 * KEPT, 64:] for block in sent))
        stats = [returned_stats(block) for block in back]
        log_total = jnp.concatenate([stat[0] for stat in stats], axis=1)
        delta = jnp.concatenate([stat[1] for stat in stats], axis=1)
        tall = tall_pair(info_ref[0], pair)
        probability = jnp.exp(dot_nt(key, query) - log_total)
        score_grad = (probability * (dot_nt(v_ref[:, cols(pair)], grad) - delta)).astype(BF)
        more_dk = diagonal(*(block[KEPT:2 * KEPT, :64] for block in back))
        more_dv = diagonal(*(block[KEPT:2 * KEPT, 64:] for block in back))
        dk = dot_nn(jnp.concatenate([score_grad, tall], axis=1), jnp.concatenate([query, more_dk], axis=0))
        dv = dot_nn(
            jnp.concatenate([probability.astype(BF), tall], axis=1), jnp.concatenate([grad, more_dv], axis=0)
        )
        crossed = dot_tn(score_grad, key) * SCALE
        more_dq = diagonal(
            crossed[:64, :64] + back[0][:KEPT, :64].astype(F32), crossed[64:, 64:] + back[1][:KEPT, :64].astype(F32)
        )
        dq = dot_nn(jnp.concatenate([tall, tall], axis=1), jnp.concatenate(split2(more_dq), axis=0))
        for which, (base_ref, more, target) in enumerate(
            ((dq_ref, dq, dq_out_ref), (dk_ref, dk, dk_out_ref), (dv_ref, dv, dv_out_ref))
        ):
            held[pair, which] = (base_ref[:, cols(pair)] + more).astype(BF)
            move = pltpu.make_async_copy(held.at[pair, which], target.at[:, cols(pair)], sems.at[pair, which])
            move.start()
            moves.append(move)
    for move in moves:
        move.wait()


def mix_base(own_att_ref, other_att_ref, own_w_ref, other_w_ref, base_ref):
    base_ref[...] = dot_tn(own_att_ref[...], own_w_ref[...]) + dot_tn(other_att_ref[...], other_w_ref[...])


def spread_kept(half, kept_ref):
    return jnp.concatenate(
        [
            dot_nn(
                tall_pair(half, pair), diagonal(kept_ref[:, span(2 * pair)], kept_ref[:, span(2 * pair + 1)])
            ).astype(BF)
            for pair in range(PAIRS)
        ],
        axis=1,
    )


def mix_own(info_ref, base_ref, kept_ref, w_ref, out_ref):
    out_ref[...] = base_ref[...] + dot_nn(spread_kept(info_ref[0], kept_ref), w_ref[...])


def mix_other(info_ref, base_ref, kept_ref, w_ref, out_ref, held, sems):
    rows = spread_kept(1 - info_ref[0], kept_ref)
    moves = []
    for pair in range(PAIRS):
        held[pair] = (base_ref[:, cols(pair)] + dot_nn(rows, w_ref[:, cols(pair)])).astype(BF)
        move = pltpu.make_async_copy(held.at[pair], out_ref.at[:, cols(pair)], sems.at[pair])
        move.start()
        moves.append(move)
    for move in moves:
        move.wait()


def call(kernel, outs, args, flops=0, info=None, after=(), scratch=(), far_in=False, far_out=False):
    shapes = tuple(jax.ShapeDtypeStruct(*out) for out in outs)
    moved = sum(a.size * a.dtype.itemsize for a in args) + sum(
        int(np.prod(shape)) * jnp.dtype(dtype).itemsize for shape, dtype in outs
    )
    scalars = () if info is None else (info,)
    last = len(scalars) + len(args)

    def run(*refs):
        kernel(*refs[:last], *refs[last + len(after):])

    run.__name__ = kernel.__name__
    near, far = pl.BlockSpec(memory_space=pltpu.VMEM), pl.BlockSpec(memory_space=pltpu.HBM)
    return pl.pallas_call(
        run,
        out_shape=shapes,
        in_specs=[pl.BlockSpec(memory_space=pltpu.SMEM)] * len(scalars)
        + [far if far_in else near] * len(args)
        + [pl.BlockSpec(memory_space=pl.ANY)] * len(after),
        out_specs=(far if far_out else near,) * len(outs),
        scratch_shapes=list(scratch),
        compiler_params=pltpu.CompilerParams(vmem_limit_bytes=VMEM_LIMIT),
        cost_estimate=pl.CostEstimate(flops=flops, bytes_accessed=moved, transcendentals=0),
        name=kernel.__name__,
    )(*scalars, *args, *after)


def partner(array):
    return lax.ppermute(array, "head", [(0, 1), (1, 0)])


def flip(array, mask):
    return lax.ppermute(array, "seq", [(i, i ^ mask) for i in range(lax.axis_size("seq"))])


def gather_pair(array, first, second):
    pair = jnp.stack([array, flip(array, first)])
    return jnp.concatenate([pair, flip(pair, second)])


def body(queries, keys, values, weight_out, cotangent):
    seq_count = lax.axis_size("seq")
    half = lax.axis_index("head")
    octets = [[8 * i + j for j in range(8)] for i in range(seq_count // 8)]
    mirror = 6 * (lax.axis_index("seq") // 8 % 2)
    info = jnp.stack([half, mirror]).astype(jnp.int32)

    block = ((8, 2 * KEPT + 16, 128), BF)
    later_block = ((272, 128), BF)
    stat = ((8, ROWS), F32)
    square = ((ROWS, WIDE), F32)

    other_cot = partner(cotangent)
    q, k, v, out_t, log0, att_t, kept_out, kept_log = call(
        local_forward,
        [((ROWS, WIDE), BF)] * 3
        + [((WIDE, ROWS), F32), stat, ((WIDE, ROWS), BF), ((KEPT, WIDE), F32), ((8, KEPT), F32)],
        (queries, keys, values), flops=400000000, info=info,
        scratch=[pltpu.SemaphoreType.DMA((PAIRS, 3))], far_in=True,
    )
    grad, delta0, sent = call(
        pack_rows, [((ROWS, WIDE), BF), stat, block],
        (q, k, v, cotangent, other_cot, weight_out, out_t, log0), flops=600000000, info=info,
    )
    block1 = lax.all_to_all(sent, "seq", 0, 0, axis_index_groups=octets)
    late_w, late_att, _ = lax.optimization_barrier((weight_out, att_t, sent))
    own_w = lax.dynamic_slice_in_dim(late_w, half * WIDE, WIDE, 1)
    mix_w = partner(lax.dynamic_slice_in_dim(late_w, (1 - half) * WIDE, WIDE, 1))
    other_att_t = partner(late_att)

    sent2, stat1, out1 = call(level_one, [later_block, stat, ((64, ROWS), F32)], (block1,), flops=100000000)
    block2 = gather_pair(sent2, 14, 16)
    sent3, stat2, out2 = call(
        level_two, [later_block, stat, ((64, 128), F32)], (block2,), flops=100000000, after=(other_att_t, mix_w)
    )
    block3 = gather_pair(sent3, 64, 48)
    (base,) = call(mix_base, [square], (late_att, other_att_t, own_w, mix_w), flops=300000000)
    (returned,) = call(
        level_three, [block], (block1, block2, block3, stat1, stat2, out1, out2), flops=300000000, after=(base,)
    )
    back = lax.all_to_all(returned, "seq", 0, 0, axis_index_groups=octets)
    dq, dk, dv = call(
        local_backward, [square] * 3, (q, k, v, grad, log0, delta0), flops=1000000000, info=info,
        after=(returned,),
    )
    (own_kept,) = call(
        kept_attended, [((KEPT, WIDE), BF)], (back, kept_out, kept_log), flops=10000000, info=info, after=(dq,)
    )
    other_kept = partner(own_kept)
    query_grad, key_grad, value_grad = call(
        final_grads, [((ROWS, WIDE), BF)] * 3, (q, k, v, sent, back, dq, dk, dv), flops=200000000, info=info,
        scratch=[pltpu.VMEM((PAIRS, 3, ROWS, 128), BF), pltpu.SemaphoreType.DMA((PAIRS, 3))], far_out=True,
    )
    (nearly,) = call(mix_own, [square], (base, own_kept, own_w), flops=200000000, info=info)
    (mixed,) = call(
        mix_other, [((ROWS, WIDE), BF)], (nearly, other_kept, mix_w), flops=200000000, info=info,
        scratch=[pltpu.VMEM((PAIRS, ROWS, 128), BF), pltpu.SemaphoreType.DMA((PAIRS,))], far_out=True,
    )
    return mixed, query_grad, key_grad, value_grad


def solution(mesh):
    specs = P("seq", "head")
    return jax.shard_map(
        body,
        mesh=mesh,
        in_specs=(specs, specs, specs, P("head", None), specs),
        out_specs=(specs, specs, specs, specs),
        check_vma=False,
    )
```

time: 99.8 us -> 84.3 us (0.84)
  blocking collectives: 17 us -> 0 us
  Pallas kernels: 21.6 us -> 27.2 us
  local copies, waits for them, and re-layouts: 11.6 us -> 7.64 us
  waiting for transfers between devices: 26.9 us -> 23.8 us
  starting transfers between devices: 20.4 us -> 22.9 us
    all_to_all x1 -> x0, blocking collectives: 17 us -> none  [body(): block1 = lax.all_to_all(sent, 'seq', 0, 0, axis_index_groups=octets)]
    ppermute x4, waiting for transfers between devices: 10.8 us -> 0.01 us  [partner(): return lax.ppermute(array, 'head', [(0, 1), (1, 0)])]
    all_to_all x0 -> x1, waiting for transfers between devices: none -> 9.91 us  [body(): block1 = lax.all_to_all(sent, 'seq', 0, 0, axis_index_groups=octets)]
    pallas_call x9 -> x11, Pallas kernels: 21.6 us -> 27.2 us  [call(): pl.pallas_call(run, out_shape=shapes, in_specs=[pl.BlockSpec(memory_space...]
    all_to_all x0 -> x1, starting transfers between devices: none -> 5.53 us  [body(): block1 = lax.all_to_all(sent, 'seq', 0, 0, axis_index_groups=octets)]
    ppermute x4, waiting for transfers between devices: 15.3 us -> 12.1 us  [flip(): lax.ppermute(array, 'seq', [(i, i ^ mask) for i in range(lax.axis_size('s...]
    unnamed x46 -> x28, local copies, waits for them, and re-layouts: 9.75 us -> 7.58 us
    ppermute x4, starting transfers between devices: 11.7 us -> 9.78 us  [flip(): lax.ppermute(array, 'seq', [(i, i ^ mask) for i in range(lax.axis_size('s...]
  transfers between devices with their start and end apart: 9 -> 10, of which waited for: 8 -> 6; matrix products, arithmetic and copies ran while one was open for 2% -> 0% of each run, Pallas kernels for 13% -> 22%
where the time goes in v1:
time: 84.3 us; the launch traced here: 82.6 us
  Pallas kernels  27.2 us (32%)
  waiting for transfers between devices  23.8 us (28%)
  starting transfers between devices  22.9 us (27%)
  local copies, waits for them, and re-layouts  7.64 us (9%)
  between operations  0.98 us (1%)
    pallas_call x11, Pallas kernels, call(): pl.pallas_call(run, out_shape=shapes, in_specs=[pl.BlockSpec(memory_space...  27.2 us
    ppermute x4, waiting for transfers between devices, flip(): lax.ppermute(array, 'seq', [(i, i ^ mask) for i in range(lax.axis_size('s...  12.1 us
    all_to_all x1, waiting for transfers between devices, body(): block1 = lax.all_to_all(sent, 'seq', 0, 0, axis_index_groups=octets)  9.91 us
    ppermute x4, starting transfers between devices, flip(): lax.ppermute(array, 'seq', [(i, i ^ mask) for i in range(lax.axis_size('s...  9.78 us
    unnamed x28, local copies, waits for them, and re-layouts  7.58 us
    all_to_all x1, starting transfers between devices, body(): block1 = lax.all_to_all(sent, 'seq', 0, 0, axis_index_groups=octets)  5.53 us
    ppermute x4, starting transfers between devices, partner(): return lax.ppermute(array, 'head', [(0, 1), (1, 0)])  4.15 us
    all_to_all x1, starting transfers between devices, body(): back = lax.all_to_all(returned, 'seq', 0, 0, axis_index_groups=octets)  3.42 us
  transfers between devices with their start and end apart: 10, of which 6 were waited for; matrix products, arithmetic and copies ran while one was open for 0% of the time, Pallas kernels for 22%

profile of v1, /device:TPU:2, one launch (start us, length us, event | category | flops | bytes accessed | tf_op | source)
XLA Modules:
  0.0 82.6 jit_solution(5851921805658107104)
XLA Ops:
  0.6 2.4 %collective-permute-start = (bf16[512,384]{1,0:T(8,128)(2,1)}, bf16[512,384]{1,0:T(8,128)(2,1)S(1)}, u32[]{:S(2)}, u32[]{:S(2)}) collective-permute-start(bf16[512,384]{1,0:T(8,128)(2,1)} %refs_4_.1), channel_id=1, source_target_pairs={{0,1},{1,0},{2,3},{3,2},{4,5},{5,4},{6,7},{7,6},{8,9},{9,8},{10,11... | collective-permute-start | bytes 1179656 | tf_op jit(solution)/shard_map/ppermute | solution.py:456
  3.0 0.1 pad_add_fusion.refs_0_
  3.1 0.0 copy-start.9
  3.1 1.0 %copy-done.9 = bf16[512,384]{1,0:T(8,128)(2,1)S(1)} copy-done((bf16[512,384]{1,0:T(8,128)(2,1)S(1)}, bf16[512,384]{1,0:T(8,128)(2,1)}, u32[]{:S(2)}) %copy-start.9) | copy-done | bytes 393240
  4.1 0.0 copy-start.10
  4.1 1.0 %copy-done.10 = bf16[512,384]{1,0:T(8,128)(2,1)S(1)} copy-done((bf16[512,384]{1,0:T(8,128)(2,1)S(1)}, bf16[512,384]{1,0:T(8,128)(2,1)}, u32[]{:S(2)}) %copy-start.10) | copy-done | bytes 393240
  5.1 0.0 copy-start.11
  5.1 1.0 %copy-done.11 = bf16[512,384]{1,0:T(8,128)(2,1)S(1)} copy-done((bf16[512,384]{1,0:T(8,128)(2,1)S(1)}, bf16[512,384]{1,0:T(8,128)(2,1)}, u32[]{:S(2)}) %copy-start.11) | copy-done | bytes 393240
  6.1 0.0 copy-start
  6.1 0.0 copy-start.8
  6.1 6.0 %local_forward.1 = (bf16[512,384]{1,0:T(8,128)(2,1)S(1)}, bf16[512,384]{1,0:T(8,128)(2,1)S(1)}, bf16[512,384]{1,0:T(8,128)(2,1)S(1)}, f32[384,512]{1,0:T(8,128)S...) custom-call(s32[2]{0:T(128)S(1)} %pad_add_fusion.refs_0_, ...), custom_call_target="tpu_custom_call" | custom-call | flops 400000000 | bytes 3655680 | tf_op jit(solution)/shard_map/local_forward/pallas_call | solution.py:441
  12.1 0.0 copy-start.1
  12.1 0.0 collective-permute-done.refs_5_
  12.1 0.0 copy-done
  12.1 0.0 copy-done.8
  12.2 2.7 %pack_rows.1 = (bf16[512,384]{1,0:T(8,128)(2,1)S(1)}, f32[8,512]{1,0:T(8,128)S(1)}, bf16[8,144,128]{2,1,0:T(8,128)(2,1)}) custom-call(s32[2]{0:T(128)S(1)} %pad_add_fusion.refs_0_, bf16[512,384]{1,0:T(8,128)(2,1)S(1)} %get-tuple-element.30.refs_1_, bf16[512,384]{1,0:T(8,128)(2,1)S(1)} %get-tuple-element.31.refs_2_, ...), custom_call_target="tpu_custom_call" | custom-call | flops 600000000 | bytes 4063232 | tf_op jit(solution)/shard_map/pack_rows/pallas_call | solution.py:441
  14.9 0.0 copy-done.1
  14.9 0.0 copy-start.12
  14.9 0.7 copy-done.12
  15.6 5.5 %all-to-all-start = ((bf16[8,144,128]{2,1,0:T(8,128)(2,1)}), bf16[8,144,128]{2,1,0:T(8,128)(2,1)S(1)}, u32[]{:S(2)}, u32[]{:S(2)}) async-start(bf16[8,144,128]{2,1,0:T(8,128)(2,1)} %get-tuple-element.35.refs_4_), calls=%async_computation | async-start | bytes 589824 | tf_op jit(solution)/shard_map/all_to_all | solution.py:492
  21.2 0.5 collective-permute-start.1
  21.7 9.9 %all-to-all-done.refs_0_ = bf16[8,144,128]{2,1,0:T(8,128)(2,1)S(1)} async-done(((bf16[8,144,128]{2,1,0:T(8,128)(2,1)}), bf16[8,144,128]{2,1,0:T(8,128)(2,1)S(1)}, u32[]{:S(2)}, u32[]{:S(2)}) %all-to-all-start) | async-done | bytes 294944 | tf_op jit(solution)/shard_map/all_to_all | solution.py:492
  31.6 0.8 level_one.1
  32.4 2.6 %collective-permute-start.3 = (bf16[272,128]{1,0:T(8,128)(2,1)S(1)}, bf16[272,128]{1,0:T(8,128)(2,1)S(1)}, u32[]{:S(2)}, u32[]{:S(2)}) collective-permute-start(bf16[272,128]{1,0:T(8,128)(2,1)S(1)} %get-tuple-element.38), channel_id=1, source_target_pairs={{0,28},{2,30},{4,24},{6,26},{8,20},{10,22},{12,16},{14,18},{16,12}... | collective-permute-start | bytes 208904 | tf_op jit(solution)/shard_map/ppermute | solution.py:460
  35.1 0.1 constant_dynamic-slice_fusion
  35.1 0.6 collective-permute-start.2
  35.8 3.2 %collective-permute-done.3 = bf16[272,128]{1,0:T(8,128)(2,1)S(1)} collective-permute-done((bf16[272,128]{1,0:T(8,128)(2,1)S(1)}, bf16[272,128]{1,0:T(8,128)(2,1)S(1)}, u32[]{:S(2)}, u32[]{:S(2)}) %collective-permute-start.3) | collective-permute-done | bytes 69664 | tf_op jit(solution)/shard_map/ppermute | solution.py:460
  39.0 1.7 %collective-permute-start.4 = (bf16[2,272,128]{2,1,0:T(8,128)(2,1)S(1)}, bf16[2,272,128]{2,1,0:T(8,128)(2,1)S(1)}, u32[]{:S(2)}, u32[]{:S(2)}) collective-permute-start(bf16[2,272,128]{2,1,0:T(8,128)(2,1)S(1)} %pad_maximum_fusion.2), channel_id=1, source_target_pairs={{0,32},{2,34},{4,36},{6,38},{8,40},{10,42},{12,44},{14,46},{16,48}... | collective-permute-start | bytes 417800 | tf_op jit(solution)/shard_map/ppermute | solution.py:460
  40.7 3.6 %collective-permute-done.4 = bf16[2,272,128]{2,1,0:T(8,128)(2,1)S(1)} collective-permute-done((bf16[2,272,128]{2,1,0:T(8,128)(2,1)S(1)}, bf16[2,272,128]{2,1,0:T(8,128)(2,1)S(1)}, u32[]{:S(2)}, u32[]{:S(2)}) %collective-permute-start.4) | collective-permute-done | bytes 139296 | tf_op jit(solution)/shard_map/ppermute | solution.py:460
  44.3 0.0 collective-permute-done.2.refs_3_.refs_2_
  44.3 0.0 collective-permute-done.1.refs_1_
  44.3 0.9 %level_two.1 = (bf16[272,128]{1,0:T(8,128)(2,1)S(1)}, f32[8,512]{1,0:T(8,128)S(1)}, f32[64,128]{1,0:T(8,128)S(1)}) custom-call(bf16[4,272,128]{2,1,0:T(8,128)(2,1)S(1)} %pad_maximum_fusion.refs_0_.refs_1_, bf16[384,512]{1,0:T(8,128)(2,1)S(1)} %collective-permute-done.1.refs_1_, bf16[384,384]{1,0:T(8,128)(2,1)S(1)} %collective-permute-done.2.refs_3_.refs_2_), custom_call_target="tpu_custom_call" | custom-call | flops 100000000 | bytes 397312 | tf_op jit(solution)/shard_map/level_two/pallas_call | solution.py:441
  45.2 2.2 %collective-permute-start.5 = (bf16[272,128]{1,0:T(8,128)(2,1)S(1)}, bf16[272,128]{1,0:T(8,128)(2,1)S(1)}, u32[]{:S(2)}, u32[]{:S(2)}) collective-permute-start(bf16[272,128]{1,0:T(8,128)(2,1)S(1)} %get-tuple-element.39), channel_id=1, source_target_pairs={{0,128},{2,130},{4,132},{6,134},{8,136},{10,138},{12,140},{14,142}... | collective-permute-start | bytes 208904 | tf_op jit(solution)/shard_map/ppermute | solution.py:460
  47.4 3.7 %collective-permute-done.5 = bf16[272,128]{1,0:T(8,128)(2,1)S(1)} collective-permute-done((bf16[272,128]{1,0:T(8,128)(2,1)S(1)}, bf16[272,128]{1,0:T(8,128)(2,1)S(1)}, u32[]{:S(2)}, u32[]{:S(2)}) %collective-permute-start.5) | collective-permute-done | bytes 69664 | tf_op jit(solution)/shard_map/ppermute | solution.py:460
  51.1 3.3 %collective-permute-start.6 = (bf16[2,272,128]{2,1,0:T(8,128)(2,1)S(1)}, bf16[2,272,128]{2,1,0:T(8,128)(2,1)S(1)}, u32[]{:S(2)}, u32[]{:S(2)}) collective-permute-start(bf16[2,272,128]{2,1,0:T(8,128)(2,1)S(1)} %pad_maximum_fusion.3), channel_id=1, source_target_pairs={{0,96},{2,98},{4,100},{6,102},{8,104},{10,106},{12,108},{14,110},{... | collective-permute-start | bytes 417800 | tf_op jit(solution)/shard_map/ppermute | solution.py:460
  54.4 1.7 %mix_base.1.refs_7_.refs_1_ = f32[512,384]{1,0:T(8,128)S(1)} custom-call(bf16[384,512]{1,0:T(8,128)(2,1)} %get-tuple-element.36.refs_0_, bf16[384,512]{1,0:T(8,128)(2,1)S(1)} %collective-permute-done.1.refs_1_, bf16[384,384]{1,0:T(8,128)(2,1)S(1)} %get-tuple-element.55.refs_2_.refs_3_, bf16[384,384]{1,0:T(8,128)(2,1)S(1)} %collective-permute-done.2.refs_3_.refs_2_), custom_call_target="tpu_custom_call" | custom-call | flops 300000000 | bytes 2162688 | tf_op jit(solution)/shard_map/mix_base/pallas_call | solution.py:441
  56.0 1.6 %collective-permute-done.6 = bf16[2,272,128]{2,1,0:T(8,128)(2,1)S(1)} collective-permute-done((bf16[2,272,128]{2,1,0:T(8,128)(2,1)S(1)}, bf16[2,272,128]{2,1,0:T(8,128)(2,1)S(1)}, u32[]{:S(2)}, u32[]{:S(2)}) %collective-permute-start.6) | collective-permute-done | bytes 139296 | tf_op jit(solution)/shard_map/ppermute | solution.py:460
  57.7 2.9 %level_three.1.refs_7_ = bf16[8,144,128]{2,1,0:T(8,128)(2,1)} custom-call(bf16[8,144,128]{2,1,0:T(8,128)(2,1)S(1)} %all-to-all-done.refs_0_, bf16[4,272,128]{2,1,0:T(8,128)(2,1)S(1)} %pad_maximum_fusion.refs_0_.refs_1_, bf16[4,272,128]{2,1,0:T(8,128)(2,1)S(1)} %pad_maximum_fusion.1.refs_2_, f32[8,512]{1,0:T(8,128)S(1)} %get-tuple-element.40.refs_3_, ...), custom_call_target="tpu_custom_call" | custom-call | flops 300000000 | bytes 1343488 | tf_op jit(solution)/shard_map/level_three/pallas_call | solution.py:441
  60.6 3.4 %all-to-all-start.1 = ((bf16[8,144,128]{2,1,0:T(8,128)(2,1)}), bf16[8,144,128]{2,1,0:T(8,128)(2,1)S(1)}, u32[]{:S(2)}, u32[]{:S(2)}) async-start(bf16[8,144,128]{2,1,0:T(8,128)(2,1)} %level_three.1.refs_7_), calls=%async_computation.1 | async-start | bytes 589824 | tf_op jit(solution)/shard_map/all_to_all | solution.py:508
  64.0 0.0 copy-start.2
  64.0 1.0 %copy-done.2 = bf16[512,384]{1,0:T(8,128)(2,1)S(1)} copy-done((bf16[512,384]{1,0:T(8,128)(2,1)S(1)}, bf16[512,384]{1,0:T(8,128)(2,1)}, u32[]{:S(2)}) %copy-start.2) | copy-done | bytes 393240
  65.0 0.0 copy-start.13
  65.0 1.0 %copy-done.13 = bf16[512,384]{1,0:T(8,128)(2,1)S(1)} copy-done((bf16[512,384]{1,0:T(8,128)(2,1)S(1)}, bf16[512,384]{1,0:T(8,128)(2,1)}, u32[]{:S(2)}) %copy-start.13) | copy-done | bytes 393240
  66.0 4.7 %local_backward.1 = (f32[512,384]{1,0:T(8,128)S(1)}, f32[512,384]{1,0:T(8,128)S(1)}, f32[512,384]{1,0:T(8,128)S(1)}) custom-call(s32[2]{0:T(128)S(1)} %pad_add_fusion.refs_0_, bf16[512,384]{1,0:T(8,128)(2,1)S(1)} %get-tuple-element.30.refs_1_, bf16[512,384]{1,0:T(8,128)(2,1)S(1)} %get-tuple-element.31.refs_2_, bf16[512,384]{1,0:T(8,128)(2,1)S(1)} %copy-done.2, ...), custom_call_target="tpu_custom_call" | custom-call | flops 1000000000 | bytes 3964928 | tf_op jit(solution)/shard_map/local_backward/pallas_call | solution.py:441
  70.7 0.0 copy-start.4
  70.7 0.9 %copy-done.4 = f32[512,384]{1,0:T(8,128)} copy-done((f32[512,384]{1,0:T(8,128)}, f32[512,384]{1,0:T(8,128)S(1)}, u32[]{:S(2)}) %copy-start.4) | copy-done | bytes 786456
  71.6 0.0 copy-start.6
  71.6 0.9 %copy-done.6 = f32[512,384]{1,0:T(8,128)} copy-done((f32[512,384]{1,0:T(8,128)}, f32[512,384]{1,0:T(8,128)S(1)}, u32[]{:S(2)}) %copy-start.6) | copy-done | bytes 786456
  72.6 1.8 %all-to-all-done.1.refs_1_.refs_5_ = bf16[8,144,128]{2,1,0:T(8,128)(2,1)S(1)} async-done(((bf16[8,144,128]{2,1,0:T(8,128)(2,1)}), bf16[8,144,128]{2,1,0:T(8,128)(2,1)S(1)}, u32[]{:S(2)}, u32[]{:S(2)}) %all-to-all-start.1) | async-done | bytes 294944 | tf_op jit(solution)/shard_map/all_to_all | solution.py:508
  74.3 0.0 copy-start.7
  74.3 0.7 kept_attended.1.refs_2_
  75.1 0.0 copy-start.3
  75.1 0.0 copy-start.5
  75.1 0.6 collective-permute-start.7
  75.7 1.1 %mix_own.1.refs_1_ = f32[512,384]{1,0:T(8,128)S(1)} custom-call(s32[2]{0:T(128)S(1)} %pad_add_fusion.refs_0_, f32[512,384]{1,0:T(8,128)S(1)} %mix_base.1.refs_7_.refs_1_, bf16[64,384]{1,0:T(8,128)(2,1)S(1)} %kept_attended.1.refs_2_, bf16[384,384]{1,0:T(8,128)(2,1)S(1)} %get-tuple-element.55.refs_2_.refs_3_), custom_call_target="tpu_custom_call" | custom-call | flops 200000000 | bytes 1916928 | tf_op jit(solution)/shard_map/mix_own/pallas_call | solution.py:441
  76.9 0.0 copy-done.7
  76.9 0.0 copy-done.3
  76.9 0.0 copy-done.5
  76.9 3.6 %final_grads.1 = (bf16[512,384]{1,0:T(8,128)(2,1)}, bf16[512,384]{1,0:T(8,128)(2,1)}, bf16[512,384]{1,0:T(8,128)(2,1)}) custom-call(s32[2]{0:T(128)S(1)} %pad_add_fusion.refs_0_, bf16[512,384]{1,0:T(8,128)(2,1)S(1)} %get-tuple-element.30.refs_1_, bf16[512,384]{1,0:T(8,128)(2,1)S(1)} %get-tuple-element.31.refs_2_, bf16[512,384]{1,0:T(8,128)(2,1)S(1)} %copy-done.3, ...), custom_call_target="tpu_custom_call" | custom-call | flops 200000000 | bytes 5308416 | tf_op jit(solution)/shard_map/final_grads/pallas_call | solution.py:441
  80.6 0.0 collective-permute-done.7.refs_2_
  80.6 1.9 %mix_other.1 = bf16[512,384]{1,0:T(8,128)(2,1)} custom-call(s32[2]{0:T(128)S(1)} %pad_add_fusion.refs_0_, f32[512,384]{1,0:T(8,128)S(1)} %mix_own.1.refs_1_, bf16[64,384]{1,0:T(8,128)(2,1)S(1)} %collective-permute-done.7.refs_2_, bf16[384,384]{1,0:T(8,128)(2,1)S(1)} %collective-permute-done.2.refs_3_.refs_2_), custom_call_target="tpu_custom_call" | custom-call | flops 200000000 | bytes 1523712 | tf_op jit(solution)/shard_map/mix_other/pallas_call | solution.py:441
  (4 shorter events, 0.1 us)
Async XLA Ops:
  0.6 11.5 %collective-permute-start = (bf16[512,384]{1,0:T(8,128)(2,1)}, bf16[512,384]{1,0:T(8,128)(2,1)S(1)}, u32[]{:S(2)}, u32[]{:S(2)}) collective-permute-start(bf16[512,384]{1,0:T(8,128)(2,1)} %refs_4_.1), channel_id=1, source_target_pairs={{0,1},{1,0},{2,3},{3,2},{4,5},{5,4},{6,7},{7,6},{8,9},{9,8},{10,11... | collective-permute-start | bytes 1179656 | tf_op jit(solution)/shard_map/ppermute | solution.py:456
  3.1 1.0 %copy-start.9 = (bf16[512,384]{1,0:T(8,128)(2,1)S(1)}, bf16[512,384]{1,0:T(8,128)(2,1)}, u32[]{:S(2)}) copy-start(bf16[512,384]{1,0:T(8,128)(2,1)} %refs_1_.1) | copy-start | bytes 1179652
  4.1 1.0 %copy-start.10 = (bf16[512,384]{1,0:T(8,128)(2,1)S(1)}, bf16[512,384]{1,0:T(8,128)(2,1)}, u32[]{:S(2)}) copy-start(bf16[512,384]{1,0:T(8,128)(2,1)} %refs_2_.1) | copy-start | bytes 1179652
  5.1 1.0 %copy-start.11 = (bf16[512,384]{1,0:T(8,128)(2,1)S(1)}, bf16[512,384]{1,0:T(8,128)(2,1)}, u32[]{:S(2)}) copy-start(bf16[512,384]{1,0:T(8,128)(2,1)} %refs_3_.1) | copy-start | bytes 1179652
  6.1 6.1 %copy-start = (bf16[384,768]{1,0:T(8,128)(2,1)S(1)}, bf16[384,768]{1,0:T(8,128)(2,1)}, u32[]{:S(2)}) copy-start(bf16[384,768]{1,0:T(8,128)(2,1)} %refs_6_.1) | copy-start | bytes 1769476
  6.1 6.1 %copy-start.8 = (bf16[512,384]{1,0:T(8,128)(2,1)S(1)}, bf16[512,384]{1,0:T(8,128)(2,1)}, u32[]{:S(2)}) copy-start(bf16[512,384]{1,0:T(8,128)(2,1)} %refs_4_.1) | copy-start | bytes 1179652
  12.1 2.8 %copy-start.1 = (bf16[512,384]{1,0:T(8,128)(2,1)}, bf16[512,384]{1,0:T(8,128)(2,1)S(1)}, u32[]{:S(2)}) copy-start(bf16[512,384]{1,0:T(8,128)(2,1)S(1)} %get-tuple-element.32.refs_3_) | copy-start | bytes 1179652
  14.9 0.7 copy-start.12
  15.6 16.0 %all-to-all-start = ((bf16[8,144,128]{2,1,0:T(8,128)(2,1)}), bf16[8,144,128]{2,1,0:T(8,128)(2,1)S(1)}, u32[]{:S(2)}, u32[]{:S(2)}) async-start(bf16[8,144,128]{2,1,0:T(8,128)(2,1)} %get-tuple-element.35.refs_4_), calls=%async_computation | async-start | bytes 589824 | tf_op jit(solution)/shard_map/all_to_all | solution.py:492
  21.2 23.1 %collective-permute-start.1 = (bf16[384,512]{1,0:T(8,128)(2,1)}, bf16[384,512]{1,0:T(8,128)(2,1)S(1)}, u32[]{:S(2)}, u32[]{:S(2)}) collective-permute-start(bf16[384,512]{1,0:T(8,128)(2,1)} %get-tuple-element.36.refs_0_), channel_id=1, source_target_pairs={{0,1},{1,0},{2,3},{3,2},{4,5},{5,4},{6,7},{7,6},{8,9},{9,8},{10,11... | collective-permute-start | bytes 1179656 | tf_op jit(solution)/shard_map/ppermute | solution.py:456
  32.4 6.5 %collective-permute-start.3 = (bf16[272,128]{1,0:T(8,128)(2,1)S(1)}, bf16[272,128]{1,0:T(8,128)(2,1)S(1)}, u32[]{:S(2)}, u32[]{:S(2)}) collective-permute-start(bf16[272,128]{1,0:T(8,128)(2,1)S(1)} %get-tuple-element.38), channel_id=1, source_target_pairs={{0,28},{2,30},{4,24},{6,26},{8,20},{10,22},{12,16},{14,18},{16,12}... | collective-permute-start | bytes 208904 | tf_op jit(solution)/shard_map/ppermute | solution.py:460
  35.1 9.2 %collective-permute-start.2 = (bf16[384,384]{1,0:T(8,128)(2,1)S(1)}, bf16[384,384]{1,0:T(8,128)(2,1)S(1)}, u32[]{:S(2)}, u32[]{:S(2)}) collective-permute-start(bf16[384,384]{1,0:T(8,128)(2,1)S(1)} %get-tuple-element.54), channel_id=1, source_target_pairs={{0,1},{1,0},{2,3},{3,2},{4,5},{5,4},{6,7},{7,6},{8,9},{9,8},{10,11... | collective-permute-start | bytes 884744 | tf_op jit(solution)/shard_map/ppermute | solution.py:456
  39.0 5.3 %collective-permute-start.4 = (bf16[2,272,128]{2,1,0:T(8,128)(2,1)S(1)}, bf16[2,272,128]{2,1,0:T(8,128)(2,1)S(1)}, u32[]{:S(2)}, u32[]{:S(2)}) collective-permute-start(bf16[2,272,128]{2,1,0:T(8,128)(2,1)S(1)} %pad_maximum_fusion.2), channel_id=1, source_target_pairs={{0,32},{2,34},{4,36},{6,38},{8,40},{10,42},{12,44},{14,46},{16,48}... | collective-permute-start | bytes 417800 | tf_op jit(solution)/shard_map/ppermute | solution.py:460
  45.2 5.9 %collective-permute-start.5 = (bf16[272,128]{1,0:T(8,128)(2,1)S(1)}, bf16[272,128]{1,0:T(8,128)(2,1)S(1)}, u32[]{:S(2)}, u32[]{:S(2)}) collective-permute-start(bf16[272,128]{1,0:T(8,128)(2,1)S(1)} %get-tuple-element.39), channel_id=1, source_target_pairs={{0,128},{2,130},{4,132},{6,134},{8,136},{10,138},{12,140},{14,142}... | collective-permute-start | bytes 208904 | tf_op jit(solution)/shard_map/ppermute | solution.py:460
  51.1 6.5 %collective-permute-start.6 = (bf16[2,272,128]{2,1,0:T(8,128)(2,1)S(1)}, bf16[2,272,128]{2,1,0:T(8,128)(2,1)S(1)}, u32[]{:S(2)}, u32[]{:S(2)}) collective-permute-start(bf16[2,272,128]{2,1,0:T(8,128)(2,1)S(1)} %pad_maximum_fusion.3), channel_id=1, source_target_pairs={{0,96},{2,98},{4,100},{6,102},{8,104},{10,106},{12,108},{14,110},{... | collective-permute-start | bytes 417800 | tf_op jit(solution)/shard_map/ppermute | solution.py:460
  60.6 13.8 %all-to-all-start.1 = ((bf16[8,144,128]{2,1,0:T(8,128)(2,1)}), bf16[8,144,128]{2,1,0:T(8,128)(2,1)S(1)}, u32[]{:S(2)}, u32[]{:S(2)}) async-start(bf16[8,144,128]{2,1,0:T(8,128)(2,1)} %level_three.1.refs_7_), calls=%async_computation.1 | async-start | bytes 589824 | tf_op jit(solution)/shard_map/all_to_all | solution.py:508
  64.0 1.0 %copy-start.2 = (bf16[512,384]{1,0:T(8,128)(2,1)S(1)}, bf16[512,384]{1,0:T(8,128)(2,1)}, u32[]{:S(2)}) copy-start(bf16[512,384]{1,0:T(8,128)(2,1)} %copy-done.1) | copy-start | bytes 1179652
  65.0 1.0 %copy-start.13 = (bf16[512,384]{1,0:T(8,128)(2,1)S(1)}, bf16[512,384]{1,0:T(8,128)(2,1)}, u32[]{:S(2)}) copy-start(bf16[512,384]{1,0:T(8,128)(2,1)} %copy-done.12) | copy-start | bytes 1179652
  70.7 0.9 %copy-start.4 = (f32[512,384]{1,0:T(8,128)}, f32[512,384]{1,0:T(8,128)S(1)}, u32[]{:S(2)}) copy-start(f32[512,384]{1,0:T(8,128)S(1)} %get-tuple-element.49.refs_7_) | copy-start | bytes 2359300
  71.6 0.9 %copy-start.6 = (f32[512,384]{1,0:T(8,128)}, f32[512,384]{1,0:T(8,128)S(1)}, u32[]{:S(2)}) copy-start(f32[512,384]{1,0:T(8,128)S(1)} %get-tuple-element.50.refs_8_) | copy-start | bytes 2359300
  74.3 2.6 %copy-start.7 = (f32[512,384]{1,0:T(8,128)S(1)}, f32[512,384]{1,0:T(8,128)}, u32[]{:S(2)}) copy-start(f32[512,384]{1,0:T(8,128)} %copy-done.6) | copy-start | bytes 2359300
  75.1 1.8 %copy-start.3 = (bf16[512,384]{1,0:T(8,128)(2,1)S(1)}, bf16[512,384]{1,0:T(8,128)(2,1)}, u32[]{:S(2)}) copy-start(bf16[512,384]{1,0:T(8,128)(2,1)} %copy-done.1) | copy-start | bytes 1179652
  75.1 1.8 %copy-start.5 = (f32[512,384]{1,0:T(8,128)S(1)}, f32[512,384]{1,0:T(8,128)}, u32[]{:S(2)}) copy-start(f32[512,384]{1,0:T(8,128)} %copy-done.4) | copy-start | bytes 2359300
  75.1 5.4 %collective-permute-start.7 = (bf16[64,384]{1,0:T(8,128)(2,1)S(1)}, bf16[64,384]{1,0:T(8,128)(2,1)S(1)}, u32[]{:S(2)}, u32[]{:S(2)}) collective-permute-start(bf16[64,384]{1,0:T(8,128)(2,1)S(1)} %kept_attended.1.refs_2_), channel_id=1, source_target_pairs={{0,1},{1,0},{2,3},{3,2},{4,5},{5,4},{6,7},{7,6},{8,9},{9,8},{10,11... | collective-permute-start | bytes 147464 | tf_op jit(solution)/shard_map/ppermute | solution.py:456

commit v2 on v1

v2 whole, which is shorter than its diff:
```python
import functools

import jax
import jax.numpy as jnp
import numpy as np
from jax import lax
from jax.experimental import pallas as pl
from jax.experimental.pallas import tpu as pltpu
from jax.sharding import PartitionSpec as P

HEAD_DIM = 64
LOCAL_HEADS = 6
PAIRS = LOCAL_HEADS // 2
ROWS = 512
KEPT = 64
WIDE = 384
SCALE = HEAD_DIM ** -0.5
BF = jnp.bfloat16
F32 = jnp.float32
MASKED = 1e30
VMEM_LIMIT = 24 * 1024 * 1024


def iota(shape, axis):
    return lax.broadcasted_iota(jnp.int32, shape, axis)


def kept_row(place, head):
    phase = lax.shift_right_logical(head, 3)
    third = 16 * place + phase
    later = place - 4
    second = 4 * (later + lax.shift_right_arithmetic(later * 11, 5) + 1) + phase
    last = place - 16
    group = lax.shift_right_arithmetic(last * 171, 9)
    spot = last - 3 * group
    first = 4 * group + spot + jnp.where(spot >= phase, 1, 0)
    chosen = jnp.where(place < 4, third, jnp.where(place < 16, second, first))
    return 8 * chosen + jnp.bitwise_and(head, 7)


def one_hot(match):
    return jnp.where(match, 1.0, 0.0).astype(BF)


def flat_pick(head):
    return one_hot(iota((KEPT, ROWS), 1) == kept_row(iota((KEPT, 1), 0), head))


def tall_pick(head):
    return one_hot(iota((ROWS, KEPT), 0) == kept_row(iota((1, KEPT), 1), head))


def subset_pick(wide, narrow):
    place = iota((128, 1), 0)
    group = lax.shift_right_logical(place, narrow)
    target = lax.shift_left(group, wide) + jnp.bitwise_and(place, (1 << narrow) - 1)
    return one_hot(iota((128, ROWS), 1) == target)


def dot_nn(left, right):
    return lax.dot_general(left, right, (((1,), (0,)), ((), ())), preferred_element_type=F32)


def dot_nt(left, right):
    return lax.dot_general(left, right, (((1,), (1,)), ((), ())), preferred_element_type=F32)


def dot_tn(left, right):
    return lax.dot_general(left, right, (((0,), (0,)), ((), ())), preferred_element_type=F32)


def split2(value):
    high = value.astype(BF)
    return high, (value - high.astype(F32)).astype(BF)


def split3(value):
    high = value.astype(BF)
    rest = value - high.astype(F32)
    middle = rest.astype(BF)
    return high, middle, (rest - middle.astype(F32)).astype(BF)


def stat_block(log_row, delta_row):
    pieces = split3(log_row) + split3(delta_row)
    rows = [piece.astype(F32) for piece in pieces]
    zero = jnp.zeros_like(log_row)
    return jnp.concatenate(rows + [zero, zero], axis=0)


def stat_rows(block):
    block = block.astype(F32)
    log_row = block[0:1] + block[1:2] + block[2:3]
    delta_row = block[3:4] + block[4:5] + block[5:6]
    return log_row, delta_row


def log_add(first, second):
    peak = jnp.maximum(first, second)
    return peak + jnp.log(jnp.exp(first - peak) + jnp.exp(second - peak))


def span(local):
    return slice(local * HEAD_DIM, (local + 1) * HEAD_DIM)


def cols(pair):
    return slice(pair * 128, (pair + 1) * 128)


OWNERS = (0, 2, 4, 3, 5, 7)
IDLE = (1, 6)


def slot_of(info_ref, place):
    return jnp.bitwise_xor(info_ref[1], place)


def slot_of_head(info_ref, local):
    return slot_of(info_ref, OWNERS[local])


def head_of(half, local):
    return half * LOCAL_HEADS + local


def diagonal(first, second):
    zero = jnp.zeros_like(first)
    return jnp.concatenate(
        [jnp.concatenate([first, zero], axis=1), jnp.concatenate([zero, second], axis=1)], axis=0
    )


def pack_data(info_ref, qkv_ref, packed_ref, hots_ref):
    for local in range(LOCAL_HEADS):
        hot = flat_pick(head_of(info_ref[0], local))
        hots_ref[span(local), :] = hot
        joined = jnp.concatenate([qkv_ref[part, :, span(local)] for part in range(3)], axis=1)
        rows = dot_nn(hot, joined).astype(BF)
        packed_ref[local, :KEPT, :] = jnp.concatenate([rows[:, :64] * BF(SCALE), rows[:, 64:128]], axis=1)
        packed_ref[local, KEPT:, :] = jnp.concatenate([rows[:, 128:], jnp.zeros((KEPT, 64), BF)], axis=1)


def kept_forward(qkv_ref, packed_ref, out_ref, log_ref):
    log_ref[LOCAL_HEADS:, :] = jnp.zeros((8 - LOCAL_HEADS, KEPT), F32)
    for pair in range(PAIRS):
        query = diagonal(packed_ref[2 * pair, :KEPT, :64], packed_ref[2 * pair + 1, :KEPT, :64])
        scores = dot_nt(qkv_ref[1, :, cols(pair)], query)
        peak = jnp.max(scores, axis=0, keepdims=True)
        powers = jnp.exp(scores - peak)
        total = jnp.sum(powers, axis=0, keepdims=True)
        crossed = (dot_tn(qkv_ref[2, :, cols(pair)], powers.astype(BF)) / total).T
        out_ref[:, cols(pair)] = jnp.concatenate([crossed[:64, :64], crossed[64:, 64:]], axis=1)
        log_row = peak + jnp.log(total)
        log_ref[2 * pair:2 * pair + 1, :] = log_row[:, :64]
        log_ref[2 * pair + 1:2 * pair + 2, :] = log_row[:, 64:]


def pack_grads(info_ref, packed_ref, own_cot_ref, other_cot_ref, w_ref, hots_ref, kept_out_ref,
               kept_log_ref, grad_ref, kept_grad_ref, near_ref, far_ref, slots):
    own_w = w_ref[:, pl.ds(pl.multiple_of(info_ref[0] * WIDE, 128), WIDE)]
    other_w = w_ref[:, pl.ds(pl.multiple_of((1 - info_ref[0]) * WIDE, 128), WIDE)]
    grad = (dot_nt(own_cot_ref[...], own_w) + dot_nt(other_cot_ref[...], other_w)).astype(BF)
    grad_ref[...] = grad
    for local in range(LOCAL_HEADS):
        rows = dot_nn(hots_ref[span(local), :], grad[:, span(local)])
        kept_grad = rows.astype(BF)
        kept_grad_ref[:, span(local)] = kept_grad
        delta = jnp.sum((rows * kept_out_ref[:, span(local)]).T, axis=0, keepdims=True)
        slot = slot_of_head(info_ref, local)
        slots[slot, :KEPT, :] = packed_ref[local, :KEPT, :]
        slots[slot, KEPT:2 * KEPT, :] = jnp.concatenate([packed_ref[local, KEPT:, :64], kept_grad], axis=1)
        slots[slot, 2 * KEPT:, :] = widen_stats(stat_block(kept_log_ref[local:local + 1, :], delta))
    for spare in IDLE:
        slots[slot_of(info_ref, spare)] = jnp.zeros((2 * KEPT + 16, 128), BF)
    for chip in range(4):
        near_ref[chip] = slots[2 * chip]
        far_ref[chip] = slots[2 * chip + 1]


def local_forward(info_ref, qkv_ref, out_t_ref, log_ref, att_t_ref):
    log_ref[LOCAL_HEADS:, :] = jnp.zeros((8 - LOCAL_HEADS, ROWS), F32)
    for local in range(LOCAL_HEADS):
        scores = dot_nt(qkv_ref[1, :, span(local)], qkv_ref[0, :, span(local)] * BF(SCALE))
        peak = jnp.max(scores, axis=0, keepdims=True)
        powers = jnp.exp(scores - peak)
        total = jnp.sum(powers, axis=0, keepdims=True)
        out_t = dot_tn(qkv_ref[2, :, span(local)], powers.astype(BF)) / total
        log_row = peak + jnp.log(total)
        out_t_ref[span(local), :] = out_t
        log_ref[local:local + 1, :] = log_row
        head = head_of(info_ref[0], local)
        is_kept = jnp.bitwise_and(iota((1, ROWS), 1), 7) == jnp.bitwise_and(head, 7)
        att_t_ref[span(local), :] = jnp.where(is_kept, 0.0, out_t).astype(BF)


def widen_stats(block):
    if block.shape[1] < 128:
        block = jnp.concatenate([block, jnp.zeros((8, 128 - block.shape[1]), F32)], axis=1)
    return jnp.concatenate([block, jnp.zeros((8, 128), F32)], axis=0).astype(BF)


def local_backward(pair, info_ref, qkv_ref, grad_ref, log_ref, out_t_ref, dq_ref, dk_ref, dv_ref):
    dq_t, dk, dv = [], [], []
    for local in (2 * pair, 2 * pair + 1):
        query = qkv_ref[0, :, span(local)] * BF(SCALE)
        key = qkv_ref[1, :, span(local)]
        grad = grad_ref[:, span(local)]
        head = head_of(info_ref[0], local)
        is_kept = jnp.bitwise_and(iota((1, ROWS), 1), 7) == jnp.bitwise_and(head, 7)
        log_row = jnp.where(is_kept, MASKED, log_ref[local:local + 1, :])
        probability = jnp.exp(dot_nt(key, query) - log_row)
        delta = jnp.sum(grad.astype(F32).T * out_t_ref[span(local), :], axis=0, keepdims=True)
        score_grad = probability * (dot_nt(qkv_ref[2, :, span(local)], grad) - delta)
        score_grad = score_grad.astype(BF)
        dv.append(dot_nn(probability.astype(BF), grad))
        dk.append(dot_nn(score_grad, query))
        dq_t.append(dot_tn(key, score_grad))
    dq_ref[...] = jnp.concatenate(dq_t, axis=0).T * SCALE
    dk_ref[...] = jnp.concatenate(dk, axis=1)
    dv_ref[...] = jnp.concatenate(dv, axis=1)


def set_stats(query, key, value, grad):
    scores = dot_nt(key, query)
    peak = jnp.max(scores, axis=0, keepdims=True)
    powers = jnp.exp(scores - peak)
    total = jnp.sum(powers, axis=0, keepdims=True)
    prob_grad = dot_nt(value, grad)
    delta = jnp.sum(powers * prob_grad, axis=0, keepdims=True) / total
    return scores, prob_grad, powers, total, peak + jnp.log(total), delta


def merge(old_log, old_delta, new_log, new_delta):
    joint = log_add(old_log, new_log)
    return joint, jnp.exp(old_log - joint) * old_delta + jnp.exp(new_log - joint) * new_delta


def first_set(block_ref):
    joined = block_ref[:, :KEPT, :].reshape(ROWS, 128)
    other = block_ref[:, KEPT:2 * KEPT, :].reshape(ROWS, 128)
    return joined[:, :64], joined[:, 64:], other[:, :64], other[:, 64:]


def later_set(block_ref):
    joined = block_ref[:, :128, :].reshape(ROWS, 128)
    other = block_ref[:, 128:256, :].reshape(ROWS, 128)
    return joined[:, :64], joined[:, 64:], other[:, :64], other[:, 64:]


def later_stats(block_ref):
    return stat_rows(jnp.concatenate([block_ref[i, 256:264, :].astype(F32) for i in range(4)], axis=1))


def level_one(block_ref, payload_ref, stat_ref, out_t_ref):
    query, key, value, grad = first_set(block_ref)
    stats = jnp.concatenate([block_ref[i, 128:136, :KEPT].astype(F32) for i in range(8)], axis=1)
    old_log, old_delta = stat_rows(stats)
    _, _, powers, total, new_log, new_delta = set_stats(query, key, value, grad)
    joint, delta = merge(old_log, old_delta, new_log, new_delta)
    out_t_ref[...] = dot_tn(value, powers.astype(BF)) * (jnp.exp(new_log - joint) / total)
    stat_ref[0:1, :] = joint
    stat_ref[1:2, :] = delta
    stat_ref[2:, :] = jnp.zeros((6, ROWS), F32)
    payload_ref[:128, :] = block_ref[:, :16, :].reshape(128, 128)
    payload_ref[128:256, :] = block_ref[:, KEPT:KEPT + 16, :].reshape(128, 128)
    picked = dot_nt(stat_block(joint, delta).astype(BF), subset_pick(6, 4))
    payload_ref[256:, :] = widen_stats(picked)


def level_two(block_ref, payload_ref, stat_ref, out_t_ref):
    pick = subset_pick(4, 2)
    query, key, value, grad = later_set(block_ref)
    old_log, old_delta = later_stats(block_ref)
    _, _, powers, total, new_log, new_delta = set_stats(query, key, value, grad)
    joint, delta = merge(old_log, old_delta, new_log, new_delta)
    weight = (jnp.exp(new_log - joint) / total)[:, :128]
    out_t_ref[...] = dot_tn(value, powers[:, :128].astype(BF)) * weight
    stat_ref[0:1, :] = joint
    stat_ref[1:2, :] = delta
    stat_ref[2:, :] = jnp.zeros((6, ROWS), F32)
    payload_ref[:128, :] = dot_nn(pick, block_ref[:, :128, :].reshape(ROWS, 128)).astype(BF)
    payload_ref[128:256, :] = dot_nn(pick, block_ref[:, 128:256, :].reshape(ROWS, 128)).astype(BF)
    picked = dot_nt(stat_block(joint, delta).astype(BF), pick)
    payload_ref[256:, :] = widen_stats(picked)


def weigh(query, key, value, grad, log_row, delta_row):
    probability = jnp.exp(dot_nt(key, query) - log_row)
    score_grad = probability * (dot_nt(value, grad) - delta_row)
    return probability.astype(BF), score_grad.astype(BF)


def key_side(probability, score_grad, query, grad):
    return jnp.concatenate([dot_nn(score_grad, query), dot_nn(probability, grad)], axis=1)


def runs(lanes, wide, narrow):
    return jnp.bitwise_and(iota((1, lanes), 1), wide - 1) < narrow


def level_one_back(block_ref, stat_ref, dq_ref, dkv_ref):
    query, key, value, grad = first_set(block_ref)
    log_row = jnp.where(runs(ROWS, 64, 16), MASKED, stat_ref[0:1, :])
    probability, score_grad = weigh(query, key, value, grad, log_row, stat_ref[1:2, :])
    dq_ref[...] = dot_tn(key, score_grad) * SCALE
    dkv_ref[...] = key_side(probability, score_grad, query, grad)


def level_two_back(first_ref, second_ref, stat_ref, dkv1_ref, dkv1_out_ref, dkv2_ref, dq_ref):
    _, key1, value1, _ = first_set(first_ref)
    query, key, value, grad = later_set(second_ref)
    log_row = jnp.where(runs(ROWS, 16, 4), MASKED, stat_ref[0:1, :])
    delta_row = stat_ref[1:2, :]
    own_query, own_grad = query[:128], grad[:128]
    probability, score_grad = weigh(own_query, key1, value1, own_grad, log_row[:, :128], delta_row[:, :128])
    dkv1_out_ref[...] = dkv1_ref[...] + key_side(probability, score_grad, own_query, own_grad)
    dq = dot_tn(key1, score_grad)
    probability, score_grad = weigh(query, key, value, grad, log_row, delta_row)
    dkv2_ref[...] = key_side(probability[:128], score_grad[:128], query, grad)
    dq_ref[...] = (dq + dot_tn(key, score_grad[:, :128])) * SCALE


def spread_lanes(value, pick):
    high, low = split2(value)
    return dot_nn(high, pick) + dot_nn(low, pick)


def spread_stats(log_row, delta_row, pick):
    return stat_rows(dot_nn(stat_block(log_row, delta_row).astype(BF), pick))


def level_three(first_ref, second_ref, third_ref, stat1_ref, stat2_ref, out1_ref, out2_ref, dq1_ref, dkv1_ref,
                dq2_ref, dkv2_ref, near_ref, far_ref):
    pick2 = subset_pick(6, 4)
    own_lane = iota((1, 128), 1) < 32

    query, key, value, grad = later_set(third_ref)
    old_log, old_delta = later_stats(third_ref)
    scores, prob_grad, powers, total, new_log, new_delta = set_stats(query, key, value, grad)
    log3, delta3 = merge(old_log, old_delta, new_log, new_delta)
    weight = (jnp.exp(new_log - log3) / total)[:, :128]
    out3 = dot_tn(value, powers[:, :128].astype(BF)) * weight
    own_query, own_grad = query[:128], grad[:128]
    own_log, own_delta = log3[:, :128], delta3[:, :128]

    _, key1, value1, _ = first_set(first_ref)
    octet_log = jnp.where(own_lane, own_log, MASKED)
    probability, score_grad = weigh(own_query, key1, value1, own_grad, octet_log, own_delta)
    dkv1 = dkv1_ref[...] + key_side(probability, score_grad, own_query, own_grad)
    dq = dot_tn(key1, score_grad)
    _, key2, value2, _ = later_set(second_ref)
    probability, score_grad = weigh(own_query, key2, value2, own_grad, own_log, own_delta)
    dkv2 = dkv2_ref[...] + key_side(probability[:128], score_grad[:128], own_query, own_grad)
    dq = dq + dot_tn(key2, score_grad)
    probability = jnp.exp(scores[:, :128] - own_log)
    dq = dq + dot_tn(key, (probability * (prob_grad[:, :128] - own_delta)).astype(BF))
    probability = jnp.exp(scores[:32] - log3)
    score_grad = (probability * (prob_grad[:32] - delta3)).astype(BF)
    dkv3 = key_side(probability.astype(BF), score_grad, query, grad)

    place = iota((128, 1), 0)
    target = lax.shift_left(lax.shift_right_logical(place, 2), 4) + jnp.bitwise_and(place, 3)
    own_pick = one_hot((iota((128, 128), 1) == target) & (place < 32))
    spread_log, spread_delta = spread_stats(own_log, own_delta, own_pick)
    in_third = runs(128, 16, 4)
    log2 = jnp.where(in_third, spread_log, stat2_ref[0:1, :128])
    delta2 = jnp.where(in_third, spread_delta, stat2_ref[1:2, :128])
    merged_t = jnp.where(own_lane, jnp.concatenate([dq * SCALE, out3], axis=0), 0.0)
    fade2 = jnp.exp(stat2_ref[0:1, :128] - log2)
    base_t = jnp.concatenate([dq2_ref[...], out2_ref[...] * fade2], axis=0)
    merged_t = base_t + spread_lanes(merged_t, own_pick)
    high, low = split2(dkv3)
    dkv2 = dkv2 + dot_tn(own_pick[:32], high) + dot_tn(own_pick[:32], low)

    spread_log, spread_delta = spread_stats(log2, delta2, pick2)
    in_second = runs(ROWS, 64, 16)
    log1 = jnp.where(in_second, spread_log, stat1_ref[0:1, :])
    delta1 = jnp.where(in_second, spread_delta, stat1_ref[1:2, :])
    fade1 = jnp.exp(stat1_ref[0:1, :] - log1)
    base_t = jnp.concatenate([dq1_ref[...], out1_ref[...] * fade1], axis=0)
    merged_t = base_t + spread_lanes(merged_t, pick2)
    high, low = split2(dkv2)
    dkv1 = dkv1 + dot_tn(pick2, high) + dot_tn(pick2, low)

    rows = merged_t.T.astype(BF)
    dkv1 = dkv1.astype(BF)
    stats = stat_block(log1, delta1)
    for slot in range(8):
        part = slice(slot * KEPT, (slot + 1) * KEPT)
        target_ref = far_ref if slot % 2 else near_ref
        target_ref[slot // 2, :KEPT, :] = rows[part]
        target_ref[slot // 2, KEPT:2 * KEPT, :] = dkv1[part]
        target_ref[slot // 2, 2 * KEPT:, :] = widen_stats(stats[:, part])


def returned_stats(block):
    return stat_rows(block[2 * KEPT:2 * KEPT + 8, :KEPT])


def kept_attended(info_ref, back_ref, kept_out_ref, kept_log_ref, att_ref):
    for local in range(LOCAL_HEADS):
        block = back_ref[slot_of_head(info_ref, local)]
        log_total, _ = returned_stats(block)
        fade = jnp.exp(kept_log_ref[local:local + 1, :] - log_total)
        fade = jnp.broadcast_to(fade, (HEAD_DIM, KEPT)).T
        sparse = block[:KEPT, 64:].astype(F32)
        att_ref[:, span(local)] = (kept_out_ref[:, span(local)] * fade + sparse).astype(BF)


def tall_pair(half, pair):
    return jnp.concatenate([tall_pick(head_of(half, 2 * pair)), tall_pick(head_of(half, 2 * pair + 1))], axis=1)


def final_grads(info_ref, qkv_ref, packed_ref, kept_grad_ref, back_ref, tall_ref, *rest):
    early, (dq_out_ref, dk_out_ref, dv_out_ref, held, sems) = rest[:9], rest[9:]
    moves = []
    for pair in range(PAIRS):
        back = [back_ref[slot_of_head(info_ref, 2 * pair + spot)] for spot in range(2)]
        key = qkv_ref[1, :, cols(pair)]
        query = diagonal(packed_ref[2 * pair, :KEPT, :64], packed_ref[2 * pair + 1, :KEPT, :64])
        grad = diagonal(kept_grad_ref[:, span(2 * pair)], kept_grad_ref[:, span(2 * pair + 1)])
        stats = [returned_stats(block) for block in back]
        log_total = jnp.concatenate([stat[0] for stat in stats], axis=1)
        delta = jnp.concatenate([stat[1] for stat in stats], axis=1)
        tall = tall_ref[:, cols(pair)]
        probability = jnp.exp(dot_nt(key, query) - log_total)
        score_grad = (probability * (dot_nt(qkv_ref[2, :, cols(pair)], grad) - delta)).astype(BF)
        more_dk = diagonal(*(block[KEPT:2 * KEPT, :64] for block in back))
        more_dv = diagonal(*(block[KEPT:2 * KEPT, 64:] for block in back))
        dk = dot_nn(jnp.concatenate([score_grad, tall], axis=1), jnp.concatenate([query, more_dk], axis=0))
        dv = dot_nn(
            jnp.concatenate([probability.astype(BF), tall], axis=1), jnp.concatenate([grad, more_dv], axis=0)
        )
        crossed = dot_tn(score_grad, key) * SCALE
        more_dq = diagonal(
            crossed[:64, :64] + back[0][:KEPT, :64].astype(F32), crossed[64:, 64:] + back[1][:KEPT, :64].astype(F32)
        )
        dq = dot_nn(jnp.concatenate([tall, tall], axis=1), jnp.concatenate(split2(more_dq), axis=0))
        for which, (more, target) in enumerate(((dq, dq_out_ref), (dk, dk_out_ref), (dv, dv_out_ref))):
            held[pair, which] = (early[3 * pair + which][...] + more).astype(BF)
            move = pltpu.make_async_copy(held.at[pair, which], target.at[:, cols(pair)], sems.at[pair, which])
            move.start()
            moves.append(move)
    for move in moves:
        move.wait()


def mix_base(info_ref, own_att_ref, other_att_ref, own_w_ref, other_w_ref, base_ref, own_tall_ref, other_tall_ref):
    base_ref[...] = dot_tn(own_att_ref[...], own_w_ref[...]) + dot_tn(other_att_ref[...], other_w_ref[...])
    for pair in range(PAIRS):
        own_tall_ref[:, cols(pair)] = tall_pair(info_ref[0], pair)
        other_tall_ref[:, cols(pair)] = tall_pair(1 - info_ref[0], pair)


def spread_kept(tall_ref, kept_ref):
    return jnp.concatenate(
        [
            dot_nn(
                tall_ref[:, cols(pair)], diagonal(kept_ref[:, span(2 * pair)], kept_ref[:, span(2 * pair + 1)])
            ).astype(BF)
            for pair in range(PAIRS)
        ],
        axis=1,
    )


def mix_own(base_ref, kept_ref, tall_ref, w_ref, out_ref):
    out_ref[...] = base_ref[...] + dot_nn(spread_kept(tall_ref, kept_ref), w_ref[...])


def mix_other(base_ref, kept_ref, tall_ref, w_ref, out_ref, held, sems):
    rows = spread_kept(tall_ref, kept_ref)
    moves = []
    for pair in range(PAIRS):
        held[pair] = (base_ref[:, cols(pair)] + dot_nn(rows, w_ref[:, cols(pair)])).astype(BF)
        move = pltpu.make_async_copy(held.at[pair], out_ref.at[:, cols(pair)], sems.at[pair])
        move.start()
        moves.append(move)
    for move in moves:
        move.wait()


def call(kernel, outs, args, flops=0, info=None, after=(), scratch=(), far_out=False):
    shapes = tuple(jax.ShapeDtypeStruct(*out) for out in outs)
    moved = sum(a.size * a.dtype.itemsize for a in args) + sum(
        int(np.prod(shape)) * jnp.dtype(dtype).itemsize for shape, dtype in outs
    )
    scalars = () if info is None else (info,)
    last = len(scalars) + len(args)

    def run(*refs):
        kernel(*refs[:last], *refs[last + len(after):])

    name = getattr(kernel, "func", kernel).__name__
    run.__name__ = name
    near, far = pl.BlockSpec(memory_space=pltpu.VMEM), pl.BlockSpec(memory_space=pltpu.HBM)
    return pl.pallas_call(
        run,
        out_shape=shapes,
        in_specs=[pl.BlockSpec(memory_space=pltpu.SMEM)] * len(scalars)
        + [near] * len(args)
        + [pl.BlockSpec(memory_space=pl.ANY)] * len(after),
        out_specs=(far if far_out else near,) * len(outs),
        scratch_shapes=list(scratch),
        compiler_params=pltpu.CompilerParams(vmem_limit_bytes=VMEM_LIMIT),
        cost_estimate=pl.CostEstimate(flops=flops, bytes_accessed=moved, transcendentals=0),
        name=name,
    )(*scalars, *args, *after)


def partner(array):
    return lax.ppermute(array, "head", [(0, 1), (1, 0)])


def flip(array, mask):
    return lax.ppermute(array, "seq", [(i, i ^ mask) for i in range(lax.axis_size("seq"))])


def gather_pair(array, first, second):
    return jnp.stack([array, flip(array, first), flip(array, second), flip(array, first ^ second)])


def octet_exchange(near, far):
    crossed = flip(far, 1)
    blocks = [jnp.stack([near[chip], crossed[chip]]) for chip in range(4)]
    arrived = [flip(blocks[chip], 2 * chip) for chip in (1, 2, 3)]
    return jnp.concatenate([blocks[0]] + arrived), blocks[3], arrived[0]


def body(queries, keys, values, weight_out, cotangent):
    half = lax.axis_index("head")
    place = lax.axis_index("seq")
    info = jnp.stack([half, jnp.bitwise_xor(place % 8, 6 * (place // 8 % 2))]).astype(jnp.int32)

    block = ((4, 2 * KEPT + 16, 128), BF)
    later_block = ((272, 128), BF)
    stat = ((8, ROWS), F32)
    square = ((ROWS, WIDE), F32)

    other_cot = partner(cotangent)
    qkv = jnp.stack([queries, keys, values])
    packed, hots = call(
        pack_data, [((LOCAL_HEADS, 2 * KEPT, 128), BF), ((WIDE, ROWS), BF)], (qkv,), flops=200000000, info=info
    )
    kept_out, kept_log = call(
        kept_forward, [((KEPT, WIDE), F32), ((8, KEPT), F32)], (qkv, packed), flops=100000000
    )
    out_t, log0, att_t = call(
        local_forward, [((WIDE, ROWS), F32), stat, ((WIDE, ROWS), BF)], (qkv,), flops=400000000, info=info,
    )
    grad, kept_grad, near, far = call(
        pack_grads, [((ROWS, WIDE), BF), ((KEPT, WIDE), BF), block, block],
        (packed, cotangent, other_cot, weight_out, hots, kept_out, kept_log), flops=400000000, info=info, after=(att_t,),
        scratch=[pltpu.VMEM((8, 2 * KEPT + 16, 128), BF)],
    )
    block1, _, arrived = octet_exchange(near, far)
    late_w, _ = lax.optimization_barrier((weight_out, near))
    late_att, _ = lax.optimization_barrier((att_t, arrived))
    own_w = lax.dynamic_slice_in_dim(late_w, half * WIDE, WIDE, 1)
    mix_w = partner(lax.dynamic_slice_in_dim(late_w, (1 - half) * WIDE, WIDE, 1))
    other_att_t = partner(late_att)

    half_rows = ((128, 128), F32)

    def backward(pair, after):
        return call(
            functools.partial(local_backward, pair), [((ROWS, 128), F32)] * 3, (qkv, grad, log0, out_t),
            flops=300000000, info=info, after=(after,),
        )

    sent2, stat1, out1 = call(
        level_one, [later_block, stat, ((64, ROWS), F32)], (block1,), flops=100000000
    )
    block2 = gather_pair(sent2, 14, 16)
    dq1, dkv1 = call(level_one_back, [((64, ROWS), F32), ((ROWS, 128), F32)], (block1, stat1), flops=100000000)
    early = list(backward(0, sent2))
    sent3, stat2, out2 = call(
        level_two, [later_block, stat, ((64, 128), F32)], (block2,), flops=100000000,
        after=(other_att_t, mix_w, dq1, early[-1]),
    )
    block3 = gather_pair(sent3, 64, 48)
    early.extend(backward(1, sent3))
    dkv1, dkv2, dq2 = call(
        level_two_back, [((ROWS, 128), F32), half_rows, ((64, 128), F32)], (block1, block2, stat2, dkv1),
        flops=100000000,
    )
    base, own_tall, other_tall = call(
        mix_base, [square, ((ROWS, WIDE), BF), ((ROWS, WIDE), BF)],
        (late_att, other_att_t, own_w, mix_w), flops=300000000, info=info,
    )
    near, far = call(
        level_three, [block, block],
        (block1, block2, block3, stat1, stat2, out1, out2, dq1, dkv1, dq2, dkv2), flops=300000000, after=(base, early[-1]),
    )
    back, crossed, _ = octet_exchange(near, far)
    early.extend(backward(2, crossed))
    (own_kept,) = call(
        kept_attended, [((KEPT, WIDE), BF)], (back, kept_out, kept_log), flops=10000000, info=info, after=(early[-1],)
    )
    other_kept = partner(own_kept)
    query_grad, key_grad, value_grad = call(
        final_grads, [((ROWS, WIDE), BF)] * 3, (qkv, packed, kept_grad, back, own_tall, *early),
        flops=200000000, info=info,
        scratch=[pltpu.VMEM((PAIRS, 3, ROWS, 128), BF), pltpu.SemaphoreType.DMA((PAIRS, 3))], far_out=True,
    )
    (nearly,) = call(mix_own, [square], (base, own_kept, own_tall, own_w), flops=200000000)
    (mixed,) = call(
        mix_other, [((ROWS, WIDE), BF)], (nearly, other_kept, other_tall, mix_w), flops=200000000,
        scratch=[pltpu.VMEM((PAIRS, ROWS, 128), BF), pltpu.SemaphoreType.DMA((PAIRS,))], far_out=True,
    )
    return mixed, query_grad, key_grad, value_grad


def solution(mesh):
    specs = P("seq", "head")
    return jax.shard_map(
        body,
        mesh=mesh,
        in_specs=(specs, specs, specs, P("head", None), specs),
        out_specs=(specs, specs, specs, specs),
        check_vma=False,
    )
```

time: 84.3 us -> 74.3 us (0.88); the launches traced: 82.6 us -> 74.2 us
  waiting for transfers between devices: 23.8 us -> 15.4 us
  local copies, waits for them, and re-layouts: 7.64 us -> 0.22 us
  starting transfers between devices: 22.9 us -> 29.3 us
  other arithmetic: 0.16 us -> 1.59 us
    ppermute x4 -> x14, starting transfers between devices: 9.78 us -> 24 us  [flip(): lax.ppermute(array, 'seq', [(i, i ^ mask) for i in range(lax.axis_size('s...]
    all_to_all x2 -> x0, waiting for transfers between devices: 11.7 us -> none  [the longest x1 9.91 us: body(): block1 = lax.all_to_all(sent, 'seq', 0, 0, axis_index_groups=octets)]
    all_to_all x2 -> x0, starting transfers between devices: 8.95 us -> none  [the longest x1 5.53 us: body(): block1 = lax.all_to_all(sent, 'seq', 0, 0, axis_index_groups=octets)]
    unnamed x28 -> x8, local copies, waits for them, and re-layouts: 7.58 us -> 0.06 us
    ppermute x4 -> x14, waiting for transfers between devices: 12.1 us -> 14.2 us  [flip(): lax.ppermute(array, 'seq', [(i, i ^ mask) for i in range(lax.axis_size('s...]
    another operation x3 -> x10, other arithmetic: 0.1 us -> 1.59 us  [the longest x1 1.39 us: body(): qkv = jnp.stack([queries, keys, values])]
    ppermute x4, waiting for transfers between devices: 0.01 us -> 1.22 us  [partner(): return lax.ppermute(array, 'head', [(0, 1), (1, 0)])]
    ppermute x4, starting transfers between devices: 4.15 us -> 5.3 us  [partner(): return lax.ppermute(array, 'head', [(0, 1), (1, 0)])]
  transfers between devices with their start and end apart: 10 -> 18, of which waited for: 6 -> 8; matrix products, arithmetic and copies ran while one was open for 0% -> 2% of each run, Pallas kernels for 22% -> 27%
where the time goes in v2:
time: 74.3 us; the launch traced here: 74.2 us
  starting transfers between devices  29.3 us (39%)
  Pallas kernels  26.6 us (36%)
  waiting for transfers between devices  15.4 us (21%)
  other arithmetic  1.59 us (2%)
  between operations  1.07 us (1%)
    pallas_call x17, Pallas kernels, call(): pl.pallas_call(run, out_shape=shapes, in_specs=[pl.BlockSpec(memory_space...  26.6 us
    ppermute x14, starting transfers between devices, flip(): lax.ppermute(array, 'seq', [(i, i ^ mask) for i in range(lax.axis_size('s...  24 us
    ppermute x14, waiting for transfers between devices, flip(): lax.ppermute(array, 'seq', [(i, i ^ mask) for i in range(lax.axis_size('s...  14.2 us
    ppermute x4, starting transfers between devices, partner(): return lax.ppermute(array, 'head', [(0, 1), (1, 0)])  5.3 us
  transfers between devices with their start and end apart: 18, of which 8 were waited for; matrix products, arithmetic and copies ran while one was open for 2% of the time, Pallas kernels for 27%

profile of v2, /device:TPU:2, one launch (start us, length us, event | category | flops | bytes accessed | tf_op | source)
XLA Modules:
  0.0 74.2 jit_solution(9227298298440377694)
XLA Ops:
  0.6 2.4 %collective-permute-start = (bf16[512,384]{1,0:T(8,128)(2,1)}, bf16[512,384]{1,0:T(8,128)(2,1)S(1)}, u32[]{:S(2)}, u32[]{:S(2)}) collective-permute-start(bf16[512,384]{1,0:T(8,128)(2,1)} %refs_2_.1), channel_id=1, source_target_pairs={{0,1},{1,0},{2,3},{3,2},{4,5},{5,4},{6,7},{7,6},{8,9},{9,8},{10,11... | collective-permute-start | bytes 1179656 | tf_op jit(solution)/shard_map/ppermute | solution.py:513
  3.0 0.1 pad_add_fusion.refs_0_
  3.1 1.4 %pad_maximum_fusion.refs_1_.refs_0_ = bf16[3,512,384]{2,1,0:T(8,128)(2,1)S(1)} fusion(bf16[1,512,384]{2,1,0:T(8,128)(2,1)} %bitcast.15, bf16[1,512,384]{2,1,0:T(8,128)(2,1)} %bitcast.16, bf16[1,512,384]{2,1,0:T(8,128)(2,1)} %bitcast.17), kind=kLoop, calls=%fused_computation | loop fusion | flops 1179648 | bytes 2359296 | tf_op jit(solution)/shard_map/stack | solution.py:542
  4.5 1.1 %pack_data.1 = (bf16[6,128,128]{2,1,0:T(8,128)(2,1)S(1)}, bf16[384,512]{1,0:T(8,128)(2,1)S(1)}) custom-call(s32[2]{0:T(128)S(1)} %pad_add_fusion.refs_0_, bf16[3,512,384]{2,1,0:T(8,128)(2,1)S(1)} %pad_maximum_fusion.refs_1_.refs_0_), custom_call_target="tpu_custom_call" | custom-call | flops 200000000 | bytes 1769472 | tf_op jit(solution)/shard_map/pack_data/pallas_call | solution.py:498
  5.6 0.0 copy-start
  5.6 0.0 copy-start.1
  5.6 0.9 %kept_forward.1 = (f32[64,384]{1,0:T(8,128)S(1)}, f32[8,64]{1,0:T(8,128)S(1)}) custom-call(bf16[3,512,384]{2,1,0:T(8,128)(2,1)S(1)} %pad_maximum_fusion.refs_1_.refs_0_, bf16[6,128,128]{2,1,0:T(8,128)(2,1)S(1)} %get-tuple-element.46.refs_1_.refs_2_), custom_call_target="tpu_custom_call" | custom-call | flops 100000000 | bytes 1476608 | tf_op jit(solution)/shard_map/kept_forward/pallas_call | solution.py:498
  6.5 4.0 %local_forward.1 = (f32[384,512]{1,0:T(8,128)S(1)}, f32[8,512]{1,0:T(8,128)S(1)}, bf16[384,512]{1,0:T(8,128)(2,1)S(1)}) custom-call(s32[2]{0:T(128)S(1)} %pad_add_fusion.refs_0_, bf16[3,512,384]{2,1,0:T(8,128)(2,1)S(1)} %pad_maximum_fusion.refs_1_.refs_0_), custom_call_target="tpu_custom_call" | custom-call | flops 400000000 | bytes 2375680 | tf_op jit(solution)/shard_map/local_forward/pallas_call | solution.py:498
  10.6 1.2 %collective-permute-done.refs_3_ = bf16[512,384]{1,0:T(8,128)(2,1)S(1)} collective-permute-done((bf16[512,384]{1,0:T(8,128)(2,1)}, bf16[512,384]{1,0:T(8,128)(2,1)S(1)}, u32[]{:S(2)}, u32[]{:S(2)}) %collective-permute-start) | collective-permute-done | bytes 393248 | tf_op jit(solution)/shard_map/ppermute | solution.py:513
  11.8 0.0 copy-done
  11.8 0.0 copy-done.1
  11.8 1.8 %pack_grads.1 = (bf16[512,384]{1,0:T(8,128)(2,1)S(1)}, bf16[64,384]{1,0:T(8,128)(2,1)S(1)}, bf16[4,144,128]{2,1,0:T(8,128)(2,1)S(1)}, bf16[4,144,128]{2,1,0:T(8,128)(2,1)S(1)}) custom-call(s32[2]{0:T(128)S(1)} %pad_add_fusion.refs_0_, bf16[6,128,128]{2,1,0:T(8,128)(2,1)S(1)} %get-tuple-element.46.refs_1_.refs_2_, bf16[512,384]{1,0:T(8,128)(2,1)S(1)} %copy-done.1, ...), custom_call_target="tpu_custom_call" | custom-call | flops 400000000 | bytes 2803712 | tf_op jit(solution)/shard_map/pack_grads/pallas_call | solution.py:498
  13.6 0.1 collective-permute-start.1
  13.7 0.1 constant_dynamic-slice_fusion
  13.8 0.4 collective-permute-start.4
  14.2 0.9 %collective-permute-done.1 = bf16[4,144,128]{2,1,0:T(8,128)(2,1)S(1)} collective-permute-done((bf16[4,144,128]{2,1,0:T(8,128)(2,1)S(1)}, bf16[4,144,128]{2,1,0:T(8,128)(2,1)S(1)}, u32[]{:S(2)}, u32[]{:S(2)}) %collective-permute-start.1) | collective-permute-done | bytes 147488 | tf_op jit(solution)/shard_map/ppermute | solution.py:517
  15.1 2.0 %collective-permute-start.2 = (bf16[2,144,128]{2,1,0:T(8,128)(2,1)S(1)}, bf16[2,144,128]{2,1,0:T(8,128)(2,1)S(1)}, u32[]{:S(2)}, u32[]{:S(2)}) collective-permute-start(bf16[2,144,128]{2,1,0:T(8,128)(2,1)S(1)} %pad_maximum_fusion.3), channel_id=1, source_target_pairs={{0,4},{2,6},{4,0},{6,2},{8,12},{10,14},{12,8},{14,10},{16,20},{18,... | collective-permute-start | bytes 221192 | tf_op jit(solution)/shard_map/ppermute | solution.py:517
  17.1 3.4 %collective-permute-start.5 = (bf16[2,144,128]{2,1,0:T(8,128)(2,1)S(1)}, bf16[2,144,128]{2,1,0:T(8,128)(2,1)S(1)}, u32[]{:S(2)}, u32[]{:S(2)}) collective-permute-start(bf16[2,144,128]{2,1,0:T(8,128)(2,1)S(1)} %pad_maximum_fusion.4), channel_id=1, source_target_pairs={{0,8},{2,10},{4,12},{6,14},{8,0},{10,2},{12,4},{14,6},{16,24},{18,... | collective-permute-start | bytes 221192 | tf_op jit(solution)/shard_map/ppermute | solution.py:517
  20.5 0.1 collective-permute-start.6
  20.6 0.0 collective-permute-done.2
  20.6 0.9 %collective-permute-start.3 = (bf16[384,512]{1,0:T(8,128)(2,1)S(1)}, bf16[384,512]{1,0:T(8,128)(2,1)S(1)}, u32[]{:S(2)}, u32[]{:S(2)}) collective-permute-start(bf16[384,512]{1,0:T(8,128)(2,1)S(1)} %get-tuple-element.52.refs_8_.refs_1_), channel_id=1, source_target_pairs={{0,1},{1,0},{2,3},{3,2},{4,5},{5,4},{6,7},{7,6},{8,9},{9,8},{10,11... | collective-permute-start | bytes 1179656 | tf_op jit(solution)/shard_map/ppermute | solution.py:513
  21.6 4.2 %collective-permute-done.5 = bf16[2,144,128]{2,1,0:T(8,128)(2,1)S(1)} collective-permute-done((bf16[2,144,128]{2,1,0:T(8,128)(2,1)S(1)}, bf16[2,144,128]{2,1,0:T(8,128)(2,1)S(1)}, u32[]{:S(2)}, u32[]{:S(2)}) %collective-permute-start.5) | collective-permute-done | bytes 73760 | tf_op jit(solution)/shard_map/ppermute | solution.py:517
  25.8 1.0 %collective-permute-done.6 = bf16[2,144,128]{2,1,0:T(8,128)(2,1)S(1)} collective-permute-done((bf16[2,144,128]{2,1,0:T(8,128)(2,1)S(1)}, bf16[2,144,128]{2,1,0:T(8,128)(2,1)S(1)}, u32[]{:S(2)}, u32[]{:S(2)}) %collective-permute-start.6) | collective-permute-done | bytes 73760 | tf_op jit(solution)/shard_map/ppermute | solution.py:517
  26.8 0.8 %level_one.1 = (bf16[272,128]{1,0:T(8,128)(2,1)S(1)}, f32[8,512]{1,0:T(8,128)S(1)}, f32[64,512]{1,0:T(8,128)S(1)}) custom-call(bf16[8,144,128]{2,1,0:T(8,128)(2,1)S(1)} %constant_dynamic-update-slice_fusion.refs_0_), custom_call_target="tpu_custom_call" | custom-call | flops 100000000 | bytes 512000 | tf_op jit(solution)/shard_map/level_one/pallas_call | solution.py:498
  27.7 5.2 %collective-permute-start.9 = (bf16[272,128]{1,0:T(8,128)(2,1)S(1)}, bf16[272,128]{1,0:T(8,128)(2,1)S(1)}, u32[]{:S(2)}, u32[]{:S(2)}) collective-permute-start(bf16[272,128]{1,0:T(8,128)(2,1)S(1)} %get-tuple-element.55.refs_5_), channel_id=1, source_target_pairs={{0,60},{2,62},{4,56},{6,58},{8,52},{10,54},{12,48},{14,50},{16,44}... | collective-permute-start | bytes 208904 | tf_op jit(solution)/shard_map/ppermute | solution.py:517
  32.9 0.5 collective-permute-start.8
  33.4 0.2 collective-permute-start.7
  33.6 1.0 %level_one_back.1 = (f32[64,512]{1,0:T(8,128)S(1)}, f32[512,128]{1,0:T(8,128)S(1)}) custom-call(bf16[8,144,128]{2,1,0:T(8,128)(2,1)S(1)} %constant_dynamic-update-slice_fusion.refs_0_, f32[8,512]{1,0:T(8,128)S(1)} %get-tuple-element.56.refs_1_.refs_3_), custom_call_target="tpu_custom_call" | custom-call | flops 100000000 | bytes 704512 | tf_op jit(solution)/shard_map/level_one_back/pallas_call | solution.py:498
  34.6 2.1 %local_backward.3 = (f32[512,128]{1,0:T(8,128)S(1)}, f32[512,128]{1,0:T(8,128)S(1)}, f32[512,128]{1,0:T(8,128)S(1)}) custom-call(s32[2]{0:T(128)S(1)} %pad_add_fusion.refs_0_, bf16[3,512,384]{2,1,0:T(8,128)(2,1)S(1)} %pad_maximum_fusion.refs_1_.refs_0_, bf16[512,384]{1,0:T(8,128)(2,1)S(1)} %get-tuple-element.58.refs_2_, ...), custom_call_target="tpu_custom_call" | custom-call | flops 300000000 | bytes 3162112 | tf_op jit(solution)/shard_map/local_backward/pallas_call | solution.py:498
  36.7 1.1 %collective-permute-done.9 = bf16[272,128]{1,0:T(8,128)(2,1)S(1)} collective-permute-done((bf16[272,128]{1,0:T(8,128)(2,1)S(1)}, bf16[272,128]{1,0:T(8,128)(2,1)S(1)}, u32[]{:S(2)}, u32[]{:S(2)}) %collective-permute-start.9) | collective-permute-done | bytes 69664 | tf_op jit(solution)/shard_map/ppermute | solution.py:517
  37.8 0.0 collective-permute-done.8
  37.8 1.9 %collective-permute-done.7 = bf16[272,128]{1,0:T(8,128)(2,1)S(1)} collective-permute-done((bf16[272,128]{1,0:T(8,128)(2,1)S(1)}, bf16[272,128]{1,0:T(8,128)(2,1)S(1)}, u32[]{:S(2)}, u32[]{:S(2)}) %collective-permute-start.7) | collective-permute-done | bytes 69664 | tf_op jit(solution)/shard_map/ppermute | solution.py:517
  39.7 0.0 collective-permute-done.4.refs_4_.refs_2_.refs_3_
  39.7 0.0 collective-permute-done.3.refs_2_.refs_1_
  39.7 0.9 %level_two.1 = (bf16[272,128]{1,0:T(8,128)(2,1)S(1)}, f32[8,512]{1,0:T(8,128)S(1)}, f32[64,128]{1,0:T(8,128)S(1)}) custom-call(bf16[4,272,128]{2,1,0:T(8,128)(2,1)S(1)} %pad_maximum_fusion.1.refs_0_.refs_1_, bf16[384,512]{1,0:T(8,128)(2,1)S(1)} %collective-permute-done.3.refs_2_.refs_1_, bf16[384,384]{1,0:T(8,128)(2,1)S(1)} %collective-permute-done.4.refs_4_.refs_2_.refs_3_, ...), custom_call_target="tpu_custom_call" | custom-call | flops 100000000 | bytes 397312 | tf_op jit(solution)/shard_map/level_two/pallas_call | solution.py:498
  40.6 4.7 %collective-permute-start.12 = (bf16[272,128]{1,0:T(8,128)(2,1)S(1)}, bf16[272,128]{1,0:T(8,128)(2,1)S(1)}, u32[]{:S(2)}, u32[]{:S(2)}) collective-permute-start(bf16[272,128]{1,0:T(8,128)(2,1)S(1)} %get-tuple-element.62.refs_5_), channel_id=1, source_target_pairs={{0,224},{2,226},{4,228},{6,230},{8,232},{10,234},{12,236},{14,238}... | collective-permute-start | bytes 208904 | tf_op jit(solution)/shard_map/ppermute | solution.py:517
  45.2 0.2 collective-permute-start.11
  45.4 1.4 %collective-permute-start.10 = (bf16[272,128]{1,0:T(8,128)(2,1)S(1)}, bf16[272,128]{1,0:T(8,128)(2,1)S(1)}, u32[]{:S(2)}, u32[]{:S(2)}) collective-permute-start(bf16[272,128]{1,0:T(8,128)(2,1)S(1)} %get-tuple-element.62.refs_5_), channel_id=1, source_target_pairs={{0,128},{2,130},{4,132},{6,134},{8,136},{10,138},{12,140},{14,142}... | collective-permute-start | bytes 208904 | tf_op jit(solution)/shard_map/ppermute | solution.py:517
  46.8 0.9 %level_two_back.1 = (f32[512,128]{1,0:T(8,128)S(1)}, f32[128,128]{1,0:T(8,128)S(1)}, f32[64,128]{1,0:T(8,128)S(1)}) custom-call(bf16[8,144,128]{2,1,0:T(8,128)(2,1)S(1)} %constant_dynamic-update-slice_fusion.refs_0_, bf16[4,272,128]{2,1,0:T(8,128)(2,1)S(1)} %pad_maximum_fusion.1.refs_0_.refs_1_, f32[8,512]{1,0:T(8,128)S(1)} %get-tuple-element.63.refs_2_.refs_4_, ...), custom_call_target="tpu_custom_call" | custom-call | flops 100000000 | bytes 1212416 | tf_op jit(solution)/shard_map/level_two_back/pallas_call | solution.py:498
  47.7 2.1 %local_backward.4 = (f32[512,128]{1,0:T(8,128)S(1)}, f32[512,128]{1,0:T(8,128)S(1)}, f32[512,128]{1,0:T(8,128)S(1)}) custom-call(s32[2]{0:T(128)S(1)} %pad_add_fusion.refs_0_, bf16[3,512,384]{2,1,0:T(8,128)(2,1)S(1)} %pad_maximum_fusion.refs_1_.refs_0_, bf16[512,384]{1,0:T(8,128)(2,1)S(1)} %get-tuple-element.58.refs_2_, ...), custom_call_target="tpu_custom_call" | custom-call | flops 300000000 | bytes 3162112 | tf_op jit(solution)/shard_map/local_backward/pallas_call | solution.py:498
  49.8 1.4 %mix_base.1 = (f32[512,384]{1,0:T(8,128)S(1)}, bf16[512,384]{1,0:T(8,128)(2,1)S(1)}, bf16[512,384]{1,0:T(8,128)(2,1)S(1)}) custom-call(s32[2]{0:T(128)S(1)} %pad_add_fusion.refs_0_, bf16[384,512]{1,0:T(8,128)(2,1)S(1)} %get-tuple-element.52.refs_8_.refs_1_, bf16[384,512]{1,0:T(8,128)(2,1)S(1)} %collective-permute-done.3.refs_2_.refs_1_, ...), custom_call_target="tpu_custom_call" | custom-call | flops 300000000 | bytes 2949120 | tf_op jit(solution)/shard_map/mix_base/pallas_call | solution.py:498
  51.2 0.0 collective-permute-done.12
  51.2 0.0 collective-permute-done.11
  51.2 0.0 collective-permute-done.10
  51.3 1.7 %level_three.1 = (bf16[4,144,128]{2,1,0:T(8,128)(2,1)S(1)}, bf16[4,144,128]{2,1,0:T(8,128)(2,1)S(1)}) custom-call(bf16[8,144,128]{2,1,0:T(8,128)(2,1)S(1)} %constant_dynamic-update-slice_fusion.refs_0_, bf16[4,272,128]{2,1,0:T(8,128)(2,1)S(1)} %pad_maximum_fusion.1.refs_0_.refs_1_, bf16[4,272,128]{2,1,0:T(8,128)(2,1)S(1)} %pad_maximum_fusion.2.refs_2_, ...), custom_call_target="tpu_custom_call" | custom-call | flops 300000000 | bytes 1835008 | tf_op jit(solution)/shard_map/level_three/pallas_call | solution.py:498
  53.0 0.1 collective-permute-start.13
  53.1 1.3 %collective-permute-done.13 = bf16[4,144,128]{2,1,0:T(8,128)(2,1)S(1)} collective-permute-done((bf16[4,144,128]{2,1,0:T(8,128)(2,1)S(1)}, bf16[4,144,128]{2,1,0:T(8,128)(2,1)S(1)}, u32[]{:S(2)}, u32[]{:S(2)}) %collective-permute-start.13) | collective-permute-done | bytes 147488 | tf_op jit(solution)/shard_map/ppermute | solution.py:517
  54.5 3.4 %collective-permute-start.14 = (bf16[2,144,128]{2,1,0:T(8,128)(2,1)S(1)}, bf16[2,144,128]{2,1,0:T(8,128)(2,1)S(1)}, u32[]{:S(2)}, u32[]{:S(2)}) collective-permute-start(bf16[2,144,128]{2,1,0:T(8,128)(2,1)S(1)} %pad_maximum_fusion.6), channel_id=1, source_target_pairs={{0,4},{2,6},{4,0},{6,2},{8,12},{10,14},{12,8},{14,10},{16,20},{18,... | collective-permute-start | bytes 221192 | tf_op jit(solution)/shard_map/ppermute | solution.py:517
  57.9 0.6 collective-permute-start.15
  58.5 2.2 %collective-permute-start.16 = (bf16[2,144,128]{2,1,0:T(8,128)(2,1)S(1)}, bf16[2,144,128]{2,1,0:T(8,128)(2,1)S(1)}, u32[]{:S(2)}, u32[]{:S(2)}) collective-permute-start(bf16[2,144,128]{2,1,0:T(8,128)(2,1)S(1)} %pad_maximum_fusion.8.refs_5_), channel_id=1, source_target_pairs={{0,12},{2,14},{4,8},{6,10},{8,4},{10,6},{12,0},{14,2},{16,28},{18,... | collective-permute-start | bytes 221192 | tf_op jit(solution)/shard_map/ppermute | solution.py:517
  60.7 2.1 %local_backward.5 = (f32[512,128]{1,0:T(8,128)S(1)}, f32[512,128]{1,0:T(8,128)S(1)}, f32[512,128]{1,0:T(8,128)S(1)}) custom-call(s32[2]{0:T(128)S(1)} %pad_add_fusion.refs_0_, bf16[3,512,384]{2,1,0:T(8,128)(2,1)S(1)} %pad_maximum_fusion.refs_1_.refs_0_, bf16[512,384]{1,0:T(8,128)(2,1)S(1)} %get-tuple-element.58.refs_2_, ...), custom_call_target="tpu_custom_call" | custom-call | flops 300000000 | bytes 3162112 | tf_op jit(solution)/shard_map/local_backward/pallas_call | solution.py:498
  62.8 0.0 collective-permute-done.14
  62.8 3.8 %collective-permute-done.15 = bf16[2,144,128]{2,1,0:T(8,128)(2,1)S(1)} collective-permute-done((bf16[2,144,128]{2,1,0:T(8,128)(2,1)S(1)}, bf16[2,144,128]{2,1,0:T(8,128)(2,1)S(1)}, u32[]{:S(2)}, u32[]{:S(2)}) %collective-permute-start.15) | collective-permute-done | bytes 73760 | tf_op jit(solution)/shard_map/ppermute | solution.py:517
  66.6 0.0 collective-permute-done.16
  66.7 0.7 %kept_attended.1.refs_1_ = bf16[64,384]{1,0:T(8,128)(2,1)S(1)} custom-call(s32[2]{0:T(128)S(1)} %pad_add_fusion.refs_0_, bf16[8,144,128]{2,1,0:T(8,128)(2,1)S(1)} %constant_dynamic-update-slice_fusion.3.refs_1_.refs_4_, f32[64,384]{1,0:T(8,128)S(1)} %get-tuple-element.48.refs_6_.refs_2_, f32[8,64]{1,0:T(8,128)S(1)} %get-tuple-element.49.refs_7_.refs_3_, ...), custom_call_target="tpu_custom_call" | custom-call | flops 10000000 | bytes 444416 | tf_op jit(solution)/shard_map/kept_attended/pallas_call | solution.py:498
  67.4 1.6 %collective-permute-start.17 = (bf16[64,384]{1,0:T(8,128)(2,1)S(1)}, bf16[64,384]{1,0:T(8,128)(2,1)S(1)}, u32[]{:S(2)}, u32[]{:S(2)}) collective-permute-start(bf16[64,384]{1,0:T(8,128)(2,1)S(1)} %kept_attended.1.refs_1_), channel_id=1, source_target_pairs={{0,1},{1,0},{2,3},{3,2},{4,5},{5,4},{6,7},{7,6},{8,9},{9,8},{10,11... | collective-permute-start | bytes 147464 | tf_op jit(solution)/shard_map/ppermute | solution.py:513
  69.0 0.5 mix_own.1.refs_0_
  69.6 3.2 %final_grads.1 = (bf16[512,384]{1,0:T(8,128)(2,1)}, bf16[512,384]{1,0:T(8,128)(2,1)}, bf16[512,384]{1,0:T(8,128)(2,1)}) custom-call(s32[2]{0:T(128)S(1)} %pad_add_fusion.refs_0_, bf16[3,512,384]{2,1,0:T(8,128)(2,1)S(1)} %pad_maximum_fusion.refs_1_.refs_0_, bf16[6,128,128]{2,1,0:T(8,128)(2,1)S(1)} %get-tuple-element.46.refs_1_.refs_2_, ...), custom_call_target="tpu_custom_call" | custom-call | flops 200000000 | bytes 5652480 | tf_op jit(solution)/shard_map/final_grads/pallas_call | solution.py:498
  72.8 0.0 collective-permute-done.17.refs_1_
  72.8 1.3 %mix_other.1 = bf16[512,384]{1,0:T(8,128)(2,1)} custom-call(f32[512,384]{1,0:T(8,128)S(1)} %mix_own.1.refs_0_, bf16[64,384]{1,0:T(8,128)(2,1)S(1)} %collective-permute-done.17.refs_1_, bf16[512,384]{1,0:T(8,128)(2,1)S(1)} %get-tuple-element.75.refs_2_, bf16[384,384]{1,0:T(8,128)(2,1)S(1)} %collective-permute-done.4.refs_4_.refs_2_.refs_3_), custom_call_target="tpu_custom_call" | custom-call | flops 200000000 | bytes 1916928 | tf_op jit(solution)/shard_map/mix_other/pallas_call | solution.py:498
  (18 shorter events, 0.3 us)
Async XLA Ops:
  0.6 11.2 %collective-permute-start = (bf16[512,384]{1,0:T(8,128)(2,1)}, bf16[512,384]{1,0:T(8,128)(2,1)S(1)}, u32[]{:S(2)}, u32[]{:S(2)}) collective-permute-start(bf16[512,384]{1,0:T(8,128)(2,1)} %refs_2_.1), channel_id=1, source_target_pairs={{0,1},{1,0},{2,3},{3,2},{4,5},{5,4},{6,7},{7,6},{8,9},{9,8},{10,11... | collective-permute-start | bytes 1179656 | tf_op jit(solution)/shard_map/ppermute | solution.py:513
  5.6 6.2 %copy-start = (bf16[384,768]{1,0:T(8,128)(2,1)S(1)}, bf16[384,768]{1,0:T(8,128)(2,1)}, u32[]{:S(2)}) copy-start(bf16[384,768]{1,0:T(8,128)(2,1)} %refs_4_.1) | copy-start | bytes 1769476
  5.6 6.2 %copy-start.1 = (bf16[512,384]{1,0:T(8,128)(2,1)S(1)}, bf16[512,384]{1,0:T(8,128)(2,1)}, u32[]{:S(2)}) copy-start(bf16[512,384]{1,0:T(8,128)(2,1)} %refs_2_.1) | copy-start | bytes 1179652
  13.6 1.5 %collective-permute-start.1 = (bf16[4,144,128]{2,1,0:T(8,128)(2,1)S(1)}, bf16[4,144,128]{2,1,0:T(8,128)(2,1)S(1)}, u32[]{:S(2)}, u32[]{:S(2)}) collective-permute-start(bf16[4,144,128]{2,1,0:T(8,128)(2,1)S(1)} %get-tuple-element.51), channel_id=1, source_target_pairs={{0,2},{2,0},{4,6},{6,4},{8,10},{10,8},{12,14},{14,12},{16,18},{18,... | collective-permute-start | bytes 442376 | tf_op jit(solution)/shard_map/ppermute | solution.py:517
  13.8 25.9 %collective-permute-start.4 = (bf16[384,384]{1,0:T(8,128)(2,1)S(1)}, bf16[384,384]{1,0:T(8,128)(2,1)S(1)}, u32[]{:S(2)}, u32[]{:S(2)}) collective-permute-start(bf16[384,384]{1,0:T(8,128)(2,1)S(1)} %get-tuple-element.86), channel_id=1, source_target_pairs={{0,1},{1,0},{2,3},{3,2},{4,5},{5,4},{6,7},{7,6},{8,9},{9,8},{10,11... | collective-permute-start | bytes 884744 | tf_op jit(solution)/shard_map/ppermute | solution.py:513
  15.1 5.5 %collective-permute-start.2 = (bf16[2,144,128]{2,1,0:T(8,128)(2,1)S(1)}, bf16[2,144,128]{2,1,0:T(8,128)(2,1)S(1)}, u32[]{:S(2)}, u32[]{:S(2)}) collective-permute-start(bf16[2,144,128]{2,1,0:T(8,128)(2,1)S(1)} %pad_maximum_fusion.3), channel_id=1, source_target_pairs={{0,4},{2,6},{4,0},{6,2},{8,12},{10,14},{12,8},{14,10},{16,20},{18,... | collective-permute-start | bytes 221192 | tf_op jit(solution)/shard_map/ppermute | solution.py:517
  17.1 8.7 %collective-permute-start.5 = (bf16[2,144,128]{2,1,0:T(8,128)(2,1)S(1)}, bf16[2,144,128]{2,1,0:T(8,128)(2,1)S(1)}, u32[]{:S(2)}, u32[]{:S(2)}) collective-permute-start(bf16[2,144,128]{2,1,0:T(8,128)(2,1)S(1)} %pad_maximum_fusion.4), channel_id=1, source_target_pairs={{0,8},{2,10},{4,12},{6,14},{8,0},{10,2},{12,4},{14,6},{16,24},{18,... | collective-permute-start | bytes 221192 | tf_op jit(solution)/shard_map/ppermute | solution.py:517
  20.5 6.3 %collective-permute-start.6 = (bf16[2,144,128]{2,1,0:T(8,128)(2,1)S(1)}, bf16[2,144,128]{2,1,0:T(8,128)(2,1)S(1)}, u32[]{:S(2)}, u32[]{:S(2)}) collective-permute-start(bf16[2,144,128]{2,1,0:T(8,128)(2,1)S(1)} %pad_maximum_fusion.5), channel_id=1, source_target_pairs={{0,12},{2,14},{4,8},{6,10},{8,4},{10,6},{12,0},{14,2},{16,28},{18,... | collective-permute-start | bytes 221192 | tf_op jit(solution)/shard_map/ppermute | solution.py:517
  20.6 19.1 %collective-permute-start.3 = (bf16[384,512]{1,0:T(8,128)(2,1)S(1)}, bf16[384,512]{1,0:T(8,128)(2,1)S(1)}, u32[]{:S(2)}, u32[]{:S(2)}) collective-permute-start(bf16[384,512]{1,0:T(8,128)(2,1)S(1)} %get-tuple-element.52.refs_8_.refs_1_), channel_id=1, source_target_pairs={{0,1},{1,0},{2,3},{3,2},{4,5},{5,4},{6,7},{7,6},{8,9},{9,8},{10,11... | collective-permute-start | bytes 1179656 | tf_op jit(solution)/shard_map/ppermute | solution.py:513
  27.7 10.1 %collective-permute-start.9 = (bf16[272,128]{1,0:T(8,128)(2,1)S(1)}, bf16[272,128]{1,0:T(8,128)(2,1)S(1)}, u32[]{:S(2)}, u32[]{:S(2)}) collective-permute-start(bf16[272,128]{1,0:T(8,128)(2,1)S(1)} %get-tuple-element.55.refs_5_), channel_id=1, source_target_pairs={{0,60},{2,62},{4,56},{6,58},{8,52},{10,54},{12,48},{14,50},{16,44}... | collective-permute-start | bytes 208904 | tf_op jit(solution)/shard_map/ppermute | solution.py:517
  32.9 4.8 %collective-permute-start.8 = (bf16[272,128]{1,0:T(8,128)(2,1)S(1)}, bf16[272,128]{1,0:T(8,128)(2,1)S(1)}, u32[]{:S(2)}, u32[]{:S(2)}) collective-permute-start(bf16[272,128]{1,0:T(8,128)(2,1)S(1)} %get-tuple-element.55.refs_5_), channel_id=1, source_target_pairs={{0,32},{2,34},{4,36},{6,38},{8,40},{10,42},{12,44},{14,46},{16,48}... | collective-permute-start | bytes 208904 | tf_op jit(solution)/shard_map/ppermute | solution.py:517
  33.4 6.3 %collective-permute-start.7 = (bf16[272,128]{1,0:T(8,128)(2,1)S(1)}, bf16[272,128]{1,0:T(8,128)(2,1)S(1)}, u32[]{:S(2)}, u32[]{:S(2)}) collective-permute-start(bf16[272,128]{1,0:T(8,128)(2,1)S(1)} %get-tuple-element.55.refs_5_), channel_id=1, source_target_pairs={{0,28},{2,30},{4,24},{6,26},{8,20},{10,22},{12,16},{14,18},{16,12}... | collective-permute-start | bytes 208904 | tf_op jit(solution)/shard_map/ppermute | solution.py:517
  40.6 10.7 %collective-permute-start.12 = (bf16[272,128]{1,0:T(8,128)(2,1)S(1)}, bf16[272,128]{1,0:T(8,128)(2,1)S(1)}, u32[]{:S(2)}, u32[]{:S(2)}) collective-permute-start(bf16[272,128]{1,0:T(8,128)(2,1)S(1)} %get-tuple-element.62.refs_5_), channel_id=1, source_target_pairs={{0,224},{2,226},{4,228},{6,230},{8,232},{10,234},{12,236},{14,238}... | collective-permute-start | bytes 208904 | tf_op jit(solution)/shard_map/ppermute | solution.py:517
  45.2 6.0 %collective-permute-start.11 = (bf16[272,128]{1,0:T(8,128)(2,1)S(1)}, bf16[272,128]{1,0:T(8,128)(2,1)S(1)}, u32[]{:S(2)}, u32[]{:S(2)}) collective-permute-start(bf16[272,128]{1,0:T(8,128)(2,1)S(1)} %get-tuple-element.62.refs_5_), channel_id=1, source_target_pairs={{0,96},{2,98},{4,100},{6,102},{8,104},{10,106},{12,108},{14,110},{... | collective-permute-start | bytes 208904 | tf_op jit(solution)/shard_map/ppermute | solution.py:517
  45.4 5.8 %collective-permute-start.10 = (bf16[272,128]{1,0:T(8,128)(2,1)S(1)}, bf16[272,128]{1,0:T(8,128)(2,1)S(1)}, u32[]{:S(2)}, u32[]{:S(2)}) collective-permute-start(bf16[272,128]{1,0:T(8,128)(2,1)S(1)} %get-tuple-element.62.refs_5_), channel_id=1, source_target_pairs={{0,128},{2,130},{4,132},{6,134},{8,136},{10,138},{12,140},{14,142}... | collective-permute-start | bytes 208904 | tf_op jit(solution)/shard_map/ppermute | solution.py:517
  53.0 1.5 %collective-permute-start.13 = (bf16[4,144,128]{2,1,0:T(8,128)(2,1)S(1)}, bf16[4,144,128]{2,1,0:T(8,128)(2,1)S(1)}, u32[]{:S(2)}, u32[]{:S(2)}) collective-permute-start(bf16[4,144,128]{2,1,0:T(8,128)(2,1)S(1)} %get-tuple-element.72), channel_id=1, source_target_pairs={{0,2},{2,0},{4,6},{6,4},{8,10},{10,8},{12,14},{14,12},{16,18},{18,... | collective-permute-start | bytes 442376 | tf_op jit(solution)/shard_map/ppermute | solution.py:517
  54.5 8.3 %collective-permute-start.14 = (bf16[2,144,128]{2,1,0:T(8,128)(2,1)S(1)}, bf16[2,144,128]{2,1,0:T(8,128)(2,1)S(1)}, u32[]{:S(2)}, u32[]{:S(2)}) collective-permute-start(bf16[2,144,128]{2,1,0:T(8,128)(2,1)S(1)} %pad_maximum_fusion.6), channel_id=1, source_target_pairs={{0,4},{2,6},{4,0},{6,2},{8,12},{10,14},{12,8},{14,10},{16,20},{18,... | collective-permute-start | bytes 221192 | tf_op jit(solution)/shard_map/ppermute | solution.py:517
  57.9 8.7 %collective-permute-start.15 = (bf16[2,144,128]{2,1,0:T(8,128)(2,1)S(1)}, bf16[2,144,128]{2,1,0:T(8,128)(2,1)S(1)}, u32[]{:S(2)}, u32[]{:S(2)}) collective-permute-start(bf16[2,144,128]{2,1,0:T(8,128)(2,1)S(1)} %pad_maximum_fusion.7), channel_id=1, source_target_pairs={{0,8},{2,10},{4,12},{6,14},{8,0},{10,2},{12,4},{14,6},{16,24},{18,... | collective-permute-start | bytes 221192 | tf_op jit(solution)/shard_map/ppermute | solution.py:517
  58.5 8.2 %collective-permute-start.16 = (bf16[2,144,128]{2,1,0:T(8,128)(2,1)S(1)}, bf16[2,144,128]{2,1,0:T(8,128)(2,1)S(1)}, u32[]{:S(2)}, u32[]{:S(2)}) collective-permute-start(bf16[2,144,128]{2,1,0:T(8,128)(2,1)S(1)} %pad_maximum_fusion.8.refs_5_), channel_id=1, source_target_pairs={{0,12},{2,14},{4,8},{6,10},{8,4},{10,6},{12,0},{14,2},{16,28},{18,... | collective-permute-start | bytes 221192 | tf_op jit(solution)/shard_map/ppermute | solution.py:517
  67.4 5.3 %collective-permute-start.17 = (bf16[64,384]{1,0:T(8,128)(2,1)S(1)}, bf16[64,384]{1,0:T(8,128)(2,1)S(1)}, u32[]{:S(2)}, u32[]{:S(2)}) collective-permute-start(bf16[64,384]{1,0:T(8,128)(2,1)S(1)} %kept_attended.1.refs_1_), channel_id=1, source_target_pairs={{0,1},{1,0},{2,3},{3,2},{4,5},{5,4},{6,7},{7,6},{8,9},{9,8},{10,11... | collective-permute-start | bytes 147464 | tf_op jit(solution)/shard_map/ppermute | solution.py:513

commit v3 on v2

--- a/solution.py
+++ b/solution.py
@@ -524,8 +524,8 @@
 def octet_exchange(near, far):
     crossed = flip(far, 1)
     blocks = [jnp.stack([near[chip], crossed[chip]]) for chip in range(4)]
-    arrived = [flip(blocks[chip], 2 * chip) for chip in (1, 2, 3)]
-    return jnp.concatenate([blocks[0]] + arrived), blocks[3], arrived[0]
+    arrived = {chip: flip(blocks[chip], 2 * chip) for chip in (3, 2, 1)}
+    return jnp.concatenate([blocks[0]] + [arrived[chip] for chip in (1, 2, 3)]), blocks[3], arrived[3]
 
 
 def body(queries, keys, values, weight_out, cotangent):
@@ -572,7 +572,7 @@
     sent2, stat1, out1 = call(
         level_one, [later_block, stat, ((64, ROWS), F32)], (block1,), flops=100000000
     )
-    block2 = gather_pair(sent2, 14, 16)
+    block2 = gather_pair(sent2, 16, 14)
     dq1, dkv1 = call(level_one_back, [((64, ROWS), F32), ((ROWS, 128), F32)], (block1, stat1), flops=100000000)
     early = list(backward(0, sent2))
     sent3, stat2, out2 = call(

time: 74.3 us -> 72.4 us (0.974)
  waiting for transfers between devices: 15.4 us -> 14.4 us
  starting transfers between devices: 29.3 us -> 28.4 us
    ppermute x14, waiting for transfers between devices: 14.2 us -> 13.2 us  [flip(): lax.ppermute(array, 'seq', [(i, i ^ mask) for i in range(lax.axis_size('s...]
    ppermute x14, starting transfers between devices: 24 us -> 23.2 us  [flip(): lax.ppermute(array, 'seq', [(i, i ^ mask) for i in range(lax.axis_size('s...]
  transfers between devices with their start and end apart: 18 -> 18, of which waited for: 8 -> 9; matrix products, arithmetic and copies ran while one was open for 2% -> 2% of each run, Pallas kernels for 27% -> 28%
where the time goes in v3:
time: 72.4 us; the launch traced here: 72.3 us
  starting transfers between devices  28.4 us (39%)
  Pallas kernels  26.6 us (37%)
  waiting for transfers between devices  14.4 us (20%)
  other arithmetic  1.6 us (2%)
  between operations  1.07 us (1%)
    pallas_call x17, Pallas kernels, call(): pl.pallas_call(run, out_shape=shapes, in_specs=[pl.BlockSpec(memory_space...  26.6 us
    ppermute x14, starting transfers between devices, flip(): lax.ppermute(array, 'seq', [(i, i ^ mask) for i in range(lax.axis_size('s...  23.2 us
    ppermute x14, waiting for transfers between devices, flip(): lax.ppermute(array, 'seq', [(i, i ^ mask) for i in range(lax.axis_size('s...  13.2 us
    ppermute x4, starting transfers between devices, partner(): return lax.ppermute(array, 'head', [(0, 1), (1, 0)])  5.21 us
  transfers between devices with their start and end apart: 18, of which 9 were waited for; matrix products, arithmetic and copies ran while one was open for 2% of the time, Pallas kernels for 28%

profile of v3, /device:TPU:2, one launch (start us, length us, event | category | flops | bytes accessed | tf_op | source)
XLA Modules:
  0.0 72.3 jit_solution(9123243988427637422)
XLA Ops:
  0.6 2.4 %collective-permute-start = (bf16[512,384]{1,0:T(8,128)(2,1)}, bf16[512,384]{1,0:T(8,128)(2,1)S(1)}, u32[]{:S(2)}, u32[]{:S(2)}) collective-permute-start(bf16[512,384]{1,0:T(8,128)(2,1)} %refs_2_.1), channel_id=1, source_target_pairs={{0,1},{1,0},{2,3},{3,2},{4,5},{5,4},{6,7},{7,6},{8,9},{9,8},{10,11... | collective-permute-start | bytes 1179656 | tf_op jit(solution)/shard_map/ppermute | solution.py:513
  3.0 0.1 pad_add_fusion.refs_0_
  3.1 1.4 %pad_maximum_fusion.refs_1_.refs_0_ = bf16[3,512,384]{2,1,0:T(8,128)(2,1)S(1)} fusion(bf16[1,512,384]{2,1,0:T(8,128)(2,1)} %bitcast.15, bf16[1,512,384]{2,1,0:T(8,128)(2,1)} %bitcast.16, bf16[1,512,384]{2,1,0:T(8,128)(2,1)} %bitcast.17), kind=kLoop, calls=%fused_computation | loop fusion | flops 1179648 | bytes 2359296 | tf_op jit(solution)/shard_map/stack | solution.py:542
  4.5 1.1 %pack_data.1 = (bf16[6,128,128]{2,1,0:T(8,128)(2,1)S(1)}, bf16[384,512]{1,0:T(8,128)(2,1)S(1)}) custom-call(s32[2]{0:T(128)S(1)} %pad_add_fusion.refs_0_, bf16[3,512,384]{2,1,0:T(8,128)(2,1)S(1)} %pad_maximum_fusion.refs_1_.refs_0_), custom_call_target="tpu_custom_call" | custom-call | flops 200000000 | bytes 1769472 | tf_op jit(solution)/shard_map/pack_data/pallas_call | solution.py:498
  5.6 0.0 copy-start
  5.6 0.0 copy-start.1
  5.6 0.9 %kept_forward.1 = (f32[64,384]{1,0:T(8,128)S(1)}, f32[8,64]{1,0:T(8,128)S(1)}) custom-call(bf16[3,512,384]{2,1,0:T(8,128)(2,1)S(1)} %pad_maximum_fusion.refs_1_.refs_0_, bf16[6,128,128]{2,1,0:T(8,128)(2,1)S(1)} %get-tuple-element.46.refs_1_.refs_2_), custom_call_target="tpu_custom_call" | custom-call | flops 100000000 | bytes 1476608 | tf_op jit(solution)/shard_map/kept_forward/pallas_call | solution.py:498
  6.5 4.0 %local_forward.1 = (f32[384,512]{1,0:T(8,128)S(1)}, f32[8,512]{1,0:T(8,128)S(1)}, bf16[384,512]{1,0:T(8,128)(2,1)S(1)}) custom-call(s32[2]{0:T(128)S(1)} %pad_add_fusion.refs_0_, bf16[3,512,384]{2,1,0:T(8,128)(2,1)S(1)} %pad_maximum_fusion.refs_1_.refs_0_), custom_call_target="tpu_custom_call" | custom-call | flops 400000000 | bytes 2375680 | tf_op jit(solution)/shard_map/local_forward/pallas_call | solution.py:498
  10.6 1.2 %collective-permute-done.refs_3_ = bf16[512,384]{1,0:T(8,128)(2,1)S(1)} collective-permute-done((bf16[512,384]{1,0:T(8,128)(2,1)}, bf16[512,384]{1,0:T(8,128)(2,1)S(1)}, u32[]{:S(2)}, u32[]{:S(2)}) %collective-permute-start) | collective-permute-done | bytes 393248 | tf_op jit(solution)/shard_map/ppermute | solution.py:513
  11.8 0.0 copy-done
  11.8 0.0 copy-done.1
  11.8 1.8 %pack_grads.1 = (bf16[512,384]{1,0:T(8,128)(2,1)S(1)}, bf16[64,384]{1,0:T(8,128)(2,1)S(1)}, bf16[4,144,128]{2,1,0:T(8,128)(2,1)S(1)}, bf16[4,144,128]{2,1,0:T(8,128)(2,1)S(1)}) custom-call(s32[2]{0:T(128)S(1)} %pad_add_fusion.refs_0_, bf16[6,128,128]{2,1,0:T(8,128)(2,1)S(1)} %get-tuple-element.46.refs_1_.refs_2_, bf16[512,384]{1,0:T(8,128)(2,1)S(1)} %copy-done.1, ...), custom_call_target="tpu_custom_call" | custom-call | flops 400000000 | bytes 2803712 | tf_op jit(solution)/shard_map/pack_grads/pallas_call | solution.py:498
  13.6 0.1 collective-permute-start.1
  13.7 0.1 constant_dynamic-slice_fusion
  13.8 0.4 collective-permute-start.4
  14.2 0.9 %collective-permute-done.1 = bf16[4,144,128]{2,1,0:T(8,128)(2,1)S(1)} collective-permute-done((bf16[4,144,128]{2,1,0:T(8,128)(2,1)S(1)}, bf16[4,144,128]{2,1,0:T(8,128)(2,1)S(1)}, u32[]{:S(2)}, u32[]{:S(2)}) %collective-permute-start.1) | collective-permute-done | bytes 147488 | tf_op jit(solution)/shard_map/ppermute | solution.py:517
  15.1 4.7 %collective-permute-start.2 = (bf16[2,144,128]{2,1,0:T(8,128)(2,1)S(1)}, bf16[2,144,128]{2,1,0:T(8,128)(2,1)S(1)}, u32[]{:S(2)}, u32[]{:S(2)}) collective-permute-start(bf16[2,144,128]{2,1,0:T(8,128)(2,1)S(1)} %pad_maximum_fusion.3), channel_id=1, source_target_pairs={{0,12},{2,14},{4,8},{6,10},{8,4},{10,6},{12,0},{14,2},{16,28},{18,... | collective-permute-start | bytes 221192 | tf_op jit(solution)/shard_map/ppermute | solution.py:517
  19.8 0.1 collective-permute-start.5
  19.9 0.6 collective-permute-start.6
  20.6 2.3 %collective-permute-done.2 = bf16[2,144,128]{2,1,0:T(8,128)(2,1)S(1)} collective-permute-done((bf16[2,144,128]{2,1,0:T(8,128)(2,1)S(1)}, bf16[2,144,128]{2,1,0:T(8,128)(2,1)S(1)}, u32[]{:S(2)}, u32[]{:S(2)}) %collective-permute-start.2) | collective-permute-done | bytes 73760 | tf_op jit(solution)/shard_map/ppermute | solution.py:517
  22.9 0.9 %collective-permute-start.3 = (bf16[384,512]{1,0:T(8,128)(2,1)S(1)}, bf16[384,512]{1,0:T(8,128)(2,1)S(1)}, u32[]{:S(2)}, u32[]{:S(2)}) collective-permute-start(bf16[384,512]{1,0:T(8,128)(2,1)S(1)} %get-tuple-element.52.refs_8_.refs_1_), channel_id=1, source_target_pairs={{0,1},{1,0},{2,3},{3,2},{4,5},{5,4},{6,7},{7,6},{8,9},{9,8},{10,11... | collective-permute-start | bytes 1179656 | tf_op jit(solution)/shard_map/ppermute | solution.py:513
  23.8 1.4 %collective-permute-done.5 = bf16[2,144,128]{2,1,0:T(8,128)(2,1)S(1)} collective-permute-done((bf16[2,144,128]{2,1,0:T(8,128)(2,1)S(1)}, bf16[2,144,128]{2,1,0:T(8,128)(2,1)S(1)}, u32[]{:S(2)}, u32[]{:S(2)}) %collective-permute-start.5) | collective-permute-done | bytes 73760 | tf_op jit(solution)/shard_map/ppermute | solution.py:517
  25.2 1.7 %collective-permute-done.6 = bf16[2,144,128]{2,1,0:T(8,128)(2,1)S(1)} collective-permute-done((bf16[2,144,128]{2,1,0:T(8,128)(2,1)S(1)}, bf16[2,144,128]{2,1,0:T(8,128)(2,1)S(1)}, u32[]{:S(2)}, u32[]{:S(2)}) %collective-permute-start.6) | collective-permute-done | bytes 73760 | tf_op jit(solution)/shard_map/ppermute | solution.py:517
  26.9 0.8 %level_one.1 = (bf16[272,128]{1,0:T(8,128)(2,1)S(1)}, f32[8,512]{1,0:T(8,128)S(1)}, f32[64,512]{1,0:T(8,128)S(1)}) custom-call(bf16[8,144,128]{2,1,0:T(8,128)(2,1)S(1)} %constant_dynamic-update-slice_fusion.refs_0_), custom_call_target="tpu_custom_call" | custom-call | flops 100000000 | bytes 512000 | tf_op jit(solution)/shard_map/level_one/pallas_call | solution.py:498
  27.7 4.8 %collective-permute-start.9 = (bf16[272,128]{1,0:T(8,128)(2,1)S(1)}, bf16[272,128]{1,0:T(8,128)(2,1)S(1)}, u32[]{:S(2)}, u32[]{:S(2)}) collective-permute-start(bf16[272,128]{1,0:T(8,128)(2,1)S(1)} %get-tuple-element.55.refs_5_), channel_id=1, source_target_pairs={{0,60},{2,62},{4,56},{6,58},{8,52},{10,54},{12,48},{14,50},{16,44}... | collective-permute-start | bytes 208904 | tf_op jit(solution)/shard_map/ppermute | solution.py:517
  32.5 0.0 collective-permute-start.8
  32.5 0.7 collective-permute-start.7
  33.1 1.0 %level_one_back.1 = (f32[64,512]{1,0:T(8,128)S(1)}, f32[512,128]{1,0:T(8,128)S(1)}) custom-call(bf16[8,144,128]{2,1,0:T(8,128)(2,1)S(1)} %constant_dynamic-update-slice_fusion.refs_0_, f32[8,512]{1,0:T(8,128)S(1)} %get-tuple-element.56.refs_1_.refs_3_), custom_call_target="tpu_custom_call" | custom-call | flops 100000000 | bytes 704512 | tf_op jit(solution)/shard_map/level_one_back/pallas_call | solution.py:498
  34.2 2.1 %local_backward.3 = (f32[512,128]{1,0:T(8,128)S(1)}, f32[512,128]{1,0:T(8,128)S(1)}, f32[512,128]{1,0:T(8,128)S(1)}) custom-call(s32[2]{0:T(128)S(1)} %pad_add_fusion.refs_0_, bf16[3,512,384]{2,1,0:T(8,128)(2,1)S(1)} %pad_maximum_fusion.refs_1_.refs_0_, bf16[512,384]{1,0:T(8,128)(2,1)S(1)} %get-tuple-element.58.refs_2_, ...), custom_call_target="tpu_custom_call" | custom-call | flops 300000000 | bytes 3162112 | tf_op jit(solution)/shard_map/local_backward/pallas_call | solution.py:498
  36.3 0.5 collective-permute-done.9
  36.7 1.3 %collective-permute-done.8 = bf16[272,128]{1,0:T(8,128)(2,1)S(1)} collective-permute-done((bf16[272,128]{1,0:T(8,128)(2,1)S(1)}, bf16[272,128]{1,0:T(8,128)(2,1)S(1)}, u32[]{:S(2)}, u32[]{:S(2)}) %collective-permute-start.8) | collective-permute-done | bytes 69664 | tf_op jit(solution)/shard_map/ppermute | solution.py:517
  38.1 0.0 collective-permute-done.7
  38.1 0.0 collective-permute-done.4.refs_4_.refs_2_.refs_3_
  38.1 0.0 collective-permute-done.3.refs_2_.refs_1_
  38.1 0.9 %level_two.1 = (bf16[272,128]{1,0:T(8,128)(2,1)S(1)}, f32[8,512]{1,0:T(8,128)S(1)}, f32[64,128]{1,0:T(8,128)S(1)}) custom-call(bf16[4,272,128]{2,1,0:T(8,128)(2,1)S(1)} %pad_maximum_fusion.1.refs_0_.refs_1_, bf16[384,512]{1,0:T(8,128)(2,1)S(1)} %collective-permute-done.3.refs_2_.refs_1_, bf16[384,384]{1,0:T(8,128)(2,1)S(1)} %collective-permute-done.4.refs_4_.refs_2_.refs_3_, ...), custom_call_target="tpu_custom_call" | custom-call | flops 100000000 | bytes 397312 | tf_op jit(solution)/shard_map/level_two/pallas_call | solution.py:498
  39.0 3.8 %collective-permute-start.12 = (bf16[272,128]{1,0:T(8,128)(2,1)S(1)}, bf16[272,128]{1,0:T(8,128)(2,1)S(1)}, u32[]{:S(2)}, u32[]{:S(2)}) collective-permute-start(bf16[272,128]{1,0:T(8,128)(2,1)S(1)} %get-tuple-element.62.refs_5_), channel_id=1, source_target_pairs={{0,224},{2,226},{4,228},{6,230},{8,232},{10,234},{12,236},{14,238}... | collective-permute-start | bytes 208904 | tf_op jit(solution)/shard_map/ppermute | solution.py:517
  42.8 1.1 %collective-permute-start.11 = (bf16[272,128]{1,0:T(8,128)(2,1)S(1)}, bf16[272,128]{1,0:T(8,128)(2,1)S(1)}, u32[]{:S(2)}, u32[]{:S(2)}) collective-permute-start(bf16[272,128]{1,0:T(8,128)(2,1)S(1)} %get-tuple-element.62.refs_5_), channel_id=1, source_target_pairs={{0,96},{2,98},{4,100},{6,102},{8,104},{10,106},{12,108},{14,110},{... | collective-permute-start | bytes 208904 | tf_op jit(solution)/shard_map/ppermute | solution.py:517
  43.9 1.4 %collective-permute-start.10 = (bf16[272,128]{1,0:T(8,128)(2,1)S(1)}, bf16[272,128]{1,0:T(8,128)(2,1)S(1)}, u32[]{:S(2)}, u32[]{:S(2)}) collective-permute-start(bf16[272,128]{1,0:T(8,128)(2,1)S(1)} %get-tuple-element.62.refs_5_), channel_id=1, source_target_pairs={{0,128},{2,130},{4,132},{6,134},{8,136},{10,138},{12,140},{14,142}... | collective-permute-start | bytes 208904 | tf_op jit(solution)/shard_map/ppermute | solution.py:517
  45.3 0.9 %level_two_back.1 = (f32[512,128]{1,0:T(8,128)S(1)}, f32[128,128]{1,0:T(8,128)S(1)}, f32[64,128]{1,0:T(8,128)S(1)}) custom-call(bf16[8,144,128]{2,1,0:T(8,128)(2,1)S(1)} %constant_dynamic-update-slice_fusion.refs_0_, bf16[4,272,128]{2,1,0:T(8,128)(2,1)S(1)} %pad_maximum_fusion.1.refs_0_.refs_1_, f32[8,512]{1,0:T(8,128)S(1)} %get-tuple-element.63.refs_2_.refs_4_, ...), custom_call_target="tpu_custom_call" | custom-call | flops 100000000 | bytes 1212416 | tf_op jit(solution)/shard_map/level_two_back/pallas_call | solution.py:498
  46.1 2.1 %local_backward.4 = (f32[512,128]{1,0:T(8,128)S(1)}, f32[512,128]{1,0:T(8,128)S(1)}, f32[512,128]{1,0:T(8,128)S(1)}) custom-call(s32[2]{0:T(128)S(1)} %pad_add_fusion.refs_0_, bf16[3,512,384]{2,1,0:T(8,128)(2,1)S(1)} %pad_maximum_fusion.refs_1_.refs_0_, bf16[512,384]{1,0:T(8,128)(2,1)S(1)} %get-tuple-element.58.refs_2_, ...), custom_call_target="tpu_custom_call" | custom-call | flops 300000000 | bytes 3162112 | tf_op jit(solution)/shard_map/local_backward/pallas_call | solution.py:498
  48.2 1.4 %mix_base.1 = (f32[512,384]{1,0:T(8,128)S(1)}, bf16[512,384]{1,0:T(8,128)(2,1)S(1)}, bf16[512,384]{1,0:T(8,128)(2,1)S(1)}) custom-call(s32[2]{0:T(128)S(1)} %pad_add_fusion.refs_0_, bf16[384,512]{1,0:T(8,128)(2,1)S(1)} %get-tuple-element.52.refs_8_.refs_1_, bf16[384,512]{1,0:T(8,128)(2,1)S(1)} %collective-permute-done.3.refs_2_.refs_1_, ...), custom_call_target="tpu_custom_call" | custom-call | flops 300000000 | bytes 2949120 | tf_op jit(solution)/shard_map/mix_base/pallas_call | solution.py:498
  49.6 0.0 collective-permute-done.12
  49.7 0.0 collective-permute-done.11
  49.7 0.0 collective-permute-done.10
  49.7 1.7 %level_three.1 = (bf16[4,144,128]{2,1,0:T(8,128)(2,1)S(1)}, bf16[4,144,128]{2,1,0:T(8,128)(2,1)S(1)}) custom-call(bf16[8,144,128]{2,1,0:T(8,128)(2,1)S(1)} %constant_dynamic-update-slice_fusion.refs_0_, bf16[4,272,128]{2,1,0:T(8,128)(2,1)S(1)} %pad_maximum_fusion.1.refs_0_.refs_1_, bf16[4,272,128]{2,1,0:T(8,128)(2,1)S(1)} %pad_maximum_fusion.2.refs_2_, ...), custom_call_target="tpu_custom_call" | custom-call | flops 300000000 | bytes 1835008 | tf_op jit(solution)/shard_map/level_three/pallas_call | solution.py:498
  51.4 0.1 collective-permute-start.13
  51.6 1.3 %collective-permute-done.13 = bf16[4,144,128]{2,1,0:T(8,128)(2,1)S(1)} collective-permute-done((bf16[4,144,128]{2,1,0:T(8,128)(2,1)S(1)}, bf16[4,144,128]{2,1,0:T(8,128)(2,1)S(1)}, u32[]{:S(2)}, u32[]{:S(2)}) %collective-permute-start.13) | collective-permute-done | bytes 147488 | tf_op jit(solution)/shard_map/ppermute | solution.py:517
  52.9 3.0 %collective-permute-start.14 = (bf16[2,144,128]{2,1,0:T(8,128)(2,1)S(1)}, bf16[2,144,128]{2,1,0:T(8,128)(2,1)S(1)}, u32[]{:S(2)}, u32[]{:S(2)}) collective-permute-start(bf16[2,144,128]{2,1,0:T(8,128)(2,1)S(1)} %pad_maximum_fusion.6), channel_id=1, source_target_pairs={{0,4},{2,6},{4,0},{6,2},{8,12},{10,14},{12,8},{14,10},{16,20},{18,... | collective-permute-start | bytes 221192 | tf_op jit(solution)/shard_map/ppermute | solution.py:517
  56.0 0.5 collective-permute-start.15
  56.5 2.2 %collective-permute-start.16 = (bf16[2,144,128]{2,1,0:T(8,128)(2,1)S(1)}, bf16[2,144,128]{2,1,0:T(8,128)(2,1)S(1)}, u32[]{:S(2)}, u32[]{:S(2)}) collective-permute-start(bf16[2,144,128]{2,1,0:T(8,128)(2,1)S(1)} %pad_maximum_fusion.8.refs_5_), channel_id=1, source_target_pairs={{0,12},{2,14},{4,8},{6,10},{8,4},{10,6},{12,0},{14,2},{16,28},{18,... | collective-permute-start | bytes 221192 | tf_op jit(solution)/shard_map/ppermute | solution.py:517
  58.8 2.1 %local_backward.5 = (f32[512,128]{1,0:T(8,128)S(1)}, f32[512,128]{1,0:T(8,128)S(1)}, f32[512,128]{1,0:T(8,128)S(1)}) custom-call(s32[2]{0:T(128)S(1)} %pad_add_fusion.refs_0_, bf16[3,512,384]{2,1,0:T(8,128)(2,1)S(1)} %pad_maximum_fusion.refs_1_.refs_0_, bf16[512,384]{1,0:T(8,128)(2,1)S(1)} %get-tuple-element.58.refs_2_, ...), custom_call_target="tpu_custom_call" | custom-call | flops 300000000 | bytes 3162112 | tf_op jit(solution)/shard_map/local_backward/pallas_call | solution.py:498
  60.9 0.0 collective-permute-done.14
  60.9 3.8 %collective-permute-done.15 = bf16[2,144,128]{2,1,0:T(8,128)(2,1)S(1)} collective-permute-done((bf16[2,144,128]{2,1,0:T(8,128)(2,1)S(1)}, bf16[2,144,128]{2,1,0:T(8,128)(2,1)S(1)}, u32[]{:S(2)}, u32[]{:S(2)}) %collective-permute-start.15) | collective-permute-done | bytes 73760 | tf_op jit(solution)/shard_map/ppermute | solution.py:517
  64.7 0.0 collective-permute-done.16
  64.7 0.7 %kept_attended.1.refs_1_ = bf16[64,384]{1,0:T(8,128)(2,1)S(1)} custom-call(s32[2]{0:T(128)S(1)} %pad_add_fusion.refs_0_, bf16[8,144,128]{2,1,0:T(8,128)(2,1)S(1)} %constant_dynamic-update-slice_fusion.3.refs_1_.refs_4_, f32[64,384]{1,0:T(8,128)S(1)} %get-tuple-element.48.refs_6_.refs_2_, f32[8,64]{1,0:T(8,128)S(1)} %get-tuple-element.49.refs_7_.refs_3_, ...), custom_call_target="tpu_custom_call" | custom-call | flops 10000000 | bytes 444416 | tf_op jit(solution)/shard_map/kept_attended/pallas_call | solution.py:498
  65.5 1.6 %collective-permute-start.17 = (bf16[64,384]{1,0:T(8,128)(2,1)S(1)}, bf16[64,384]{1,0:T(8,128)(2,1)S(1)}, u32[]{:S(2)}, u32[]{:S(2)}) collective-permute-start(bf16[64,384]{1,0:T(8,128)(2,1)S(1)} %kept_attended.1.refs_1_), channel_id=1, source_target_pairs={{0,1},{1,0},{2,3},{3,2},{4,5},{5,4},{6,7},{7,6},{8,9},{9,8},{10,11... | collective-permute-start | bytes 147464 | tf_op jit(solution)/shard_map/ppermute | solution.py:513
  67.1 0.5 mix_own.1.refs_0_
  67.6 3.2 %final_grads.1 = (bf16[512,384]{1,0:T(8,128)(2,1)}, bf16[512,384]{1,0:T(8,128)(2,1)}, bf16[512,384]{1,0:T(8,128)(2,1)}) custom-call(s32[2]{0:T(128)S(1)} %pad_add_fusion.refs_0_, bf16[3,512,384]{2,1,0:T(8,128)(2,1)S(1)} %pad_maximum_fusion.refs_1_.refs_0_, bf16[6,128,128]{2,1,0:T(8,128)(2,1)S(1)} %get-tuple-element.46.refs_1_.refs_2_, ...), custom_call_target="tpu_custom_call" | custom-call | flops 200000000 | bytes 5652480 | tf_op jit(solution)/shard_map/final_grads/pallas_call | solution.py:498
  70.8 0.0 collective-permute-done.17.refs_1_
  70.8 1.3 %mix_other.1 = bf16[512,384]{1,0:T(8,128)(2,1)} custom-call(f32[512,384]{1,0:T(8,128)S(1)} %mix_own.1.refs_0_, bf16[64,384]{1,0:T(8,128)(2,1)S(1)} %collective-permute-done.17.refs_1_, bf16[512,384]{1,0:T(8,128)(2,1)S(1)} %get-tuple-element.75.refs_2_, bf16[384,384]{1,0:T(8,128)(2,1)S(1)} %collective-permute-done.4.refs_4_.refs_2_.refs_3_), custom_call_target="tpu_custom_call" | custom-call | flops 200000000 | bytes 1916928 | tf_op jit(solution)/shard_map/mix_other/pallas_call | solution.py:498
  (18 shorter events, 0.3 us)
Async XLA Ops:
  0.6 11.2 %collective-permute-start = (bf16[512,384]{1,0:T(8,128)(2,1)}, bf16[512,384]{1,0:T(8,128)(2,1)S(1)}, u32[]{:S(2)}, u32[]{:S(2)}) collective-permute-start(bf16[512,384]{1,0:T(8,128)(2,1)} %refs_2_.1), channel_id=1, source_target_pairs={{0,1},{1,0},{2,3},{3,2},{4,5},{5,4},{6,7},{7,6},{8,9},{9,8},{10,11... | collective-permute-start | bytes 1179656 | tf_op jit(solution)/shard_map/ppermute | solution.py:513
  5.6 6.2 %copy-start = (bf16[384,768]{1,0:T(8,128)(2,1)S(1)}, bf16[384,768]{1,0:T(8,128)(2,1)}, u32[]{:S(2)}) copy-start(bf16[384,768]{1,0:T(8,128)(2,1)} %refs_4_.1) | copy-start | bytes 1769476
  5.6 6.2 %copy-start.1 = (bf16[512,384]{1,0:T(8,128)(2,1)S(1)}, bf16[512,384]{1,0:T(8,128)(2,1)}, u32[]{:S(2)}) copy-start(bf16[512,384]{1,0:T(8,128)(2,1)} %refs_2_.1) | copy-start | bytes 1179652
  13.6 1.5 %collective-permute-start.1 = (bf16[4,144,128]{2,1,0:T(8,128)(2,1)S(1)}, bf16[4,144,128]{2,1,0:T(8,128)(2,1)S(1)}, u32[]{:S(2)}, u32[]{:S(2)}) collective-permute-start(bf16[4,144,128]{2,1,0:T(8,128)(2,1)S(1)} %get-tuple-element.51), channel_id=1, source_target_pairs={{0,2},{2,0},{4,6},{6,4},{8,10},{10,8},{12,14},{14,12},{16,18},{18,... | collective-permute-start | bytes 442376 | tf_op jit(solution)/shard_map/ppermute | solution.py:517
  13.8 24.3 %collective-permute-start.4 = (bf16[384,384]{1,0:T(8,128)(2,1)S(1)}, bf16[384,384]{1,0:T(8,128)(2,1)S(1)}, u32[]{:S(2)}, u32[]{:S(2)}) collective-permute-start(bf16[384,384]{1,0:T(8,128)(2,1)S(1)} %get-tuple-element.86), channel_id=1, source_target_pairs={{0,1},{1,0},{2,3},{3,2},{4,5},{5,4},{6,7},{7,6},{8,9},{9,8},{10,11... | collective-permute-start | bytes 884744 | tf_op jit(solution)/shard_map/ppermute | solution.py:513
  15.1 7.8 %collective-permute-start.2 = (bf16[2,144,128]{2,1,0:T(8,128)(2,1)S(1)}, bf16[2,144,128]{2,1,0:T(8,128)(2,1)S(1)}, u32[]{:S(2)}, u32[]{:S(2)}) collective-permute-start(bf16[2,144,128]{2,1,0:T(8,128)(2,1)S(1)} %pad_maximum_fusion.3), channel_id=1, source_target_pairs={{0,12},{2,14},{4,8},{6,10},{8,4},{10,6},{12,0},{14,2},{16,28},{18,... | collective-permute-start | bytes 221192 | tf_op jit(solution)/shard_map/ppermute | solution.py:517
  19.8 5.3 %collective-permute-start.5 = (bf16[2,144,128]{2,1,0:T(8,128)(2,1)S(1)}, bf16[2,144,128]{2,1,0:T(8,128)(2,1)S(1)}, u32[]{:S(2)}, u32[]{:S(2)}) collective-permute-start(bf16[2,144,128]{2,1,0:T(8,128)(2,1)S(1)} %pad_maximum_fusion.4), channel_id=1, source_target_pairs={{0,4},{2,6},{4,0},{6,2},{8,12},{10,14},{12,8},{14,10},{16,20},{18,... | collective-permute-start | bytes 221192 | tf_op jit(solution)/shard_map/ppermute | solution.py:517
  19.9 6.9 %collective-permute-start.6 = (bf16[2,144,128]{2,1,0:T(8,128)(2,1)S(1)}, bf16[2,144,128]{2,1,0:T(8,128)(2,1)S(1)}, u32[]{:S(2)}, u32[]{:S(2)}) collective-permute-start(bf16[2,144,128]{2,1,0:T(8,128)(2,1)S(1)} %pad_maximum_fusion.5), channel_id=1, source_target_pairs={{0,8},{2,10},{4,12},{6,14},{8,0},{10,2},{12,4},{14,6},{16,24},{18,... | collective-permute-start | bytes 221192 | tf_op jit(solution)/shard_map/ppermute | solution.py:517
  22.9 15.2 %collective-permute-start.3 = (bf16[384,512]{1,0:T(8,128)(2,1)S(1)}, bf16[384,512]{1,0:T(8,128)(2,1)S(1)}, u32[]{:S(2)}, u32[]{:S(2)}) collective-permute-start(bf16[384,512]{1,0:T(8,128)(2,1)S(1)} %get-tuple-element.52.refs_8_.refs_1_), channel_id=1, source_target_pairs={{0,1},{1,0},{2,3},{3,2},{4,5},{5,4},{6,7},{7,6},{8,9},{9,8},{10,11... | collective-permute-start | bytes 1179656 | tf_op jit(solution)/shard_map/ppermute | solution.py:513
  27.7 9.0 %collective-permute-start.9 = (bf16[272,128]{1,0:T(8,128)(2,1)S(1)}, bf16[272,128]{1,0:T(8,128)(2,1)S(1)}, u32[]{:S(2)}, u32[]{:S(2)}) collective-permute-start(bf16[272,128]{1,0:T(8,128)(2,1)S(1)} %get-tuple-element.55.refs_5_), channel_id=1, source_target_pairs={{0,60},{2,62},{4,56},{6,58},{8,52},{10,54},{12,48},{14,50},{16,44}... | collective-permute-start | bytes 208904 | tf_op jit(solution)/shard_map/ppermute | solution.py:517
  32.5 5.6 %collective-permute-start.8 = (bf16[272,128]{1,0:T(8,128)(2,1)S(1)}, bf16[272,128]{1,0:T(8,128)(2,1)S(1)}, u32[]{:S(2)}, u32[]{:S(2)}) collective-permute-start(bf16[272,128]{1,0:T(8,128)(2,1)S(1)} %get-tuple-element.55.refs_5_), channel_id=1, source_target_pairs={{0,28},{2,30},{4,24},{6,26},{8,20},{10,22},{12,16},{14,18},{16,12}... | collective-permute-start | bytes 208904 | tf_op jit(solution)/shard_map/ppermute | solution.py:517
  32.5 5.6 %collective-permute-start.7 = (bf16[272,128]{1,0:T(8,128)(2,1)S(1)}, bf16[272,128]{1,0:T(8,128)(2,1)S(1)}, u32[]{:S(2)}, u32[]{:S(2)}) collective-permute-start(bf16[272,128]{1,0:T(8,128)(2,1)S(1)} %get-tuple-element.55.refs_5_), channel_id=1, source_target_pairs={{0,32},{2,34},{4,36},{6,38},{8,40},{10,42},{12,44},{14,46},{16,48}... | collective-permute-start | bytes 208904 | tf_op jit(solution)/shard_map/ppermute | solution.py:517
  39.0 10.7 %collective-permute-start.12 = (bf16[272,128]{1,0:T(8,128)(2,1)S(1)}, bf16[272,128]{1,0:T(8,128)(2,1)S(1)}, u32[]{:S(2)}, u32[]{:S(2)}) collective-permute-start(bf16[272,128]{1,0:T(8,128)(2,1)S(1)} %get-tuple-element.62.refs_5_), channel_id=1, source_target_pairs={{0,224},{2,226},{4,228},{6,230},{8,232},{10,234},{12,236},{14,238}... | collective-permute-start | bytes 208904 | tf_op jit(solution)/shard_map/ppermute | solution.py:517
  42.8 6.9 %collective-permute-start.11 = (bf16[272,128]{1,0:T(8,128)(2,1)S(1)}, bf16[272,128]{1,0:T(8,128)(2,1)S(1)}, u32[]{:S(2)}, u32[]{:S(2)}) collective-permute-start(bf16[272,128]{1,0:T(8,128)(2,1)S(1)} %get-tuple-element.62.refs_5_), channel_id=1, source_target_pairs={{0,96},{2,98},{4,100},{6,102},{8,104},{10,106},{12,108},{14,110},{... | collective-permute-start | bytes 208904 | tf_op jit(solution)/shard_map/ppermute | solution.py:517
  43.9 5.8 %collective-permute-start.10 = (bf16[272,128]{1,0:T(8,128)(2,1)S(1)}, bf16[272,128]{1,0:T(8,128)(2,1)S(1)}, u32[]{:S(2)}, u32[]{:S(2)}) collective-permute-start(bf16[272,128]{1,0:T(8,128)(2,1)S(1)} %get-tuple-element.62.refs_5_), channel_id=1, source_target_pairs={{0,128},{2,130},{4,132},{6,134},{8,136},{10,138},{12,140},{14,142}... | collective-permute-start | bytes 208904 | tf_op jit(solution)/shard_map/ppermute | solution.py:517
  51.4 1.5 %collective-permute-start.13 = (bf16[4,144,128]{2,1,0:T(8,128)(2,1)S(1)}, bf16[4,144,128]{2,1,0:T(8,128)(2,1)S(1)}, u32[]{:S(2)}, u32[]{:S(2)}) collective-permute-start(bf16[4,144,128]{2,1,0:T(8,128)(2,1)S(1)} %get-tuple-element.72), channel_id=1, source_target_pairs={{0,2},{2,0},{4,6},{6,4},{8,10},{10,8},{12,14},{14,12},{16,18},{18,... | collective-permute-start | bytes 442376 | tf_op jit(solution)/shard_map/ppermute | solution.py:517
  52.9 7.9 %collective-permute-start.14 = (bf16[2,144,128]{2,1,0:T(8,128)(2,1)S(1)}, bf16[2,144,128]{2,1,0:T(8,128)(2,1)S(1)}, u32[]{:S(2)}, u32[]{:S(2)}) collective-permute-start(bf16[2,144,128]{2,1,0:T(8,128)(2,1)S(1)} %pad_maximum_fusion.6), channel_id=1, source_target_pairs={{0,4},{2,6},{4,0},{6,2},{8,12},{10,14},{12,8},{14,10},{16,20},{18,... | collective-permute-start | bytes 221192 | tf_op jit(solution)/shard_map/ppermute | solution.py:517
  56.0 8.7 %collective-permute-start.15 = (bf16[2,144,128]{2,1,0:T(8,128)(2,1)S(1)}, bf16[2,144,128]{2,1,0:T(8,128)(2,1)S(1)}, u32[]{:S(2)}, u32[]{:S(2)}) collective-permute-start(bf16[2,144,128]{2,1,0:T(8,128)(2,1)S(1)} %pad_maximum_fusion.7), channel_id=1, source_target_pairs={{0,8},{2,10},{4,12},{6,14},{8,0},{10,2},{12,4},{14,6},{16,24},{18,... | collective-permute-start | bytes 221192 | tf_op jit(solution)/shard_map/ppermute | solution.py:517
  56.5 8.2 %collective-permute-start.16 = (bf16[2,144,128]{2,1,0:T(8,128)(2,1)S(1)}, bf16[2,144,128]{2,1,0:T(8,128)(2,1)S(1)}, u32[]{:S(2)}, u32[]{:S(2)}) collective-permute-start(bf16[2,144,128]{2,1,0:T(8,128)(2,1)S(1)} %pad_maximum_fusion.8.refs_5_), channel_id=1, source_target_pairs={{0,12},{2,14},{4,8},{6,10},{8,4},{10,6},{12,0},{14,2},{16,28},{18,... | collective-permute-start | bytes 221192 | tf_op jit(solution)/shard_map/ppermute | solution.py:517
  65.5 5.3 %collective-permute-start.17 = (bf16[64,384]{1,0:T(8,128)(2,1)S(1)}, bf16[64,384]{1,0:T(8,128)(2,1)S(1)}, u32[]{:S(2)}, u32[]{:S(2)}) collective-permute-start(bf16[64,384]{1,0:T(8,128)(2,1)S(1)} %kept_attended.1.refs_1_), channel_id=1, source_target_pairs={{0,1},{1,0},{2,3},{3,2},{4,5},{5,4},{6,7},{7,6},{8,9},{9,8},{10,11... | collective-permute-start | bytes 147464 | tf_op jit(solution)/shard_map/ppermute | solution.py:513

commit v4 on v3

--- a/solution.py
+++ b/solution.py
@@ -156,11 +156,15 @@
         log_ref[2 * pair + 1:2 * pair + 2, :] = log_row[:, 64:]
 
 
-def pack_grads(info_ref, packed_ref, own_cot_ref, other_cot_ref, w_ref, hots_ref, kept_out_ref,
+def own_grads(info_ref, own_cot_ref, w_ref, out_ref):
+    own_w = w_ref[:, pl.ds(pl.multiple_of(info_ref[0] * WIDE, 128), WIDE)]
+    out_ref[...] = dot_nt(own_cot_ref[...], own_w)
+
+
+def pack_grads(info_ref, packed_ref, own_part_ref, other_cot_ref, w_ref, hots_ref, kept_out_ref,
                kept_log_ref, grad_ref, kept_grad_ref, near_ref, far_ref, slots):
-    own_w = w_ref[:, pl.ds(pl.multiple_of(info_ref[0] * WIDE, 128), WIDE)]
     other_w = w_ref[:, pl.ds(pl.multiple_of((1 - info_ref[0]) * WIDE, 128), WIDE)]
-    grad = (dot_nt(own_cot_ref[...], own_w) + dot_nt(other_cot_ref[...], other_w)).astype(BF)
+    grad = (own_part_ref[...] + dot_nt(other_cot_ref[...], other_w)).astype(BF)
     grad_ref[...] = grad
     for local in range(LOCAL_HEADS):
         rows = dot_nn(hots_ref[span(local), :], grad[:, span(local)])
@@ -521,11 +525,11 @@
     return jnp.stack([array, flip(array, first), flip(array, second), flip(array, first ^ second)])
 
 
-def octet_exchange(near, far):
+def octet_exchange(near, far, order):
     crossed = flip(far, 1)
     blocks = [jnp.stack([near[chip], crossed[chip]]) for chip in range(4)]
-    arrived = {chip: flip(blocks[chip], 2 * chip) for chip in (3, 2, 1)}
-    return jnp.concatenate([blocks[0]] + [arrived[chip] for chip in (1, 2, 3)]), blocks[3], arrived[3]
+    arrived = {chip: flip(blocks[chip], 2 * chip) for chip in order}
+    return jnp.concatenate([blocks[0]] + [arrived[chip] for chip in (1, 2, 3)]), blocks[3], arrived[order[0]]
 
 
 def body(queries, keys, values, weight_out, cotangent):
@@ -549,12 +553,13 @@
     out_t, log0, att_t = call(
         local_forward, [((WIDE, ROWS), F32), stat, ((WIDE, ROWS), BF)], (qkv,), flops=400000000, info=info,
     )
+    (own_part,) = call(own_grads, [square], (cotangent, weight_out), flops=200000000, info=info)
     grad, kept_grad, near, far = call(
         pack_grads, [((ROWS, WIDE), BF), ((KEPT, WIDE), BF), block, block],
-        (packed, cotangent, other_cot, weight_out, hots, kept_out, kept_log), flops=400000000, info=info, after=(att_t,),
+        (packed, own_part, other_cot, weight_out, hots, kept_out, kept_log), flops=400000000, info=info, after=(att_t,),
         scratch=[pltpu.VMEM((8, 2 * KEPT + 16, 128), BF)],
     )
-    block1, _, arrived = octet_exchange(near, far)
+    block1, _, arrived = octet_exchange(near, far, (3, 2, 1))
     late_w, _ = lax.optimization_barrier((weight_out, near))
     late_att, _ = lax.optimization_barrier((att_t, arrived))
     own_w = lax.dynamic_slice_in_dim(late_w, half * WIDE, WIDE, 1)
@@ -593,7 +598,7 @@
         level_three, [block, block],
         (block1, block2, block3, stat1, stat2, out1, out2, dq1, dkv1, dq2, dkv2), flops=300000000, after=(base, early[-1]),
     )
-    back, crossed, _ = octet_exchange(near, far)
+    back, crossed, _ = octet_exchange(near, far, (2, 3, 1))
     early.extend(backward(2, crossed))
     (own_kept,) = call(
         kept_attended, [((KEPT, WIDE), BF)], (back, kept_out, kept_log), flops=10000000, info=info, after=(early[-1],)

time: 72.4 us -> 72.1 us (level)
  waiting for transfers between devices: 14.4 us -> 13.4 us
    ppermute x4, waiting for transfers between devices: 1.22 us -> 0.23 us  [partner(): return lax.ppermute(array, 'head', [(0, 1), (1, 0)])]
    pallas_call x17 -> x18, Pallas kernels: 26.6 us -> 27.3 us  [call(): pl.pallas_call(run, out_shape=shapes, in_specs=[pl.BlockSpec(memory_space...]
  transfers between devices with their start and end apart: 18 -> 18, of which waited for: 9 -> 9; matrix products, arithmetic and copies ran while one was open for 2% -> 2% of each run, Pallas kernels for 28% -> 29%
where the time goes in v4:
time: 72.1 us; the launch traced here: 72 us
  starting transfers between devices  28.4 us (39%)
  Pallas kernels  27.3 us (38%)
  waiting for transfers between devices  13.4 us (19%)
  other arithmetic  1.6 us (2%)
  between operations  1.09 us (2%)
    pallas_call x18, Pallas kernels, call(): pl.pallas_call(run, out_shape=shapes, in_specs=[pl.BlockSpec(memory_space...  27.3 us
    ppermute x14, starting transfers between devices, flip(): lax.ppermute(array, 'seq', [(i, i ^ mask) for i in range(lax.axis_size('s...  23.2 us
    ppermute x14, waiting for transfers between devices, flip(): lax.ppermute(array, 'seq', [(i, i ^ mask) for i in range(lax.axis_size('s...  13.2 us
    ppermute x4, starting transfers between devices, partner(): return lax.ppermute(array, 'head', [(0, 1), (1, 0)])  5.22 us
  transfers between devices with their start and end apart: 18, of which 9 were waited for; matrix products, arithmetic and copies ran while one was open for 2% of the time, Pallas kernels for 29%

profile of v4, /device:TPU:2, one launch (start us, length us, event | category | flops | bytes accessed | tf_op | source)
XLA Modules:
  0.0 72.0 jit_solution(15846242503488276756)
XLA Ops:
  0.6 2.4 %collective-permute-start = (bf16[512,384]{1,0:T(8,128)(2,1)}, bf16[512,384]{1,0:T(8,128)(2,1)S(1)}, u32[]{:S(2)}, u32[]{:S(2)}) collective-permute-start(bf16[512,384]{1,0:T(8,128)(2,1)} %refs_1_.1), channel_id=1, source_target_pairs={{0,1},{1,0},{2,3},{3,2},{4,5},{5,4},{6,7},{7,6},{8,9},{9,8},{10,11... | collective-permute-start | bytes 1179656 | tf_op jit(solution)/shard_map/ppermute | solution.py:517
  3.0 0.1 pad_add_fusion.refs_0_
  3.1 1.4 %pad_maximum_fusion.refs_1_.refs_0_ = bf16[3,512,384]{2,1,0:T(8,128)(2,1)S(1)} fusion(bf16[1,512,384]{2,1,0:T(8,128)(2,1)} %bitcast.15, bf16[1,512,384]{2,1,0:T(8,128)(2,1)} %bitcast.16, bf16[1,512,384]{2,1,0:T(8,128)(2,1)} %bitcast.17), kind=kLoop, calls=%fused_computation | loop fusion | flops 1179648 | bytes 2359296 | tf_op jit(solution)/shard_map/stack | solution.py:546
  4.5 0.0 copy-start
  4.5 0.0 copy-start.1
  4.5 1.1 %pack_data.1 = (bf16[6,128,128]{2,1,0:T(8,128)(2,1)S(1)}, bf16[384,512]{1,0:T(8,128)(2,1)S(1)}) custom-call(s32[2]{0:T(128)S(1)} %pad_add_fusion.refs_0_, bf16[3,512,384]{2,1,0:T(8,128)(2,1)S(1)} %pad_maximum_fusion.refs_1_.refs_0_), custom_call_target="tpu_custom_call" | custom-call | flops 200000000 | bytes 1769472 | tf_op jit(solution)/shard_map/pack_data/pallas_call | solution.py:502
  5.6 0.9 %kept_forward.1 = (f32[64,384]{1,0:T(8,128)S(1)}, f32[8,64]{1,0:T(8,128)S(1)}) custom-call(bf16[3,512,384]{2,1,0:T(8,128)(2,1)S(1)} %pad_maximum_fusion.refs_1_.refs_0_, bf16[6,128,128]{2,1,0:T(8,128)(2,1)S(1)} %get-tuple-element.46.refs_1_.refs_2_), custom_call_target="tpu_custom_call" | custom-call | flops 100000000 | bytes 1476608 | tf_op jit(solution)/shard_map/kept_forward/pallas_call | solution.py:502
  6.5 0.0 copy-done
  6.5 0.0 copy-done.1
  6.6 1.0 %own_grads.1.refs_2_ = f32[512,384]{1,0:T(8,128)S(1)} custom-call(s32[2]{0:T(128)S(1)} %pad_add_fusion.refs_0_, bf16[512,384]{1,0:T(8,128)(2,1)S(1)} %copy-done.1, bf16[384,768]{1,0:T(8,128)(2,1)S(1)} %copy-done), custom_call_target="tpu_custom_call" | custom-call | flops 200000000 | bytes 1769472 | tf_op jit(solution)/shard_map/own_grads/pallas_call | solution.py:502
  7.5 4.0 %local_forward.1 = (f32[384,512]{1,0:T(8,128)S(1)}, f32[8,512]{1,0:T(8,128)S(1)}, bf16[384,512]{1,0:T(8,128)(2,1)S(1)}) custom-call(s32[2]{0:T(128)S(1)} %pad_add_fusion.refs_0_, bf16[3,512,384]{2,1,0:T(8,128)(2,1)S(1)} %pad_maximum_fusion.refs_1_.refs_0_), custom_call_target="tpu_custom_call" | custom-call | flops 400000000 | bytes 2375680 | tf_op jit(solution)/shard_map/local_forward/pallas_call | solution.py:502
  11.6 0.2 collective-permute-done.refs_3_
  11.8 1.5 %pack_grads.1 = (bf16[512,384]{1,0:T(8,128)(2,1)S(1)}, bf16[64,384]{1,0:T(8,128)(2,1)S(1)}, bf16[4,144,128]{2,1,0:T(8,128)(2,1)S(1)}, bf16[4,144,128]{2,1,0:T(8,128)(2,1)S(1)}) custom-call(s32[2]{0:T(128)S(1)} %pad_add_fusion.refs_0_, bf16[6,128,128]{2,1,0:T(8,128)(2,1)S(1)} %get-tuple-element.46.refs_1_.refs_2_, f32[512,384]{1,0:T(8,128)S(1)} %own_grads.1.refs_2_, ...), custom_call_target="tpu_custom_call" | custom-call | flops 400000000 | bytes 3196928 | tf_op jit(solution)/shard_map/pack_grads/pallas_call | solution.py:502
  13.3 0.1 collective-permute-start.1
  13.4 0.1 constant_dynamic-slice_fusion
  13.5 0.4 collective-permute-start.4
  13.9 0.9 %collective-permute-done.1 = bf16[4,144,128]{2,1,0:T(8,128)(2,1)S(1)} collective-permute-done((bf16[4,144,128]{2,1,0:T(8,128)(2,1)S(1)}, bf16[4,144,128]{2,1,0:T(8,128)(2,1)S(1)}, u32[]{:S(2)}, u32[]{:S(2)}) %collective-permute-start.1) | collective-permute-done | bytes 147488 | tf_op jit(solution)/shard_map/ppermute | solution.py:521
  14.8 4.7 %collective-permute-start.2 = (bf16[2,144,128]{2,1,0:T(8,128)(2,1)S(1)}, bf16[2,144,128]{2,1,0:T(8,128)(2,1)S(1)}, u32[]{:S(2)}, u32[]{:S(2)}) collective-permute-start(bf16[2,144,128]{2,1,0:T(8,128)(2,1)S(1)} %pad_maximum_fusion.3), channel_id=1, source_target_pairs={{0,12},{2,14},{4,8},{6,10},{8,4},{10,6},{12,0},{14,2},{16,28},{18,... | collective-permute-start | bytes 221192 | tf_op jit(solution)/shard_map/ppermute | solution.py:521
  19.5 0.1 collective-permute-start.5
  19.6 0.6 collective-permute-start.6
  20.3 2.3 %collective-permute-done.2 = bf16[2,144,128]{2,1,0:T(8,128)(2,1)S(1)} collective-permute-done((bf16[2,144,128]{2,1,0:T(8,128)(2,1)S(1)}, bf16[2,144,128]{2,1,0:T(8,128)(2,1)S(1)}, u32[]{:S(2)}, u32[]{:S(2)}) %collective-permute-start.2) | collective-permute-done | bytes 73760 | tf_op jit(solution)/shard_map/ppermute | solution.py:521
  22.6 0.9 %collective-permute-start.3 = (bf16[384,512]{1,0:T(8,128)(2,1)S(1)}, bf16[384,512]{1,0:T(8,128)(2,1)S(1)}, u32[]{:S(2)}, u32[]{:S(2)}) collective-permute-start(bf16[384,512]{1,0:T(8,128)(2,1)S(1)} %get-tuple-element.52.refs_8_.refs_1_), channel_id=1, source_target_pairs={{0,1},{1,0},{2,3},{3,2},{4,5},{5,4},{6,7},{7,6},{8,9},{9,8},{10,11... | collective-permute-start | bytes 1179656 | tf_op jit(solution)/shard_map/ppermute | solution.py:517
  23.5 1.4 %collective-permute-done.5 = bf16[2,144,128]{2,1,0:T(8,128)(2,1)S(1)} collective-permute-done((bf16[2,144,128]{2,1,0:T(8,128)(2,1)S(1)}, bf16[2,144,128]{2,1,0:T(8,128)(2,1)S(1)}, u32[]{:S(2)}, u32[]{:S(2)}) %collective-permute-start.5) | collective-permute-done | bytes 73760 | tf_op jit(solution)/shard_map/ppermute | solution.py:521
  24.9 1.7 %collective-permute-done.6 = bf16[2,144,128]{2,1,0:T(8,128)(2,1)S(1)} collective-permute-done((bf16[2,144,128]{2,1,0:T(8,128)(2,1)S(1)}, bf16[2,144,128]{2,1,0:T(8,128)(2,1)S(1)}, u32[]{:S(2)}, u32[]{:S(2)}) %collective-permute-start.6) | collective-permute-done | bytes 73760 | tf_op jit(solution)/shard_map/ppermute | solution.py:521
  26.6 0.8 %level_one.1 = (bf16[272,128]{1,0:T(8,128)(2,1)S(1)}, f32[8,512]{1,0:T(8,128)S(1)}, f32[64,512]{1,0:T(8,128)S(1)}) custom-call(bf16[8,144,128]{2,1,0:T(8,128)(2,1)S(1)} %constant_dynamic-update-slice_fusion.refs_0_), custom_call_target="tpu_custom_call" | custom-call | flops 100000000 | bytes 512000 | tf_op jit(solution)/shard_map/level_one/pallas_call | solution.py:502
  27.4 4.8 %collective-permute-start.9 = (bf16[272,128]{1,0:T(8,128)(2,1)S(1)}, bf16[272,128]{1,0:T(8,128)(2,1)S(1)}, u32[]{:S(2)}, u32[]{:S(2)}) collective-permute-start(bf16[272,128]{1,0:T(8,128)(2,1)S(1)} %get-tuple-element.55.refs_5_), channel_id=1, source_target_pairs={{0,60},{2,62},{4,56},{6,58},{8,52},{10,54},{12,48},{14,50},{16,44}... | collective-permute-start | bytes 208904 | tf_op jit(solution)/shard_map/ppermute | solution.py:521
  32.2 0.0 collective-permute-start.8
  32.2 0.7 collective-permute-start.7
  32.8 1.0 %level_one_back.1 = (f32[64,512]{1,0:T(8,128)S(1)}, f32[512,128]{1,0:T(8,128)S(1)}) custom-call(bf16[8,144,128]{2,1,0:T(8,128)(2,1)S(1)} %constant_dynamic-update-slice_fusion.refs_0_, f32[8,512]{1,0:T(8,128)S(1)} %get-tuple-element.56.refs_1_.refs_3_), custom_call_target="tpu_custom_call" | custom-call | flops 100000000 | bytes 704512 | tf_op jit(solution)/shard_map/level_one_back/pallas_call | solution.py:502
  33.9 2.1 %local_backward.3 = (f32[512,128]{1,0:T(8,128)S(1)}, f32[512,128]{1,0:T(8,128)S(1)}, f32[512,128]{1,0:T(8,128)S(1)}) custom-call(s32[2]{0:T(128)S(1)} %pad_add_fusion.refs_0_, bf16[3,512,384]{2,1,0:T(8,128)(2,1)S(1)} %pad_maximum_fusion.refs_1_.refs_0_, bf16[512,384]{1,0:T(8,128)(2,1)S(1)} %get-tuple-element.58.refs_2_, ...), custom_call_target="tpu_custom_call" | custom-call | flops 300000000 | bytes 3162112 | tf_op jit(solution)/shard_map/local_backward/pallas_call | solution.py:502
  36.0 0.5 collective-permute-done.9
  36.4 1.3 %collective-permute-done.8 = bf16[272,128]{1,0:T(8,128)(2,1)S(1)} collective-permute-done((bf16[272,128]{1,0:T(8,128)(2,1)S(1)}, bf16[272,128]{1,0:T(8,128)(2,1)S(1)}, u32[]{:S(2)}, u32[]{:S(2)}) %collective-permute-start.8) | collective-permute-done | bytes 69664 | tf_op jit(solution)/shard_map/ppermute | solution.py:521
  37.8 0.0 collective-permute-done.7
  37.8 0.0 collective-permute-done.4.refs_4_.refs_2_.refs_3_
  37.8 0.0 collective-permute-done.3.refs_2_.refs_1_
  37.8 0.9 %level_two.1 = (bf16[272,128]{1,0:T(8,128)(2,1)S(1)}, f32[8,512]{1,0:T(8,128)S(1)}, f32[64,128]{1,0:T(8,128)S(1)}) custom-call(bf16[4,272,128]{2,1,0:T(8,128)(2,1)S(1)} %pad_maximum_fusion.1.refs_0_.refs_1_, bf16[384,512]{1,0:T(8,128)(2,1)S(1)} %collective-permute-done.3.refs_2_.refs_1_, bf16[384,384]{1,0:T(8,128)(2,1)S(1)} %collective-permute-done.4.refs_4_.refs_2_.refs_3_, ...), custom_call_target="tpu_custom_call" | custom-call | flops 100000000 | bytes 397312 | tf_op jit(solution)/shard_map/level_two/pallas_call | solution.py:502
  38.7 3.8 %collective-permute-start.12 = (bf16[272,128]{1,0:T(8,128)(2,1)S(1)}, bf16[272,128]{1,0:T(8,128)(2,1)S(1)}, u32[]{:S(2)}, u32[]{:S(2)}) collective-permute-start(bf16[272,128]{1,0:T(8,128)(2,1)S(1)} %get-tuple-element.62.refs_5_), channel_id=1, source_target_pairs={{0,224},{2,226},{4,228},{6,230},{8,232},{10,234},{12,236},{14,238}... | collective-permute-start | bytes 208904 | tf_op jit(solution)/shard_map/ppermute | solution.py:521
  42.5 1.0 %collective-permute-start.11 = (bf16[272,128]{1,0:T(8,128)(2,1)S(1)}, bf16[272,128]{1,0:T(8,128)(2,1)S(1)}, u32[]{:S(2)}, u32[]{:S(2)}) collective-permute-start(bf16[272,128]{1,0:T(8,128)(2,1)S(1)} %get-tuple-element.62.refs_5_), channel_id=1, source_target_pairs={{0,96},{2,98},{4,100},{6,102},{8,104},{10,106},{12,108},{14,110},{... | collective-permute-start | bytes 208904 | tf_op jit(solution)/shard_map/ppermute | solution.py:521
  43.6 1.4 %collective-permute-start.10 = (bf16[272,128]{1,0:T(8,128)(2,1)S(1)}, bf16[272,128]{1,0:T(8,128)(2,1)S(1)}, u32[]{:S(2)}, u32[]{:S(2)}) collective-permute-start(bf16[272,128]{1,0:T(8,128)(2,1)S(1)} %get-tuple-element.62.refs_5_), channel_id=1, source_target_pairs={{0,128},{2,130},{4,132},{6,134},{8,136},{10,138},{12,140},{14,142}... | collective-permute-start | bytes 208904 | tf_op jit(solution)/shard_map/ppermute | solution.py:521
  45.0 0.8 %level_two_back.1 = (f32[512,128]{1,0:T(8,128)S(1)}, f32[128,128]{1,0:T(8,128)S(1)}, f32[64,128]{1,0:T(8,128)S(1)}) custom-call(bf16[8,144,128]{2,1,0:T(8,128)(2,1)S(1)} %constant_dynamic-update-slice_fusion.refs_0_, bf16[4,272,128]{2,1,0:T(8,128)(2,1)S(1)} %pad_maximum_fusion.1.refs_0_.refs_1_, f32[8,512]{1,0:T(8,128)S(1)} %get-tuple-element.63.refs_2_.refs_4_, ...), custom_call_target="tpu_custom_call" | custom-call | flops 100000000 | bytes 1212416 | tf_op jit(solution)/shard_map/level_two_back/pallas_call | solution.py:502
  45.8 2.1 %local_backward.4 = (f32[512,128]{1,0:T(8,128)S(1)}, f32[512,128]{1,0:T(8,128)S(1)}, f32[512,128]{1,0:T(8,128)S(1)}) custom-call(s32[2]{0:T(128)S(1)} %pad_add_fusion.refs_0_, bf16[3,512,384]{2,1,0:T(8,128)(2,1)S(1)} %pad_maximum_fusion.refs_1_.refs_0_, bf16[512,384]{1,0:T(8,128)(2,1)S(1)} %get-tuple-element.58.refs_2_, ...), custom_call_target="tpu_custom_call" | custom-call | flops 300000000 | bytes 3162112 | tf_op jit(solution)/shard_map/local_backward/pallas_call | solution.py:502
  47.9 1.4 %mix_base.1 = (f32[512,384]{1,0:T(8,128)S(1)}, bf16[512,384]{1,0:T(8,128)(2,1)S(1)}, bf16[512,384]{1,0:T(8,128)(2,1)S(1)}) custom-call(s32[2]{0:T(128)S(1)} %pad_add_fusion.refs_0_, bf16[384,512]{1,0:T(8,128)(2,1)S(1)} %get-tuple-element.52.refs_8_.refs_1_, bf16[384,512]{1,0:T(8,128)(2,1)S(1)} %collective-permute-done.3.refs_2_.refs_1_, ...), custom_call_target="tpu_custom_call" | custom-call | flops 300000000 | bytes 2949120 | tf_op jit(solution)/shard_map/mix_base/pallas_call | solution.py:502
  49.3 0.0 collective-permute-done.12
  49.4 0.0 collective-permute-done.11
  49.4 0.0 collective-permute-done.10
  49.4 1.7 %level_three.1 = (bf16[4,144,128]{2,1,0:T(8,128)(2,1)S(1)}, bf16[4,144,128]{2,1,0:T(8,128)(2,1)S(1)}) custom-call(bf16[8,144,128]{2,1,0:T(8,128)(2,1)S(1)} %constant_dynamic-update-slice_fusion.refs_0_, bf16[4,272,128]{2,1,0:T(8,128)(2,1)S(1)} %pad_maximum_fusion.1.refs_0_.refs_1_, bf16[4,272,128]{2,1,0:T(8,128)(2,1)S(1)} %pad_maximum_fusion.2.refs_2_, ...), custom_call_target="tpu_custom_call" | custom-call | flops 300000000 | bytes 1835008 | tf_op jit(solution)/shard_map/level_three/pallas_call | solution.py:502
  51.1 0.1 collective-permute-start.13
  51.2 1.3 %collective-permute-done.13 = bf16[4,144,128]{2,1,0:T(8,128)(2,1)S(1)} collective-permute-done((bf16[4,144,128]{2,1,0:T(8,128)(2,1)S(1)}, bf16[4,144,128]{2,1,0:T(8,128)(2,1)S(1)}, u32[]{:S(2)}, u32[]{:S(2)}) %collective-permute-start.13) | collective-permute-done | bytes 147488 | tf_op jit(solution)/shard_map/ppermute | solution.py:521
  52.6 3.0 %collective-permute-start.14 = (bf16[2,144,128]{2,1,0:T(8,128)(2,1)S(1)}, bf16[2,144,128]{2,1,0:T(8,128)(2,1)S(1)}, u32[]{:S(2)}, u32[]{:S(2)}) collective-permute-start(bf16[2,144,128]{2,1,0:T(8,128)(2,1)S(1)} %pad_maximum_fusion.6), channel_id=1, source_target_pairs={{0,4},{2,6},{4,0},{6,2},{8,12},{10,14},{12,8},{14,10},{16,20},{18,... | collective-permute-start | bytes 221192 | tf_op jit(solution)/shard_map/ppermute | solution.py:521
  55.7 0.6 collective-permute-start.15
  56.2 2.2 %collective-permute-start.16 = (bf16[2,144,128]{2,1,0:T(8,128)(2,1)S(1)}, bf16[2,144,128]{2,1,0:T(8,128)(2,1)S(1)}, u32[]{:S(2)}, u32[]{:S(2)}) collective-permute-start(bf16[2,144,128]{2,1,0:T(8,128)(2,1)S(1)} %pad_maximum_fusion.8.refs_5_), channel_id=1, source_target_pairs={{0,12},{2,14},{4,8},{6,10},{8,4},{10,6},{12,0},{14,2},{16,28},{18,... | collective-permute-start | bytes 221192 | tf_op jit(solution)/shard_map/ppermute | solution.py:521
  58.5 2.1 %local_backward.5 = (f32[512,128]{1,0:T(8,128)S(1)}, f32[512,128]{1,0:T(8,128)S(1)}, f32[512,128]{1,0:T(8,128)S(1)}) custom-call(s32[2]{0:T(128)S(1)} %pad_add_fusion.refs_0_, bf16[3,512,384]{2,1,0:T(8,128)(2,1)S(1)} %pad_maximum_fusion.refs_1_.refs_0_, bf16[512,384]{1,0:T(8,128)(2,1)S(1)} %get-tuple-element.58.refs_2_, ...), custom_call_target="tpu_custom_call" | custom-call | flops 300000000 | bytes 3162112 | tf_op jit(solution)/shard_map/local_backward/pallas_call | solution.py:502
  60.6 0.0 collective-permute-done.14
  60.6 3.8 %collective-permute-done.15 = bf16[2,144,128]{2,1,0:T(8,128)(2,1)S(1)} collective-permute-done((bf16[2,144,128]{2,1,0:T(8,128)(2,1)S(1)}, bf16[2,144,128]{2,1,0:T(8,128)(2,1)S(1)}, u32[]{:S(2)}, u32[]{:S(2)}) %collective-permute-start.15) | collective-permute-done | bytes 73760 | tf_op jit(solution)/shard_map/ppermute | solution.py:521
  64.4 0.0 collective-permute-done.16
  64.4 0.7 %kept_attended.1.refs_1_ = bf16[64,384]{1,0:T(8,128)(2,1)S(1)} custom-call(s32[2]{0:T(128)S(1)} %pad_add_fusion.refs_0_, bf16[8,144,128]{2,1,0:T(8,128)(2,1)S(1)} %constant_dynamic-update-slice_fusion.3.refs_1_.refs_4_, f32[64,384]{1,0:T(8,128)S(1)} %get-tuple-element.48.refs_6_.refs_2_, f32[8,64]{1,0:T(8,128)S(1)} %get-tuple-element.49.refs_7_.refs_3_, ...), custom_call_target="tpu_custom_call" | custom-call | flops 10000000 | bytes 444416 | tf_op jit(solution)/shard_map/kept_attended/pallas_call | solution.py:502
  65.2 1.6 %collective-permute-start.17 = (bf16[64,384]{1,0:T(8,128)(2,1)S(1)}, bf16[64,384]{1,0:T(8,128)(2,1)S(1)}, u32[]{:S(2)}, u32[]{:S(2)}) collective-permute-start(bf16[64,384]{1,0:T(8,128)(2,1)S(1)} %kept_attended.1.refs_1_), channel_id=1, source_target_pairs={{0,1},{1,0},{2,3},{3,2},{4,5},{5,4},{6,7},{7,6},{8,9},{9,8},{10,11... | collective-permute-start | bytes 147464 | tf_op jit(solution)/shard_map/ppermute | solution.py:517
  66.8 0.5 mix_own.1.refs_0_
  67.3 3.2 %final_grads.1 = (bf16[512,384]{1,0:T(8,128)(2,1)}, bf16[512,384]{1,0:T(8,128)(2,1)}, bf16[512,384]{1,0:T(8,128)(2,1)}) custom-call(s32[2]{0:T(128)S(1)} %pad_add_fusion.refs_0_, bf16[3,512,384]{2,1,0:T(8,128)(2,1)S(1)} %pad_maximum_fusion.refs_1_.refs_0_, bf16[6,128,128]{2,1,0:T(8,128)(2,1)S(1)} %get-tuple-element.46.refs_1_.refs_2_, ...), custom_call_target="tpu_custom_call" | custom-call | flops 200000000 | bytes 5652480 | tf_op jit(solution)/shard_map/final_grads/pallas_call | solution.py:502
  70.5 0.0 collective-permute-done.17.refs_1_
  70.5 1.3 %mix_other.1 = bf16[512,384]{1,0:T(8,128)(2,1)} custom-call(f32[512,384]{1,0:T(8,128)S(1)} %mix_own.1.refs_0_, bf16[64,384]{1,0:T(8,128)(2,1)S(1)} %collective-permute-done.17.refs_1_, bf16[512,384]{1,0:T(8,128)(2,1)S(1)} %get-tuple-element.75.refs_2_, bf16[384,384]{1,0:T(8,128)(2,1)S(1)} %collective-permute-done.4.refs_4_.refs_2_.refs_3_), custom_call_target="tpu_custom_call" | custom-call | flops 200000000 | bytes 1916928 | tf_op jit(solution)/shard_map/mix_other/pallas_call | solution.py:502
  (18 shorter events, 0.3 us)
Async XLA Ops:
  0.6 11.2 %collective-permute-start = (bf16[512,384]{1,0:T(8,128)(2,1)}, bf16[512,384]{1,0:T(8,128)(2,1)S(1)}, u32[]{:S(2)}, u32[]{:S(2)}) collective-permute-start(bf16[512,384]{1,0:T(8,128)(2,1)} %refs_1_.1), channel_id=1, source_target_pairs={{0,1},{1,0},{2,3},{3,2},{4,5},{5,4},{6,7},{7,6},{8,9},{9,8},{10,11... | collective-permute-start | bytes 1179656 | tf_op jit(solution)/shard_map/ppermute | solution.py:517
  4.5 2.1 %copy-start = (bf16[384,768]{1,0:T(8,128)(2,1)S(1)}, bf16[384,768]{1,0:T(8,128)(2,1)}, u32[]{:S(2)}) copy-start(bf16[384,768]{1,0:T(8,128)(2,1)} %refs_4_.1) | copy-start | bytes 1769476
  4.5 2.1 %copy-start.1 = (bf16[512,384]{1,0:T(8,128)(2,1)S(1)}, bf16[512,384]{1,0:T(8,128)(2,1)}, u32[]{:S(2)}) copy-start(bf16[512,384]{1,0:T(8,128)(2,1)} %refs_1_.1) | copy-start | bytes 1179652
  13.3 1.5 %collective-permute-start.1 = (bf16[4,144,128]{2,1,0:T(8,128)(2,1)S(1)}, bf16[4,144,128]{2,1,0:T(8,128)(2,1)S(1)}, u32[]{:S(2)}, u32[]{:S(2)}) collective-permute-start(bf16[4,144,128]{2,1,0:T(8,128)(2,1)S(1)} %get-tuple-element.51), channel_id=1, source_target_pairs={{0,2},{2,0},{4,6},{6,4},{8,10},{10,8},{12,14},{14,12},{16,18},{18,... | collective-permute-start | bytes 442376 | tf_op jit(solution)/shard_map/ppermute | solution.py:521
  13.5 24.3 %collective-permute-start.4 = (bf16[384,384]{1,0:T(8,128)(2,1)S(1)}, bf16[384,384]{1,0:T(8,128)(2,1)S(1)}, u32[]{:S(2)}, u32[]{:S(2)}) collective-permute-start(bf16[384,384]{1,0:T(8,128)(2,1)S(1)} %get-tuple-element.86), channel_id=1, source_target_pairs={{0,1},{1,0},{2,3},{3,2},{4,5},{5,4},{6,7},{7,6},{8,9},{9,8},{10,11... | collective-permute-start | bytes 884744 | tf_op jit(solution)/shard_map/ppermute | solution.py:517
  14.8 7.8 %collective-permute-start.2 = (bf16[2,144,128]{2,1,0:T(8,128)(2,1)S(1)}, bf16[2,144,128]{2,1,0:T(8,128)(2,1)S(1)}, u32[]{:S(2)}, u32[]{:S(2)}) collective-permute-start(bf16[2,144,128]{2,1,0:T(8,128)(2,1)S(1)} %pad_maximum_fusion.3), channel_id=1, source_target_pairs={{0,12},{2,14},{4,8},{6,10},{8,4},{10,6},{12,0},{14,2},{16,28},{18,... | collective-permute-start | bytes 221192 | tf_op jit(solution)/shard_map/ppermute | solution.py:521
  19.5 5.3 %collective-permute-start.5 = (bf16[2,144,128]{2,1,0:T(8,128)(2,1)S(1)}, bf16[2,144,128]{2,1,0:T(8,128)(2,1)S(1)}, u32[]{:S(2)}, u32[]{:S(2)}) collective-permute-start(bf16[2,144,128]{2,1,0:T(8,128)(2,1)S(1)} %pad_maximum_fusion.4), channel_id=1, source_target_pairs={{0,4},{2,6},{4,0},{6,2},{8,12},{10,14},{12,8},{14,10},{16,20},{18,... | collective-permute-start | bytes 221192 | tf_op jit(solution)/shard_map/ppermute | solution.py:521
  19.6 6.9 %collective-permute-start.6 = (bf16[2,144,128]{2,1,0:T(8,128)(2,1)S(1)}, bf16[2,144,128]{2,1,0:T(8,128)(2,1)S(1)}, u32[]{:S(2)}, u32[]{:S(2)}) collective-permute-start(bf16[2,144,128]{2,1,0:T(8,128)(2,1)S(1)} %pad_maximum_fusion.5), channel_id=1, source_target_pairs={{0,8},{2,10},{4,12},{6,14},{8,0},{10,2},{12,4},{14,6},{16,24},{18,... | collective-permute-start | bytes 221192 | tf_op jit(solution)/shard_map/ppermute | solution.py:521
  22.6 15.2 %collective-permute-start.3 = (bf16[384,512]{1,0:T(8,128)(2,1)S(1)}, bf16[384,512]{1,0:T(8,128)(2,1)S(1)}, u32[]{:S(2)}, u32[]{:S(2)}) collective-permute-start(bf16[384,512]{1,0:T(8,128)(2,1)S(1)} %get-tuple-element.52.refs_8_.refs_1_), channel_id=1, source_target_pairs={{0,1},{1,0},{2,3},{3,2},{4,5},{5,4},{6,7},{7,6},{8,9},{9,8},{10,11... | collective-permute-start | bytes 1179656 | tf_op jit(solution)/shard_map/ppermute | solution.py:517
  27.4 9.0 %collective-permute-start.9 = (bf16[272,128]{1,0:T(8,128)(2,1)S(1)}, bf16[272,128]{1,0:T(8,128)(2,1)S(1)}, u32[]{:S(2)}, u32[]{:S(2)}) collective-permute-start(bf16[272,128]{1,0:T(8,128)(2,1)S(1)} %get-tuple-element.55.refs_5_), channel_id=1, source_target_pairs={{0,60},{2,62},{4,56},{6,58},{8,52},{10,54},{12,48},{14,50},{16,44}... | collective-permute-start | bytes 208904 | tf_op jit(solution)/shard_map/ppermute | solution.py:521
  32.2 5.6 %collective-permute-start.8 = (bf16[272,128]{1,0:T(8,128)(2,1)S(1)}, bf16[272,128]{1,0:T(8,128)(2,1)S(1)}, u32[]{:S(2)}, u32[]{:S(2)}) collective-permute-start(bf16[272,128]{1,0:T(8,128)(2,1)S(1)} %get-tuple-element.55.refs_5_), channel_id=1, source_target_pairs={{0,28},{2,30},{4,24},{6,26},{8,20},{10,22},{12,16},{14,18},{16,12}... | collective-permute-start | bytes 208904 | tf_op jit(solution)/shard_map/ppermute | solution.py:521
  32.2 5.6 %collective-permute-start.7 = (bf16[272,128]{1,0:T(8,128)(2,1)S(1)}, bf16[272,128]{1,0:T(8,128)(2,1)S(1)}, u32[]{:S(2)}, u32[]{:S(2)}) collective-permute-start(bf16[272,128]{1,0:T(8,128)(2,1)S(1)} %get-tuple-element.55.refs_5_), channel_id=1, source_target_pairs={{0,32},{2,34},{4,36},{6,38},{8,40},{10,42},{12,44},{14,46},{16,48}... | collective-permute-start | bytes 208904 | tf_op jit(solution)/shard_map/ppermute | solution.py:521
  38.7 10.7 %collective-permute-start.12 = (bf16[272,128]{1,0:T(8,128)(2,1)S(1)}, bf16[272,128]{1,0:T(8,128)(2,1)S(1)}, u32[]{:S(2)}, u32[]{:S(2)}) collective-permute-start(bf16[272,128]{1,0:T(8,128)(2,1)S(1)} %get-tuple-element.62.refs_5_), channel_id=1, source_target_pairs={{0,224},{2,226},{4,228},{6,230},{8,232},{10,234},{12,236},{14,238}... | collective-permute-start | bytes 208904 | tf_op jit(solution)/shard_map/ppermute | solution.py:521
  42.5 6.8 %collective-permute-start.11 = (bf16[272,128]{1,0:T(8,128)(2,1)S(1)}, bf16[272,128]{1,0:T(8,128)(2,1)S(1)}, u32[]{:S(2)}, u32[]{:S(2)}) collective-permute-start(bf16[272,128]{1,0:T(8,128)(2,1)S(1)} %get-tuple-element.62.refs_5_), channel_id=1, source_target_pairs={{0,96},{2,98},{4,100},{6,102},{8,104},{10,106},{12,108},{14,110},{... | collective-permute-start | bytes 208904 | tf_op jit(solution)/shard_map/ppermute | solution.py:521
  43.6 5.8 %collective-permute-start.10 = (bf16[272,128]{1,0:T(8,128)(2,1)S(1)}, bf16[272,128]{1,0:T(8,128)(2,1)S(1)}, u32[]{:S(2)}, u32[]{:S(2)}) collective-permute-start(bf16[272,128]{1,0:T(8,128)(2,1)S(1)} %get-tuple-element.62.refs_5_), channel_id=1, source_target_pairs={{0,128},{2,130},{4,132},{6,134},{8,136},{10,138},{12,140},{14,142}... | collective-permute-start | bytes 208904 | tf_op jit(solution)/shard_map/ppermute | solution.py:521
  51.1 1.5 %collective-permute-start.13 = (bf16[4,144,128]{2,1,0:T(8,128)(2,1)S(1)}, bf16[4,144,128]{2,1,0:T(8,128)(2,1)S(1)}, u32[]{:S(2)}, u32[]{:S(2)}) collective-permute-start(bf16[4,144,128]{2,1,0:T(8,128)(2,1)S(1)} %get-tuple-element.72), channel_id=1, source_target_pairs={{0,2},{2,0},{4,6},{6,4},{8,10},{10,8},{12,14},{14,12},{16,18},{18,... | collective-permute-start | bytes 442376 | tf_op jit(solution)/shard_map/ppermute | solution.py:521
  52.6 7.9 %collective-permute-start.14 = (bf16[2,144,128]{2,1,0:T(8,128)(2,1)S(1)}, bf16[2,144,128]{2,1,0:T(8,128)(2,1)S(1)}, u32[]{:S(2)}, u32[]{:S(2)}) collective-permute-start(bf16[2,144,128]{2,1,0:T(8,128)(2,1)S(1)} %pad_maximum_fusion.6), channel_id=1, source_target_pairs={{0,4},{2,6},{4,0},{6,2},{8,12},{10,14},{12,8},{14,10},{16,20},{18,... | collective-permute-start | bytes 221192 | tf_op jit(solution)/shard_map/ppermute | solution.py:521
  55.7 8.7 %collective-permute-start.15 = (bf16[2,144,128]{2,1,0:T(8,128)(2,1)S(1)}, bf16[2,144,128]{2,1,0:T(8,128)(2,1)S(1)}, u32[]{:S(2)}, u32[]{:S(2)}) collective-permute-start(bf16[2,144,128]{2,1,0:T(8,128)(2,1)S(1)} %pad_maximum_fusion.7), channel_id=1, source_target_pairs={{0,8},{2,10},{4,12},{6,14},{8,0},{10,2},{12,4},{14,6},{16,24},{18,... | collective-permute-start | bytes 221192 | tf_op jit(solution)/shard_map/ppermute | solution.py:521
  56.2 8.2 %collective-permute-start.16 = (bf16[2,144,128]{2,1,0:T(8,128)(2,1)S(1)}, bf16[2,144,128]{2,1,0:T(8,128)(2,1)S(1)}, u32[]{:S(2)}, u32[]{:S(2)}) collective-permute-start(bf16[2,144,128]{2,1,0:T(8,128)(2,1)S(1)} %pad_maximum_fusion.8.refs_5_), channel_id=1, source_target_pairs={{0,12},{2,14},{4,8},{6,10},{8,4},{10,6},{12,0},{14,2},{16,28},{18,... | collective-permute-start | bytes 221192 | tf_op jit(solution)/shard_map/ppermute | solution.py:521
  65.2 5.3 %collective-permute-start.17 = (bf16[64,384]{1,0:T(8,128)(2,1)S(1)}, bf16[64,384]{1,0:T(8,128)(2,1)S(1)}, u32[]{:S(2)}, u32[]{:S(2)}) collective-permute-start(bf16[64,384]{1,0:T(8,128)(2,1)S(1)} %kept_attended.1.refs_1_), channel_id=1, source_target_pairs={{0,1},{1,0},{2,3},{3,2},{4,5},{5,4},{6,7},{7,6},{8,9},{9,8},{10,11... | collective-permute-start | bytes 147464 | tf_op jit(solution)/shard_map/ppermute | solution.py:517

commit v5 on v3

--- a/solution.py
+++ b/solution.py
@@ -521,11 +521,11 @@
     return jnp.stack([array, flip(array, first), flip(array, second), flip(array, first ^ second)])
 
 
-def octet_exchange(near, far):
+def octet_exchange(near, far, order):
     crossed = flip(far, 1)
     blocks = [jnp.stack([near[chip], crossed[chip]]) for chip in range(4)]
-    arrived = {chip: flip(blocks[chip], 2 * chip) for chip in (3, 2, 1)}
-    return jnp.concatenate([blocks[0]] + [arrived[chip] for chip in (1, 2, 3)]), blocks[3], arrived[3]
+    arrived = {chip: flip(blocks[chip], 2 * chip) for chip in order}
+    return jnp.concatenate([blocks[0]] + [arrived[chip] for chip in (1, 2, 3)]), blocks[3], arrived[order[0]]
 
 
 def body(queries, keys, values, weight_out, cotangent):
@@ -554,7 +554,7 @@
         (packed, cotangent, other_cot, weight_out, hots, kept_out, kept_log), flops=400000000, info=info, after=(att_t,),
         scratch=[pltpu.VMEM((8, 2 * KEPT + 16, 128), BF)],
     )
-    block1, _, arrived = octet_exchange(near, far)
+    block1, _, arrived = octet_exchange(near, far, (3, 2, 1))
     late_w, _ = lax.optimization_barrier((weight_out, near))
     late_att, _ = lax.optimization_barrier((att_t, arrived))
     own_w = lax.dynamic_slice_in_dim(late_w, half * WIDE, WIDE, 1)
@@ -593,7 +593,7 @@
         level_three, [block, block],
         (block1, block2, block3, stat1, stat2, out1, out2, dq1, dkv1, dq2, dkv2), flops=300000000, after=(base, early[-1]),
     )
-    back, crossed, _ = octet_exchange(near, far)
+    back, crossed, _ = octet_exchange(near, far, (2, 3, 1))
     early.extend(backward(2, crossed))
     (own_kept,) = call(
         kept_attended, [((KEPT, WIDE), BF)], (back, kept_out, kept_log), flops=10000000, info=info, after=(early[-1],)

time: 72.4 us -> 72.4 us (level)
  no operation moved by 1% of the time
where the time goes in v5:
time: 72.4 us; the launch traced here: 72.3 us
  starting transfers between devices  28.4 us (39%)
  Pallas kernels  26.6 us (37%)
  waiting for transfers between devices  14.4 us (20%)
  other arithmetic  1.6 us (2%)
  between operations  1.07 us (1%)
    pallas_call x17, Pallas kernels, call(): pl.pallas_call(run, out_shape=shapes, in_specs=[pl.BlockSpec(memory_space...  26.6 us
    ppermute x14, starting transfers between devices, flip(): lax.ppermute(array, 'seq', [(i, i ^ mask) for i in range(lax.axis_size('s...  23.2 us
    ppermute x14, waiting for transfers between devices, flip(): lax.ppermute(array, 'seq', [(i, i ^ mask) for i in range(lax.axis_size('s...  13.2 us
    ppermute x4, starting transfers between devices, partner(): return lax.ppermute(array, 'head', [(0, 1), (1, 0)])  5.21 us
  transfers between devices with their start and end apart: 18, of which 9 were waited for; matrix products, arithmetic and copies ran while one was open for 2% of the time, Pallas kernels for 28%

profile of v5, /device:TPU:2, one launch (start us, length us, event | category | flops | bytes accessed | tf_op | source)
XLA Modules:
  0.0 72.3 jit_solution(9123243988427637422)
XLA Ops:
  0.6 2.4 %collective-permute-start = (bf16[512,384]{1,0:T(8,128)(2,1)}, bf16[512,384]{1,0:T(8,128)(2,1)S(1)}, u32[]{:S(2)}, u32[]{:S(2)}) collective-permute-start(bf16[512,384]{1,0:T(8,128)(2,1)} %refs_2_.1), channel_id=1, source_target_pairs={{0,1},{1,0},{2,3},{3,2},{4,5},{5,4},{6,7},{7,6},{8,9},{9,8},{10,11... | collective-permute-start | bytes 1179656 | tf_op jit(solution)/shard_map/ppermute | solution.py:513
  3.0 0.1 pad_add_fusion.refs_0_
  3.1 1.4 %pad_maximum_fusion.refs_1_.refs_0_ = bf16[3,512,384]{2,1,0:T(8,128)(2,1)S(1)} fusion(bf16[1,512,384]{2,1,0:T(8,128)(2,1)} %bitcast.15, bf16[1,512,384]{2,1,0:T(8,128)(2,1)} %bitcast.16, bf16[1,512,384]{2,1,0:T(8,128)(2,1)} %bitcast.17), kind=kLoop, calls=%fused_computation | loop fusion | flops 1179648 | bytes 2359296 | tf_op jit(solution)/shard_map/stack | solution.py:542
  4.5 1.1 %pack_data.1 = (bf16[6,128,128]{2,1,0:T(8,128)(2,1)S(1)}, bf16[384,512]{1,0:T(8,128)(2,1)S(1)}) custom-call(s32[2]{0:T(128)S(1)} %pad_add_fusion.refs_0_, bf16[3,512,384]{2,1,0:T(8,128)(2,1)S(1)} %pad_maximum_fusion.refs_1_.refs_0_), custom_call_target="tpu_custom_call" | custom-call | flops 200000000 | bytes 1769472 | tf_op jit(solution)/shard_map/pack_data/pallas_call | solution.py:498
  5.6 0.0 copy-start
  5.6 0.0 copy-start.1
  5.6 0.9 %kept_forward.1 = (f32[64,384]{1,0:T(8,128)S(1)}, f32[8,64]{1,0:T(8,128)S(1)}) custom-call(bf16[3,512,384]{2,1,0:T(8,128)(2,1)S(1)} %pad_maximum_fusion.refs_1_.refs_0_, bf16[6,128,128]{2,1,0:T(8,128)(2,1)S(1)} %get-tuple-element.46.refs_1_.refs_2_), custom_call_target="tpu_custom_call" | custom-call | flops 100000000 | bytes 1476608 | tf_op jit(solution)/shard_map/kept_forward/pallas_call | solution.py:498
  6.5 4.0 %local_forward.1 = (f32[384,512]{1,0:T(8,128)S(1)}, f32[8,512]{1,0:T(8,128)S(1)}, bf16[384,512]{1,0:T(8,128)(2,1)S(1)}) custom-call(s32[2]{0:T(128)S(1)} %pad_add_fusion.refs_0_, bf16[3,512,384]{2,1,0:T(8,128)(2,1)S(1)} %pad_maximum_fusion.refs_1_.refs_0_), custom_call_target="tpu_custom_call" | custom-call | flops 400000000 | bytes 2375680 | tf_op jit(solution)/shard_map/local_forward/pallas_call | solution.py:498
  10.6 1.2 %collective-permute-done.refs_3_ = bf16[512,384]{1,0:T(8,128)(2,1)S(1)} collective-permute-done((bf16[512,384]{1,0:T(8,128)(2,1)}, bf16[512,384]{1,0:T(8,128)(2,1)S(1)}, u32[]{:S(2)}, u32[]{:S(2)}) %collective-permute-start) | collective-permute-done | bytes 393248 | tf_op jit(solution)/shard_map/ppermute | solution.py:513
  11.8 0.0 copy-done
  11.8 0.0 copy-done.1
  11.8 1.8 %pack_grads.1 = (bf16[512,384]{1,0:T(8,128)(2,1)S(1)}, bf16[64,384]{1,0:T(8,128)(2,1)S(1)}, bf16[4,144,128]{2,1,0:T(8,128)(2,1)S(1)}, bf16[4,144,128]{2,1,0:T(8,128)(2,1)S(1)}) custom-call(s32[2]{0:T(128)S(1)} %pad_add_fusion.refs_0_, bf16[6,128,128]{2,1,0:T(8,128)(2,1)S(1)} %get-tuple-element.46.refs_1_.refs_2_, bf16[512,384]{1,0:T(8,128)(2,1)S(1)} %copy-done.1, ...), custom_call_target="tpu_custom_call" | custom-call | flops 400000000 | bytes 2803712 | tf_op jit(solution)/shard_map/pack_grads/pallas_call | solution.py:498
  13.6 0.1 collective-permute-start.1
  13.7 0.1 constant_dynamic-slice_fusion
  13.8 0.4 collective-permute-start.4
  14.2 0.9 %collective-permute-done.1 = bf16[4,144,128]{2,1,0:T(8,128)(2,1)S(1)} collective-permute-done((bf16[4,144,128]{2,1,0:T(8,128)(2,1)S(1)}, bf16[4,144,128]{2,1,0:T(8,128)(2,1)S(1)}, u32[]{:S(2)}, u32[]{:S(2)}) %collective-permute-start.1) | collective-permute-done | bytes 147488 | tf_op jit(solution)/shard_map/ppermute | solution.py:517
  15.1 4.7 %collective-permute-start.2 = (bf16[2,144,128]{2,1,0:T(8,128)(2,1)S(1)}, bf16[2,144,128]{2,1,0:T(8,128)(2,1)S(1)}, u32[]{:S(2)}, u32[]{:S(2)}) collective-permute-start(bf16[2,144,128]{2,1,0:T(8,128)(2,1)S(1)} %pad_maximum_fusion.3), channel_id=1, source_target_pairs={{0,12},{2,14},{4,8},{6,10},{8,4},{10,6},{12,0},{14,2},{16,28},{18,... | collective-permute-start | bytes 221192 | tf_op jit(solution)/shard_map/ppermute | solution.py:517
  19.8 0.1 collective-permute-start.5
  19.9 0.6 collective-permute-start.6
  20.6 2.3 %collective-permute-done.2 = bf16[2,144,128]{2,1,0:T(8,128)(2,1)S(1)} collective-permute-done((bf16[2,144,128]{2,1,0:T(8,128)(2,1)S(1)}, bf16[2,144,128]{2,1,0:T(8,128)(2,1)S(1)}, u32[]{:S(2)}, u32[]{:S(2)}) %collective-permute-start.2) | collective-permute-done | bytes 73760 | tf_op jit(solution)/shard_map/ppermute | solution.py:517
  22.9 0.9 %collective-permute-start.3 = (bf16[384,512]{1,0:T(8,128)(2,1)S(1)}, bf16[384,512]{1,0:T(8,128)(2,1)S(1)}, u32[]{:S(2)}, u32[]{:S(2)}) collective-permute-start(bf16[384,512]{1,0:T(8,128)(2,1)S(1)} %get-tuple-element.52.refs_8_.refs_1_), channel_id=1, source_target_pairs={{0,1},{1,0},{2,3},{3,2},{4,5},{5,4},{6,7},{7,6},{8,9},{9,8},{10,11... | collective-permute-start | bytes 1179656 | tf_op jit(solution)/shard_map/ppermute | solution.py:513
  23.8 1.4 %collective-permute-done.5 = bf16[2,144,128]{2,1,0:T(8,128)(2,1)S(1)} collective-permute-done((bf16[2,144,128]{2,1,0:T(8,128)(2,1)S(1)}, bf16[2,144,128]{2,1,0:T(8,128)(2,1)S(1)}, u32[]{:S(2)}, u32[]{:S(2)}) %collective-permute-start.5) | collective-permute-done | bytes 73760 | tf_op jit(solution)/shard_map/ppermute | solution.py:517
  25.2 1.7 %collective-permute-done.6 = bf16[2,144,128]{2,1,0:T(8,128)(2,1)S(1)} collective-permute-done((bf16[2,144,128]{2,1,0:T(8,128)(2,1)S(1)}, bf16[2,144,128]{2,1,0:T(8,128)(2,1)S(1)}, u32[]{:S(2)}, u32[]{:S(2)}) %collective-permute-start.6) | collective-permute-done | bytes 73760 | tf_op jit(solution)/shard_map/ppermute | solution.py:517
  26.9 0.8 %level_one.1 = (bf16[272,128]{1,0:T(8,128)(2,1)S(1)}, f32[8,512]{1,0:T(8,128)S(1)}, f32[64,512]{1,0:T(8,128)S(1)}) custom-call(bf16[8,144,128]{2,1,0:T(8,128)(2,1)S(1)} %constant_dynamic-update-slice_fusion.refs_0_), custom_call_target="tpu_custom_call" | custom-call | flops 100000000 | bytes 512000 | tf_op jit(solution)/shard_map/level_one/pallas_call | solution.py:498
  27.7 4.8 %collective-permute-start.9 = (bf16[272,128]{1,0:T(8,128)(2,1)S(1)}, bf16[272,128]{1,0:T(8,128)(2,1)S(1)}, u32[]{:S(2)}, u32[]{:S(2)}) collective-permute-start(bf16[272,128]{1,0:T(8,128)(2,1)S(1)} %get-tuple-element.55.refs_5_), channel_id=1, source_target_pairs={{0,60},{2,62},{4,56},{6,58},{8,52},{10,54},{12,48},{14,50},{16,44}... | collective-permute-start | bytes 208904 | tf_op jit(solution)/shard_map/ppermute | solution.py:517
  32.5 0.0 collective-permute-start.8
  32.5 0.7 collective-permute-start.7
  33.1 1.0 %level_one_back.1 = (f32[64,512]{1,0:T(8,128)S(1)}, f32[512,128]{1,0:T(8,128)S(1)}) custom-call(bf16[8,144,128]{2,1,0:T(8,128)(2,1)S(1)} %constant_dynamic-update-slice_fusion.refs_0_, f32[8,512]{1,0:T(8,128)S(1)} %get-tuple-element.56.refs_1_.refs_3_), custom_call_target="tpu_custom_call" | custom-call | flops 100000000 | bytes 704512 | tf_op jit(solution)/shard_map/level_one_back/pallas_call | solution.py:498
  34.2 2.1 %local_backward.3 = (f32[512,128]{1,0:T(8,128)S(1)}, f32[512,128]{1,0:T(8,128)S(1)}, f32[512,128]{1,0:T(8,128)S(1)}) custom-call(s32[2]{0:T(128)S(1)} %pad_add_fusion.refs_0_, bf16[3,512,384]{2,1,0:T(8,128)(2,1)S(1)} %pad_maximum_fusion.refs_1_.refs_0_, bf16[512,384]{1,0:T(8,128)(2,1)S(1)} %get-tuple-element.58.refs_2_, ...), custom_call_target="tpu_custom_call" | custom-call | flops 300000000 | bytes 3162112 | tf_op jit(solution)/shard_map/local_backward/pallas_call | solution.py:498
  36.3 0.5 collective-permute-done.9
  36.7 1.3 %collective-permute-done.8 = bf16[272,128]{1,0:T(8,128)(2,1)S(1)} collective-permute-done((bf16[272,128]{1,0:T(8,128)(2,1)S(1)}, bf16[272,128]{1,0:T(8,128)(2,1)S(1)}, u32[]{:S(2)}, u32[]{:S(2)}) %collective-permute-start.8) | collective-permute-done | bytes 69664 | tf_op jit(solution)/shard_map/ppermute | solution.py:517
  38.1 0.0 collective-permute-done.7
  38.1 0.0 collective-permute-done.4.refs_4_.refs_2_.refs_3_
  38.1 0.0 collective-permute-done.3.refs_2_.refs_1_
  38.1 0.9 %level_two.1 = (bf16[272,128]{1,0:T(8,128)(2,1)S(1)}, f32[8,512]{1,0:T(8,128)S(1)}, f32[64,128]{1,0:T(8,128)S(1)}) custom-call(bf16[4,272,128]{2,1,0:T(8,128)(2,1)S(1)} %pad_maximum_fusion.1.refs_0_.refs_1_, bf16[384,512]{1,0:T(8,128)(2,1)S(1)} %collective-permute-done.3.refs_2_.refs_1_, bf16[384,384]{1,0:T(8,128)(2,1)S(1)} %collective-permute-done.4.refs_4_.refs_2_.refs_3_, ...), custom_call_target="tpu_custom_call" | custom-call | flops 100000000 | bytes 397312 | tf_op jit(solution)/shard_map/level_two/pallas_call | solution.py:498
  39.0 3.8 %collective-permute-start.12 = (bf16[272,128]{1,0:T(8,128)(2,1)S(1)}, bf16[272,128]{1,0:T(8,128)(2,1)S(1)}, u32[]{:S(2)}, u32[]{:S(2)}) collective-permute-start(bf16[272,128]{1,0:T(8,128)(2,1)S(1)} %get-tuple-element.62.refs_5_), channel_id=1, source_target_pairs={{0,224},{2,226},{4,228},{6,230},{8,232},{10,234},{12,236},{14,238}... | collective-permute-start | bytes 208904 | tf_op jit(solution)/shard_map/ppermute | solution.py:517
  42.8 1.1 %collective-permute-start.11 = (bf16[272,128]{1,0:T(8,128)(2,1)S(1)}, bf16[272,128]{1,0:T(8,128)(2,1)S(1)}, u32[]{:S(2)}, u32[]{:S(2)}) collective-permute-start(bf16[272,128]{1,0:T(8,128)(2,1)S(1)} %get-tuple-element.62.refs_5_), channel_id=1, source_target_pairs={{0,96},{2,98},{4,100},{6,102},{8,104},{10,106},{12,108},{14,110},{... | collective-permute-start | bytes 208904 | tf_op jit(solution)/shard_map/ppermute | solution.py:517
  43.9 1.4 %collective-permute-start.10 = (bf16[272,128]{1,0:T(8,128)(2,1)S(1)}, bf16[272,128]{1,0:T(8,128)(2,1)S(1)}, u32[]{:S(2)}, u32[]{:S(2)}) collective-permute-start(bf16[272,128]{1,0:T(8,128)(2,1)S(1)} %get-tuple-element.62.refs_5_), channel_id=1, source_target_pairs={{0,128},{2,130},{4,132},{6,134},{8,136},{10,138},{12,140},{14,142}... | collective-permute-start | bytes 208904 | tf_op jit(solution)/shard_map/ppermute | solution.py:517
  45.3 0.9 %level_two_back.1 = (f32[512,128]{1,0:T(8,128)S(1)}, f32[128,128]{1,0:T(8,128)S(1)}, f32[64,128]{1,0:T(8,128)S(1)}) custom-call(bf16[8,144,128]{2,1,0:T(8,128)(2,1)S(1)} %constant_dynamic-update-slice_fusion.refs_0_, bf16[4,272,128]{2,1,0:T(8,128)(2,1)S(1)} %pad_maximum_fusion.1.refs_0_.refs_1_, f32[8,512]{1,0:T(8,128)S(1)} %get-tuple-element.63.refs_2_.refs_4_, ...), custom_call_target="tpu_custom_call" | custom-call | flops 100000000 | bytes 1212416 | tf_op jit(solution)/shard_map/level_two_back/pallas_call | solution.py:498
  46.1 2.1 %local_backward.4 = (f32[512,128]{1,0:T(8,128)S(1)}, f32[512,128]{1,0:T(8,128)S(1)}, f32[512,128]{1,0:T(8,128)S(1)}) custom-call(s32[2]{0:T(128)S(1)} %pad_add_fusion.refs_0_, bf16[3,512,384]{2,1,0:T(8,128)(2,1)S(1)} %pad_maximum_fusion.refs_1_.refs_0_, bf16[512,384]{1,0:T(8,128)(2,1)S(1)} %get-tuple-element.58.refs_2_, ...), custom_call_target="tpu_custom_call" | custom-call | flops 300000000 | bytes 3162112 | tf_op jit(solution)/shard_map/local_backward/pallas_call | solution.py:498
  48.2 1.4 %mix_base.1 = (f32[512,384]{1,0:T(8,128)S(1)}, bf16[512,384]{1,0:T(8,128)(2,1)S(1)}, bf16[512,384]{1,0:T(8,128)(2,1)S(1)}) custom-call(s32[2]{0:T(128)S(1)} %pad_add_fusion.refs_0_, bf16[384,512]{1,0:T(8,128)(2,1)S(1)} %get-tuple-element.52.refs_8_.refs_1_, bf16[384,512]{1,0:T(8,128)(2,1)S(1)} %collective-permute-done.3.refs_2_.refs_1_, ...), custom_call_target="tpu_custom_call" | custom-call | flops 300000000 | bytes 2949120 | tf_op jit(solution)/shard_map/mix_base/pallas_call | solution.py:498
  49.6 0.0 collective-permute-done.12
  49.7 0.0 collective-permute-done.11
  49.7 0.0 collective-permute-done.10
  49.7 1.7 %level_three.1 = (bf16[4,144,128]{2,1,0:T(8,128)(2,1)S(1)}, bf16[4,144,128]{2,1,0:T(8,128)(2,1)S(1)}) custom-call(bf16[8,144,128]{2,1,0:T(8,128)(2,1)S(1)} %constant_dynamic-update-slice_fusion.refs_0_, bf16[4,272,128]{2,1,0:T(8,128)(2,1)S(1)} %pad_maximum_fusion.1.refs_0_.refs_1_, bf16[4,272,128]{2,1,0:T(8,128)(2,1)S(1)} %pad_maximum_fusion.2.refs_2_, ...), custom_call_target="tpu_custom_call" | custom-call | flops 300000000 | bytes 1835008 | tf_op jit(solution)/shard_map/level_three/pallas_call | solution.py:498
  51.4 0.1 collective-permute-start.13
  51.6 1.3 %collective-permute-done.13 = bf16[4,144,128]{2,1,0:T(8,128)(2,1)S(1)} collective-permute-done((bf16[4,144,128]{2,1,0:T(8,128)(2,1)S(1)}, bf16[4,144,128]{2,1,0:T(8,128)(2,1)S(1)}, u32[]{:S(2)}, u32[]{:S(2)}) %collective-permute-start.13) | collective-permute-done | bytes 147488 | tf_op jit(solution)/shard_map/ppermute | solution.py:517
  52.9 3.0 %collective-permute-start.14 = (bf16[2,144,128]{2,1,0:T(8,128)(2,1)S(1)}, bf16[2,144,128]{2,1,0:T(8,128)(2,1)S(1)}, u32[]{:S(2)}, u32[]{:S(2)}) collective-permute-start(bf16[2,144,128]{2,1,0:T(8,128)(2,1)S(1)} %pad_maximum_fusion.6), channel_id=1, source_target_pairs={{0,4},{2,6},{4,0},{6,2},{8,12},{10,14},{12,8},{14,10},{16,20},{18,... | collective-permute-start | bytes 221192 | tf_op jit(solution)/shard_map/ppermute | solution.py:517
  56.0 0.5 collective-permute-start.15
  56.5 2.2 %collective-permute-start.16 = (bf16[2,144,128]{2,1,0:T(8,128)(2,1)S(1)}, bf16[2,144,128]{2,1,0:T(8,128)(2,1)S(1)}, u32[]{:S(2)}, u32[]{:S(2)}) collective-permute-start(bf16[2,144,128]{2,1,0:T(8,128)(2,1)S(1)} %pad_maximum_fusion.8.refs_5_), channel_id=1, source_target_pairs={{0,12},{2,14},{4,8},{6,10},{8,4},{10,6},{12,0},{14,2},{16,28},{18,... | collective-permute-start | bytes 221192 | tf_op jit(solution)/shard_map/ppermute | solution.py:517
  58.8 2.1 %local_backward.5 = (f32[512,128]{1,0:T(8,128)S(1)}, f32[512,128]{1,0:T(8,128)S(1)}, f32[512,128]{1,0:T(8,128)S(1)}) custom-call(s32[2]{0:T(128)S(1)} %pad_add_fusion.refs_0_, bf16[3,512,384]{2,1,0:T(8,128)(2,1)S(1)} %pad_maximum_fusion.refs_1_.refs_0_, bf16[512,384]{1,0:T(8,128)(2,1)S(1)} %get-tuple-element.58.refs_2_, ...), custom_call_target="tpu_custom_call" | custom-call | flops 300000000 | bytes 3162112 | tf_op jit(solution)/shard_map/local_backward/pallas_call | solution.py:498
  60.9 0.0 collective-permute-done.14
  60.9 3.8 %collective-permute-done.15 = bf16[2,144,128]{2,1,0:T(8,128)(2,1)S(1)} collective-permute-done((bf16[2,144,128]{2,1,0:T(8,128)(2,1)S(1)}, bf16[2,144,128]{2,1,0:T(8,128)(2,1)S(1)}, u32[]{:S(2)}, u32[]{:S(2)}) %collective-permute-start.15) | collective-permute-done | bytes 73760 | tf_op jit(solution)/shard_map/ppermute | solution.py:517
  64.7 0.0 collective-permute-done.16
  64.7 0.7 %kept_attended.1.refs_1_ = bf16[64,384]{1,0:T(8,128)(2,1)S(1)} custom-call(s32[2]{0:T(128)S(1)} %pad_add_fusion.refs_0_, bf16[8,144,128]{2,1,0:T(8,128)(2,1)S(1)} %constant_dynamic-update-slice_fusion.3.refs_1_.refs_4_, f32[64,384]{1,0:T(8,128)S(1)} %get-tuple-element.48.refs_6_.refs_2_, f32[8,64]{1,0:T(8,128)S(1)} %get-tuple-element.49.refs_7_.refs_3_, ...), custom_call_target="tpu_custom_call" | custom-call | flops 10000000 | bytes 444416 | tf_op jit(solution)/shard_map/kept_attended/pallas_call | solution.py:498
  65.5 1.6 %collective-permute-start.17 = (bf16[64,384]{1,0:T(8,128)(2,1)S(1)}, bf16[64,384]{1,0:T(8,128)(2,1)S(1)}, u32[]{:S(2)}, u32[]{:S(2)}) collective-permute-start(bf16[64,384]{1,0:T(8,128)(2,1)S(1)} %kept_attended.1.refs_1_), channel_id=1, source_target_pairs={{0,1},{1,0},{2,3},{3,2},{4,5},{5,4},{6,7},{7,6},{8,9},{9,8},{10,11... | collective-permute-start | bytes 147464 | tf_op jit(solution)/shard_map/ppermute | solution.py:513
  67.1 0.5 mix_own.1.refs_0_
  67.6 3.2 %final_grads.1 = (bf16[512,384]{1,0:T(8,128)(2,1)}, bf16[512,384]{1,0:T(8,128)(2,1)}, bf16[512,384]{1,0:T(8,128)(2,1)}) custom-call(s32[2]{0:T(128)S(1)} %pad_add_fusion.refs_0_, bf16[3,512,384]{2,1,0:T(8,128)(2,1)S(1)} %pad_maximum_fusion.refs_1_.refs_0_, bf16[6,128,128]{2,1,0:T(8,128)(2,1)S(1)} %get-tuple-element.46.refs_1_.refs_2_, ...), custom_call_target="tpu_custom_call" | custom-call | flops 200000000 | bytes 5652480 | tf_op jit(solution)/shard_map/final_grads/pallas_call | solution.py:498
  70.8 0.0 collective-permute-done.17.refs_1_
  70.8 1.3 %mix_other.1 = bf16[512,384]{1,0:T(8,128)(2,1)} custom-call(f32[512,384]{1,0:T(8,128)S(1)} %mix_own.1.refs_0_, bf16[64,384]{1,0:T(8,128)(2,1)S(1)} %collective-permute-done.17.refs_1_, bf16[512,384]{1,0:T(8,128)(2,1)S(1)} %get-tuple-element.75.refs_2_, bf16[384,384]{1,0:T(8,128)(2,1)S(1)} %collective-permute-done.4.refs_4_.refs_2_.refs_3_), custom_call_target="tpu_custom_call" | custom-call | flops 200000000 | bytes 1916928 | tf_op jit(solution)/shard_map/mix_other/pallas_call | solution.py:498
  (18 shorter events, 0.3 us)
Async XLA Ops:
  0.6 11.2 %collective-permute-start = (bf16[512,384]{1,0:T(8,128)(2,1)}, bf16[512,384]{1,0:T(8,128)(2,1)S(1)}, u32[]{:S(2)}, u32[]{:S(2)}) collective-permute-start(bf16[512,384]{1,0:T(8,128)(2,1)} %refs_2_.1), channel_id=1, source_target_pairs={{0,1},{1,0},{2,3},{3,2},{4,5},{5,4},{6,7},{7,6},{8,9},{9,8},{10,11... | collective-permute-start | bytes 1179656 | tf_op jit(solution)/shard_map/ppermute | solution.py:513
  5.6 6.2 %copy-start = (bf16[384,768]{1,0:T(8,128)(2,1)S(1)}, bf16[384,768]{1,0:T(8,128)(2,1)}, u32[]{:S(2)}) copy-start(bf16[384,768]{1,0:T(8,128)(2,1)} %refs_4_.1) | copy-start | bytes 1769476
  5.6 6.2 %copy-start.1 = (bf16[512,384]{1,0:T(8,128)(2,1)S(1)}, bf16[512,384]{1,0:T(8,128)(2,1)}, u32[]{:S(2)}) copy-start(bf16[512,384]{1,0:T(8,128)(2,1)} %refs_2_.1) | copy-start | bytes 1179652
  13.6 1.5 %collective-permute-start.1 = (bf16[4,144,128]{2,1,0:T(8,128)(2,1)S(1)}, bf16[4,144,128]{2,1,0:T(8,128)(2,1)S(1)}, u32[]{:S(2)}, u32[]{:S(2)}) collective-permute-start(bf16[4,144,128]{2,1,0:T(8,128)(2,1)S(1)} %get-tuple-element.51), channel_id=1, source_target_pairs={{0,2},{2,0},{4,6},{6,4},{8,10},{10,8},{12,14},{14,12},{16,18},{18,... | collective-permute-start | bytes 442376 | tf_op jit(solution)/shard_map/ppermute | solution.py:517
  13.8 24.3 %collective-permute-start.4 = (bf16[384,384]{1,0:T(8,128)(2,1)S(1)}, bf16[384,384]{1,0:T(8,128)(2,1)S(1)}, u32[]{:S(2)}, u32[]{:S(2)}) collective-permute-start(bf16[384,384]{1,0:T(8,128)(2,1)S(1)} %get-tuple-element.86), channel_id=1, source_target_pairs={{0,1},{1,0},{2,3},{3,2},{4,5},{5,4},{6,7},{7,6},{8,9},{9,8},{10,11... | collective-permute-start | bytes 884744 | tf_op jit(solution)/shard_map/ppermute | solution.py:513
  15.1 7.8 %collective-permute-start.2 = (bf16[2,144,128]{2,1,0:T(8,128)(2,1)S(1)}, bf16[2,144,128]{2,1,0:T(8,128)(2,1)S(1)}, u32[]{:S(2)}, u32[]{:S(2)}) collective-permute-start(bf16[2,144,128]{2,1,0:T(8,128)(2,1)S(1)} %pad_maximum_fusion.3), channel_id=1, source_target_pairs={{0,12},{2,14},{4,8},{6,10},{8,4},{10,6},{12,0},{14,2},{16,28},{18,... | collective-permute-start | bytes 221192 | tf_op jit(solution)/shard_map/ppermute | solution.py:517
  19.8 5.3 %collective-permute-start.5 = (bf16[2,144,128]{2,1,0:T(8,128)(2,1)S(1)}, bf16[2,144,128]{2,1,0:T(8,128)(2,1)S(1)}, u32[]{:S(2)}, u32[]{:S(2)}) collective-permute-start(bf16[2,144,128]{2,1,0:T(8,128)(2,1)S(1)} %pad_maximum_fusion.4), channel_id=1, source_target_pairs={{0,4},{2,6},{4,0},{6,2},{8,12},{10,14},{12,8},{14,10},{16,20},{18,... | collective-permute-start | bytes 221192 | tf_op jit(solution)/shard_map/ppermute | solution.py:517
  19.9 6.9 %collective-permute-start.6 = (bf16[2,144,128]{2,1,0:T(8,128)(2,1)S(1)}, bf16[2,144,128]{2,1,0:T(8,128)(2,1)S(1)}, u32[]{:S(2)}, u32[]{:S(2)}) collective-permute-start(bf16[2,144,128]{2,1,0:T(8,128)(2,1)S(1)} %pad_maximum_fusion.5), channel_id=1, source_target_pairs={{0,8},{2,10},{4,12},{6,14},{8,0},{10,2},{12,4},{14,6},{16,24},{18,... | collective-permute-start | bytes 221192 | tf_op jit(solution)/shard_map/ppermute | solution.py:517
  22.9 15.2 %collective-permute-start.3 = (bf16[384,512]{1,0:T(8,128)(2,1)S(1)}, bf16[384,512]{1,0:T(8,128)(2,1)S(1)}, u32[]{:S(2)}, u32[]{:S(2)}) collective-permute-start(bf16[384,512]{1,0:T(8,128)(2,1)S(1)} %get-tuple-element.52.refs_8_.refs_1_), channel_id=1, source_target_pairs={{0,1},{1,0},{2,3},{3,2},{4,5},{5,4},{6,7},{7,6},{8,9},{9,8},{10,11... | collective-permute-start | bytes 1179656 | tf_op jit(solution)/shard_map/ppermute | solution.py:513
  27.7 9.0 %collective-permute-start.9 = (bf16[272,128]{1,0:T(8,128)(2,1)S(1)}, bf16[272,128]{1,0:T(8,128)(2,1)S(1)}, u32[]{:S(2)}, u32[]{:S(2)}) collective-permute-start(bf16[272,128]{1,0:T(8,128)(2,1)S(1)} %get-tuple-element.55.refs_5_), channel_id=1, source_target_pairs={{0,60},{2,62},{4,56},{6,58},{8,52},{10,54},{12,48},{14,50},{16,44}... | collective-permute-start | bytes 208904 | tf_op jit(solution)/shard_map/ppermute | solution.py:517
  32.5 5.6 %collective-permute-start.8 = (bf16[272,128]{1,0:T(8,128)(2,1)S(1)}, bf16[272,128]{1,0:T(8,128)(2,1)S(1)}, u32[]{:S(2)}, u32[]{:S(2)}) collective-permute-start(bf16[272,128]{1,0:T(8,128)(2,1)S(1)} %get-tuple-element.55.refs_5_), channel_id=1, source_target_pairs={{0,28},{2,30},{4,24},{6,26},{8,20},{10,22},{12,16},{14,18},{16,12}... | collective-permute-start | bytes 208904 | tf_op jit(solution)/shard_map/ppermute | solution.py:517
  32.5 5.6 %collective-permute-start.7 = (bf16[272,128]{1,0:T(8,128)(2,1)S(1)}, bf16[272,128]{1,0:T(8,128)(2,1)S(1)}, u32[]{:S(2)}, u32[]{:S(2)}) collective-permute-start(bf16[272,128]{1,0:T(8,128)(2,1)S(1)} %get-tuple-element.55.refs_5_), channel_id=1, source_target_pairs={{0,32},{2,34},{4,36},{6,38},{8,40},{10,42},{12,44},{14,46},{16,48}... | collective-permute-start | bytes 208904 | tf_op jit(solution)/shard_map/ppermute | solution.py:517
  39.0 10.7 %collective-permute-start.12 = (bf16[272,128]{1,0:T(8,128)(2,1)S(1)}, bf16[272,128]{1,0:T(8,128)(2,1)S(1)}, u32[]{:S(2)}, u32[]{:S(2)}) collective-permute-start(bf16[272,128]{1,0:T(8,128)(2,1)S(1)} %get-tuple-element.62.refs_5_), channel_id=1, source_target_pairs={{0,224},{2,226},{4,228},{6,230},{8,232},{10,234},{12,236},{14,238}... | collective-permute-start | bytes 208904 | tf_op jit(solution)/shard_map/ppermute | solution.py:517
  42.8 6.9 %collective-permute-start.11 = (bf16[272,128]{1,0:T(8,128)(2,1)S(1)}, bf16[272,128]{1,0:T(8,128)(2,1)S(1)}, u32[]{:S(2)}, u32[]{:S(2)}) collective-permute-start(bf16[272,128]{1,0:T(8,128)(2,1)S(1)} %get-tuple-element.62.refs_5_), channel_id=1, source_target_pairs={{0,96},{2,98},{4,100},{6,102},{8,104},{10,106},{12,108},{14,110},{... | collective-permute-start | bytes 208904 | tf_op jit(solution)/shard_map/ppermute | solution.py:517
  43.9 5.8 %collective-permute-start.10 = (bf16[272,128]{1,0:T(8,128)(2,1)S(1)}, bf16[272,128]{1,0:T(8,128)(2,1)S(1)}, u32[]{:S(2)}, u32[]{:S(2)}) collective-permute-start(bf16[272,128]{1,0:T(8,128)(2,1)S(1)} %get-tuple-element.62.refs_5_), channel_id=1, source_target_pairs={{0,128},{2,130},{4,132},{6,134},{8,136},{10,138},{12,140},{14,142}... | collective-permute-start | bytes 208904 | tf_op jit(solution)/shard_map/ppermute | solution.py:517
  51.4 1.5 %collective-permute-start.13 = (bf16[4,144,128]{2,1,0:T(8,128)(2,1)S(1)}, bf16[4,144,128]{2,1,0:T(8,128)(2,1)S(1)}, u32[]{:S(2)}, u32[]{:S(2)}) collective-permute-start(bf16[4,144,128]{2,1,0:T(8,128)(2,1)S(1)} %get-tuple-element.72), channel_id=1, source_target_pairs={{0,2},{2,0},{4,6},{6,4},{8,10},{10,8},{12,14},{14,12},{16,18},{18,... | collective-permute-start | bytes 442376 | tf_op jit(solution)/shard_map/ppermute | solution.py:517
  52.9 7.9 %collective-permute-start.14 = (bf16[2,144,128]{2,1,0:T(8,128)(2,1)S(1)}, bf16[2,144,128]{2,1,0:T(8,128)(2,1)S(1)}, u32[]{:S(2)}, u32[]{:S(2)}) collective-permute-start(bf16[2,144,128]{2,1,0:T(8,128)(2,1)S(1)} %pad_maximum_fusion.6), channel_id=1, source_target_pairs={{0,4},{2,6},{4,0},{6,2},{8,12},{10,14},{12,8},{14,10},{16,20},{18,... | collective-permute-start | bytes 221192 | tf_op jit(solution)/shard_map/ppermute | solution.py:517
  56.0 8.7 %collective-permute-start.15 = (bf16[2,144,128]{2,1,0:T(8,128)(2,1)S(1)}, bf16[2,144,128]{2,1,0:T(8,128)(2,1)S(1)}, u32[]{:S(2)}, u32[]{:S(2)}) collective-permute-start(bf16[2,144,128]{2,1,0:T(8,128)(2,1)S(1)} %pad_maximum_fusion.7), channel_id=1, source_target_pairs={{0,8},{2,10},{4,12},{6,14},{8,0},{10,2},{12,4},{14,6},{16,24},{18,... | collective-permute-start | bytes 221192 | tf_op jit(solution)/shard_map/ppermute | solution.py:517
  56.5 8.2 %collective-permute-start.16 = (bf16[2,144,128]{2,1,0:T(8,128)(2,1)S(1)}, bf16[2,144,128]{2,1,0:T(8,128)(2,1)S(1)}, u32[]{:S(2)}, u32[]{:S(2)}) collective-permute-start(bf16[2,144,128]{2,1,0:T(8,128)(2,1)S(1)} %pad_maximum_fusion.8.refs_5_), channel_id=1, source_target_pairs={{0,12},{2,14},{4,8},{6,10},{8,4},{10,6},{12,0},{14,2},{16,28},{18,... | collective-permute-start | bytes 221192 | tf_op jit(solution)/shard_map/ppermute | solution.py:517
  65.5 5.3 %collective-permute-start.17 = (bf16[64,384]{1,0:T(8,128)(2,1)S(1)}, bf16[64,384]{1,0:T(8,128)(2,1)S(1)}, u32[]{:S(2)}, u32[]{:S(2)}) collective-permute-start(bf16[64,384]{1,0:T(8,128)(2,1)S(1)} %kept_attended.1.refs_1_), channel_id=1, source_target_pairs={{0,1},{1,0},{2,3},{3,2},{4,5},{5,4},{6,7},{7,6},{8,9},{9,8},{10,11... | collective-permute-start | bytes 147464 | tf_op jit(solution)/shard_map/ppermute | solution.py:513
